TPU v7x, 32 devices: a whole 2x2x4 slice. The times are simulated.
32 devices in a mesh: groups: 2 (over x), expert: 8 (over z, y), dp: 2 (over core).
Axes of the slice: x: 2, y: 2, z: 4, core: 2. Of those that a mesh axis runs over, the one named last changes fastest.
Arguments:
- tokens: bfloat16 [4096, 1536], P(('groups', 'expert', 'dp')), parts along dimension 0, may hold values from -6 to 6
- cotangent: bfloat16 [4096, 1536], P(('groups', 'expert', 'dp')), parts along dimension 0, may hold values from -6 to 6
- mixture: bfloat16 [4096, 1536], P(('groups', 'expert', 'dp')), parts along dimension 0, may hold values from -3 to 3
- stamp: int32 [4096], P(('groups', 'expert', 'dp')), parts along dimension 0, may hold values from 0 to 31
- expert_ids: int32 [4096, 2], P(('groups', 'expert', 'dp')), parts along dimension 0, may hold values from 0 to 7, all different within a row; in each aligned block of 128 rows (0 to 127, 128 to 255, ...) at most 64 rows name the same one
- modulation: float32 [3, 32, 1536], replicated, may hold values from -3 to 3
- router: bfloat16 [8, 1536], replicated, may hold values from -0.15625 to 0.15625
- w_gate: bfloat16 [8, 1536, 768], P('expert', None, 'dp'), may hold values from -0.15625 to 0.15625
- w_up: bfloat16 [8, 1536, 768], P('expert', None, 'dp'), may hold values from -0.15625 to 0.15625
- w_down: bfloat16 [8, 1536, 768], P('expert', None, 'dp'), may hold values from -0.21875 to 0.21875
Outputs:
- d_tokens: bfloat16 [4096, 1536], P(('groups', 'expert', 'dp')), parts along dimension 0
- d_gate_w: bfloat16 [16, 1536, 768], P(('groups', 'expert'), None, 'dp'), parts along dimension 0
- d_up_w: bfloat16 [16, 1536, 768], P(('groups', 'expert'), None, 'dp'), parts along dimension 0
- d_down_w: bfloat16 [16, 1536, 768], P(('groups', 'expert'), None, 'dp'), parts along dimension 0
- d_router: float32 [16, 1536], P('groups'), parts along dimension 0
- d_modulation: float32 [3, 64, 1536], P(None, 'groups'), parts along dimension 1
There are 2 independent parts, one for each index of `groups`. A program takes and returns all parts, laid end to end along the dimension named above; an argument that names none is the same for every part. Nothing has to cross between parts.
Inputs may be any that keep to these rules, and one draw needn't show every extreme that they name: `expert_ids`: each token names two different experts. Within the tokens of one device (aligned blocks of 128 tokens) no expert is named more than 64 times, and in every draw some expert is named exactly 64 times in some block.
All inputs are finite; a program needn't handle non-finite values.
Results may differ from a plain program's by a relative error of at most 0.015.
Values may be sent and summed in bfloat16 or wider, within the bound.
No kernel may reach another device: no remote copies, remote signals or barrier semaphores. Data moves between devices by JAX's collectives and lax.ppermute only.
A program may use at most 128 MiB of HBM per device.

v0:
```python
import jax
import jax.numpy as jnp
from jax import lax
from jax.sharding import PartitionSpec as P

epsilon = 1e-06
highest = lax.Precision.HIGHEST


def normalize(tokens):
    values = tokens.astype(jnp.float32)
    centred = values - jnp.mean(values, axis=-1, keepdims=True)
    inverse = lax.rsqrt(jnp.mean(centred * centred, axis=-1, keepdims=True) + epsilon)
    return (centred * inverse, inverse)


def slot_positions(flat_ids, experts):
    onehot = (flat_ids[:, None] == jnp.arange(experts, dtype=jnp.int32)).astype(jnp.int32)
    before = jnp.cumsum(onehot, axis=0) - onehot
    return jnp.sum(before * onehot, axis=1)


def expert_backward(in_rows, cot_rows, prob_rows, gate_weight, up_weight, down_weight):
    contract_one = (((1,), (1,)), ((), ()))
    contract_zero = (((0,), (0,)), ((), ()))
    pre_gate = jnp.dot(in_rows, gate_weight, preferred_element_type=jnp.float32)
    pre_up = jnp.dot(in_rows, up_weight, preferred_element_type=jnp.float32)
    sigmoid_gate = jax.nn.sigmoid(pre_gate)
    active = pre_gate * sigmoid_gate
    hidden = (active * pre_up).astype(jnp.bfloat16)
    out_grad = (prob_rows[:, None] * cot_rows.astype(jnp.float32)).astype(jnp.bfloat16)
    output = lax.dot_general(hidden, down_weight, contract_one, preferred_element_type=jnp.float32)
    prob_grad = jnp.sum(cot_rows.astype(jnp.float32) * output, axis=1)
    hidden_grad = jnp.dot(out_grad, down_weight, preferred_element_type=jnp.float32)
    gate_grad = (
        hidden_grad * pre_up * sigmoid_gate * (1.0 + pre_gate * (1.0 - sigmoid_gate))
    ).astype(jnp.bfloat16)
    up_grad = (hidden_grad * active).astype(jnp.bfloat16)
    grad_gate = lax.dot_general(
        in_rows, gate_grad, contract_zero, preferred_element_type=jnp.float32
    )
    grad_up = lax.dot_general(in_rows, up_grad, contract_zero, preferred_element_type=jnp.float32)
    grad_down = lax.dot_general(out_grad, hidden, contract_zero, preferred_element_type=jnp.float32)
    row_grad = lax.dot_general(
        gate_grad, gate_weight, contract_one, preferred_element_type=jnp.float32
    )
    row_grad = row_grad + lax.dot_general(
        up_grad, up_weight, contract_one, preferred_element_type=jnp.float32
    )
    return (row_grad, prob_grad, grad_gate, grad_up, grad_down)


def local(tokens, cotangent, mixture, stamp, expert_ids, modulation, router, w_gate, w_up, w_down):
    tok_count = tokens.shape[0]
    model_width = tokens.shape[1]
    experts = router.shape[0]
    conditions = modulation.shape[1]
    capacity = min(tok_count, 4 * tok_count // lax.axis_size("expert"))
    normed, inverse = normalize(tokens)
    onehot_t = (stamp[:, None] == jnp.arange(conditions, dtype=jnp.int32)).astype(jnp.float32)
    stacked_table = jnp.transpose(modulation, (1, 0, 2)).reshape(conditions, 3 * model_width)
    table_rows = jnp.dot(onehot_t, stacked_table, precision=highest)
    shift_rows = table_rows[:, :model_width]
    scale_rows = table_rows[:, model_width : 2 * model_width]
    gate_rows = table_rows[:, 2 * model_width :]
    modulated = (normed * (1.0 + scale_rows) + shift_rows).astype(jnp.bfloat16)
    upstream = (gate_rows * cotangent.astype(jnp.float32)).astype(jnp.bfloat16)
    logits = lax.dot_general(
        modulated, router, (((1,), (1,)), ((), ())), preferred_element_type=jnp.float32
    )
    chosen_prob = jax.nn.sigmoid(jnp.take_along_axis(logits, expert_ids, axis=1))
    flat_ids = expert_ids.reshape(-1)
    places = flat_ids * capacity + slot_positions(flat_ids, experts)
    send_rows = (
        jnp.zeros((experts * capacity, model_width), jnp.bfloat16)
        .at[places]
        .set(jnp.repeat(modulated, 2, axis=0))
    )
    send_cot = (
        jnp.zeros((experts * capacity, model_width), jnp.bfloat16)
        .at[places]
        .set(jnp.repeat(upstream, 2, axis=0))
    )
    send_prob = (
        jnp.zeros((experts * capacity,), jnp.float32).at[places].set(chosen_prob.reshape(-1))
    )
    got_rows, got_cot, got_prob = (
        lax.all_to_all(
            send_rows.reshape(experts, capacity, model_width),
            "expert",
            split_axis=0,
            concat_axis=0,
            tiled=True,
        ),
        lax.all_to_all(
            send_cot.reshape(experts, capacity, model_width),
            "expert",
            split_axis=0,
            concat_axis=0,
            tiled=True,
        ),
        lax.all_to_all(
            send_prob.reshape(experts, capacity).astype(jnp.bfloat16),
            "expert",
            split_axis=0,
            concat_axis=0,
            tiled=True,
        ).astype(jnp.float32),
    )
    full_gate, full_up, full_down = (
        lax.all_gather(w_gate, "dp", axis=2, tiled=True),
        lax.all_gather(w_up, "dp", axis=2, tiled=True),
        lax.all_gather(w_down, "dp", axis=2, tiled=True),
    )
    flat_count = experts * capacity
    row_grad, prob_grad, grad_gate, grad_up, grad_down = expert_backward(
        got_rows.reshape(flat_count, model_width),
        got_cot.reshape(flat_count, model_width),
        got_prob.reshape(-1),
        full_gate[0],
        full_up[0],
        full_down[0],
    )
    grad_gate, grad_up, grad_down = (
        lax.psum_scatter(
            grad_gate[None].astype(jnp.bfloat16), "dp", scatter_dimension=2, tiled=True
        ).astype(jnp.float32),
        lax.psum_scatter(
            grad_up[None].astype(jnp.bfloat16), "dp", scatter_dimension=2, tiled=True
        ).astype(jnp.float32),
        lax.psum_scatter(
            grad_down[None].astype(jnp.bfloat16), "dp", scatter_dimension=2, tiled=True
        ).astype(jnp.float32),
    )
    back_rows = row_grad.astype(jnp.bfloat16).reshape(experts, capacity, model_width)
    back_prob = prob_grad.reshape(experts, capacity)
    ret_rows, ret_prob = (
        lax.all_to_all(back_rows, "expert", split_axis=0, concat_axis=0, tiled=True),
        lax.all_to_all(
            back_prob.astype(jnp.bfloat16), "expert", split_axis=0, concat_axis=0, tiled=True
        ).astype(back_prob.dtype),
    )
    mine_rows = (
        ret_rows.reshape(experts * capacity, model_width)[places]
        .astype(jnp.float32)
        .reshape(tok_count, 2, model_width)
    )
    mine_prob = ret_prob.reshape(-1)[places].reshape(tok_count, 2)
    logit_grad = mine_prob * chosen_prob * (1.0 - chosen_prob)
    onehot_e = (expert_ids[:, :, None] == jnp.arange(experts, dtype=jnp.int32)).astype(jnp.float32)
    logit_table = jnp.sum(onehot_e * logit_grad[:, :, None], axis=1)
    mod_grad = jnp.sum(mine_rows, axis=1) + jnp.dot(
        logit_table, router.astype(jnp.float32), precision=highest
    )
    router_part = jnp.dot(logit_table.T, modulated.astype(jnp.float32), precision=highest)
    d_normed = mod_grad * (1.0 + scale_rows)
    d_input = inverse * (
        d_normed
        - jnp.mean(d_normed, axis=-1, keepdims=True)
        - normed * jnp.mean(d_normed * normed, axis=-1, keepdims=True)
    )
    d_tokens = (cotangent.astype(jnp.float32) + d_input).astype(jnp.bfloat16)
    gate_terms = cotangent.astype(jnp.float32) * mixture.astype(jnp.float32)
    table_part = jnp.stack(
        [
            jnp.dot(onehot_t.T, mod_grad, precision=highest),
            jnp.dot(onehot_t.T, mod_grad * normed, precision=highest),
            jnp.dot(onehot_t.T, gate_terms, precision=highest),
        ]
    )
    d_modulation, d_router = lax.psum((table_part, router_part), ("expert", "dp"))
    return (
        d_tokens,
        grad_gate.astype(jnp.bfloat16),
        grad_up.astype(jnp.bfloat16),
        grad_down.astype(jnp.bfloat16),
        d_router,
        d_modulation,
    )


def solution(mesh):
    return jax.shard_map(
        local,
        mesh=mesh,
        in_specs=(
            P(("groups", "expert", "dp"), None),
            P(("groups", "expert", "dp"), None),
            P(("groups", "expert", "dp"), None),
            P(("groups", "expert", "dp")),
            P(("groups", "expert", "dp"), None),
            P(),
            P(),
            P("expert", None, "dp"),
            P("expert", None, "dp"),
            P("expert", None, "dp"),
        ),
        out_specs=(
            P(("groups", "expert", "dp"), None),
            P(("groups", "expert"), None, "dp"),
            P(("groups", "expert"), None, "dp"),
            P(("groups", "expert"), None, "dp"),
            P("groups", None),
            P(None, "groups", None),
        ),
        check_vma=False,
    )
```

profile of v0, /device:TPU:1, one launch (start us, length us, event | category | flops | bytes accessed | tf_op | source)
XLA Modules:
  0.0 395.7 jit_solution(5253297608363062470)
XLA Ops:
  9.5 1.1 fusion.42
  11.1 0.9 copy-done.1
  12.5 1.2 reshape.255
  14.8 3.8 scatter_custom_fusion.2
  18.6 6.4 %all-to-all-start.2 = ((bf16[8,64,1536]{2,1,0:T(8,128)(2,1)}), bf16[8,64,1536]{2,1,0:T(8,128)(2,1)}, u32[]{:S(2)}, u32[]{:S(2)}) async-start(bf16[8,64,1536]{2,1,0:T(8,128)(2,1)} %bitcast.10), calls=%async_computation.2 | async-start | bytes 3145728 | tf_op jit(solution)/shard_map/all_to_all | solution.py:88
  26.5 3.2 scatter_custom_fusion.1
  29.7 31.6 %all-to-all-done.2 = bf16[8,64,1536]{2,1,0:T(8,128)(2,1)} async-done(((bf16[8,64,1536]{2,1,0:T(8,128)(2,1)}), bf16[8,64,1536]{2,1,0:T(8,128)(2,1)}, u32[]{:S(2)}, u32[]{:S(2)}) %all-to-all-start.2) | async-done | bytes 1572896 | tf_op jit(solution)/shard_map/all_to_all | solution.py:88
  61.3 4.7 %all-to-all-start.1 = ((bf16[8,64,1536]{2,1,0:T(8,128)(2,1)}), bf16[8,64,1536]{2,1,0:T(8,128)(2,1)S(1)}, u32[]{:S(2)}, u32[]{:S(2)}) async-start(bf16[8,64,1536]{2,1,0:T(8,128)(2,1)} %bitcast.108), calls=%async_computation.1 | async-start | bytes 3145728 | tf_op jit(solution)/shard_map/all_to_all | solution.py:95
  66.9 4.7 %fusion.7 = f32[512,768]{1,0:T(8,128)} fusion(bf16[512,1536]{1,0:T(8,128)(2,1)} %bitcast.11, bf16[1,1536,768]{2,1,0:T(8,128)(2,1)} %all-gather.8.cloned.1.call-done), kind=kOutput, calls=%fused_computation.27 | convolution fusion | flops 1207959552 | bytes 5505024 | tf_op jit(solution)/shard_map/dot_general | solution.py:26
  71.6 5.4 %multiply_convert_fusion.1 = (bf16[512,768]{1,0:T(8,128)(2,1)}, f32[512,768]{1,0:T(8,128)}) fusion(f32[512,768]{1,0:T(8,128)} %fusion.7, bf16[512,1536]{1,0:T(8,128)(2,1)} %bitcast.11, bf16[1,1536,768]{2,1,0:T(8,128)(2,1)} %all-gather.6.cloned.1.call-done), kind=kOutput, calls=%fused_computation.38 | convolution fusion | flops 1210318848 | bytes 7864320 | tf_op jit(solution)/shard_map/dot_general | solution.py:27
  77.0 4.1 %all-gather.4.cloned.1.call-done = bf16[1,1536,768]{2,1,0:T(8,128)(2,1)} async-done(((bf16[1,1536,384]{2,1,0:T(8,128)(2,1)}), bf16[1,1536,768]{2,1,0:T(8,128)(2,1)}) %all-gather.4.cloned.1.call-update) | async-done | bytes 2359312 | tf_op jit(solution)/shard_map/all_gather | solution.py:113
  81.1 21.1 %all-to-all-done.1 = bf16[8,64,1536]{2,1,0:T(8,128)(2,1)S(1)} async-done(((bf16[8,64,1536]{2,1,0:T(8,128)(2,1)}), bf16[8,64,1536]{2,1,0:T(8,128)(2,1)S(1)}, u32[]{:S(2)}, u32[]{:S(2)}) %all-to-all-start.1) | async-done | bytes 1572896 | tf_op jit(solution)/shard_map/all_to_all | solution.py:95
  102.3 3.5 fusion.16
  106.4 4.5 %all-to-all-start.4 = ((bf16[8,1,64]{2,1,0:T(2,128)(2,1)}), bf16[8,1,64]{2,1,0:T(2,128)(2,1)S(1)}, u32[]{:S(2)}, u32[]{:S(2)}) async-start(bf16[8,1,64]{2,1,0:T(2,128)(2,1)} %convert_element_type.183), calls=%async_computation.4 | async-start | bytes 8192 | tf_op jit(solution)/shard_map/all_to_all | solution.py:139
  111.4 1.4 gather_fusion.2
  113.0 3.2 all-to-all-done.4
  116.2 1.9 gather_fusion.1
  118.7 1.4 scatter_custom_fusion
  120.2 7.7 %all_to_all.27 = bf16[8,1,64]{2,1,0:T(2,128)(2,1)S(1)} all-to-all(bf16[8,1,64]{2,1,0:T(2,128)(2,1)S(1)} %convert_element_type.182), channel_id=1, replica_groups=mesh['groups'=2,'expert'=8,'dp'=2] {'expert'}, dimensions={0} | all-to-all | bytes 2048 | tf_op jit(solution)/shard_map/all_to_all | solution.py:102
  129.1 2.9 fusion.3
  132.0 12.1 %copy.77 = bf16[1,1536,768]{1,0,2:T(2,128)(2,1)} copy(bf16[1,1536,768]{2,1,0:T(8,128)(2,1)} %fusion.3) | data formatting | bytes 4718592
  144.1 4.4 %copy.86 = bf16[768,1,1536]{2,0,1:T(8,128)(2,1)} copy(bf16[768,1,1536]{2,1,0:T(2,128)(2,1)} %bitcast.101) | data formatting | bytes 4718592
  148.9 1.3 copy-done.10
  150.2 3.6 multiply_convert_fusion.2
  153.8 4.7 %fusion.1 = bf16[1,1536,768]{2,1,0:T(8,128)(2,1)} fusion(bf16[512,1536]{1,0:T(8,128)(2,1)} %bitcast.11, bf16[512,768]{1,0:T(8,128)(2,1)S(1)} %get-tuple-element.11), kind=kOutput, calls=%fused_computation.14 | convolution fusion | flops 1209139200 | bytes 4718592 | tf_op jit(solution)/shard_map/dot_general | solution.py:39
  158.5 12.1 %copy.73 = bf16[1,1536,768]{1,0,2:T(2,128)(2,1)} copy(bf16[1,1536,768]{2,1,0:T(8,128)(2,1)} %fusion.1) | data formatting | bytes 4718592
  170.6 4.4 %copy.88 = bf16[768,1,1536]{2,0,1:T(8,128)(2,1)} copy(bf16[768,1,1536]{2,1,0:T(2,128)(2,1)} %bitcast.102) | data formatting | bytes 4718592
  175.1 4.2 %fusion.2 = bf16[1,1536,768]{2,1,0:T(8,128)(2,1)} fusion(bf16[512,1536]{1,0:T(8,128)(2,1)} %bitcast.11, bf16[512,768]{1,0:T(8,128)(2,1)S(1)} %get-tuple-element.10), kind=kOutput, calls=%fused_computation.15 | convolution fusion | flops 1209139200 | bytes 4718592 | tf_op jit(solution)/shard_map/dot_general | solution.py:42
  179.3 12.2 %copy.75 = bf16[1,1536,768]{1,0,2:T(2,128)(2,1)} copy(bf16[1,1536,768]{2,1,0:T(8,128)(2,1)} %fusion.2) | data formatting | bytes 4718592
  191.5 4.3 %copy.87 = bf16[768,1,1536]{2,0,1:T(8,128)(2,1)} copy(bf16[768,1,1536]{2,1,0:T(2,128)(2,1)} %bitcast.103) | data formatting | bytes 4718592
  195.8 3.2 fusion.5
  199.0 2.6 fusion.4
  201.6 3.6 all-to-all-start.3
  205.3 1.5 convolution_bitcast_fusion
  207.1 75.6 %psum.14 = f32[8,1536]{1,0:T(8,128)} all-reduce(f32[8,1536]{1,0:T(8,128)S(1)} %fusion.55), channel_id=1, replica_groups=mesh['groups'=2,'expert'=8,'dp'=2] {'expert','dp'}, use_global_device_ids=true, to_apply=%region_16.17 | all-reduce | flops 12288 | bytes 98304 | tf_op jit(solution)/shard_map/psum | solution.py:171
  282.7 1.3 gather_fusion
  284.0 2.1 reshape.209
  286.1 4.3 %reduce_sum.78 = f32[128,1536]{1,0:T(8,128)} reduce(f32[128,2,1536]{2,1,0:T(2,128)} %reshape.209, f32[]{:T(128)} %constant.14.clone.1), dimensions={1}, to_apply=%region_8.9 | reduce | flops 196608 | bytes 2359300 | tf_op jit(solution)/shard_map/reduce_sum | solution.py:152
  290.4 1.9 fusion.53
  294.7 2.3 fusion.33
  297.0 2.5 reshape_bitcast_fusion
  299.5 4.2 %copy.78 = bf16[1,1536,384]{2,1,0:T(8,128)(2,1)} copy(bf16[1,1536,384]{1,0,2:T(2,128)(2,1)S(1)} %reshape_bitcast_fusion) | data formatting | bytes 2359296
  303.7 2.5 reshape_bitcast_fusion.2
  306.2 4.2 %copy.74 = bf16[1,1536,384]{2,1,0:T(8,128)(2,1)} copy(bf16[1,1536,384]{1,0,2:T(2,128)(2,1)S(1)} %reshape_bitcast_fusion.2) | data formatting | bytes 2359296
  310.4 2.5 reshape_bitcast_fusion.1
  312.9 4.2 %copy.76 = bf16[1,1536,384]{2,1,0:T(8,128)(2,1)} copy(bf16[1,1536,384]{1,0,2:T(2,128)(2,1)S(1)} %reshape_bitcast_fusion.1) | data formatting | bytes 2359296
  317.1 69.8 %all-reduce.2.cloned.1.call-done = f32[3,32,1536]{2,1,0:T(8,128)} async-done(((f32[3,32,1536]{2,1,0:T(8,128)}), f32[3,32,1536]{2,1,0:T(8,128)}) %all-reduce.2.cloned.1.call-update) | async-done | bytes 589840 | tf_op jit(solution)/shard_map/psum | solution.py:171
  387.0 1.9 copy.90
  (92 shorter events, 13.0 us)
Async XLA Ops:
  7.2 59.5 %copy-start = (bf16[8,1536]{1,0:T(8,128)(2,1)S(1)}, bf16[8,1536]{1,0:T(8,128)(2,1)}, u32[]{:S(2)}) copy-start(bf16[8,1536]{1,0:T(8,128)(2,1)} %param.16) | copy-start | bytes 73732
  7.2 1.8 copy-start.3
  7.2 2.2 copy-start.6
  7.2 2.3 copy-start.8
  7.2 59.7 %all-gather.8.cloned.1.call-start = ((), (), s32[]{:S(2)}) async-start(), calls=%async_computation.10 | async-start | bytes 3538944 | tf_op jit(solution)/shard_map/all_gather | solution.py:111
  9.5 1.2 copy-start.5
  10.6 1.4 copy-start.1
  12.1 2.4 copy-start.7
  18.6 42.6 %all-to-all-start.2 = ((bf16[8,64,1536]{2,1,0:T(8,128)(2,1)}), bf16[8,64,1536]{2,1,0:T(8,128)(2,1)}, u32[]{:S(2)}, u32[]{:S(2)}) async-start(bf16[8,64,1536]{2,1,0:T(8,128)(2,1)} %bitcast.10), calls=%async_computation.2 | async-start | bytes 3145728 | tf_op jit(solution)/shard_map/all_to_all | solution.py:88
  25.0 46.6 %all-gather.6.cloned.1.call-start = ((), (), s32[]{:S(2)}) async-start(), calls=%async_computation.9 | async-start | bytes 3538944 | tf_op jit(solution)/shard_map/all_gather | solution.py:112
  61.3 41.0 %all-to-all-start.1 = ((bf16[8,64,1536]{2,1,0:T(8,128)(2,1)}), bf16[8,64,1536]{2,1,0:T(8,128)(2,1)S(1)}, u32[]{:S(2)}, u32[]{:S(2)}) async-start(bf16[8,64,1536]{2,1,0:T(8,128)(2,1)} %bitcast.108), calls=%async_computation.1 | async-start | bytes 3145728 | tf_op jit(solution)/shard_map/all_to_all | solution.py:95
  65.9 15.2 %all-gather.4.cloned.1.call-start = ((), (), s32[]{:S(2)}) async-start(), calls=%async_computation.8 | async-start | bytes 3538944 | tf_op jit(solution)/shard_map/all_gather | solution.py:113
  106.4 9.7 %all-to-all-start.4 = ((bf16[8,1,64]{2,1,0:T(2,128)(2,1)}), bf16[8,1,64]{2,1,0:T(2,128)(2,1)S(1)}, u32[]{:S(2)}, u32[]{:S(2)}) async-start(bf16[8,1,64]{2,1,0:T(2,128)(2,1)} %convert_element_type.183), calls=%async_computation.4 | async-start | bytes 8192 | tf_op jit(solution)/shard_map/all_to_all | solution.py:139
  110.9 186.1 %reduce-scatter.14.cloned.1.call-start = ((), (), s32[]{:S(2)}) async-start(), calls=%async_computation.14 | async-start | bytes 3538944
  128.0 1.1 copy-start.11
  148.5 155.3 %reduce-scatter.10.cloned.1.call-start = ((), (), s32[]{:S(2)}) async-start(), calls=%async_computation.12 | async-start | bytes 3538944
  148.5 1.7 copy-start.10
  175.0 135.4 %reduce-scatter.12.cloned.1.call-start = ((), (), s32[]{:S(2)}) async-start(), calls=%async_computation.13 | async-start | bytes 3538944
  195.8 3.2 copy-start.9
  201.6 81.1 %all-to-all-start.3 = ((bf16[8,64,1536]{2,1,0:T(8,128)(2,1)}), bf16[8,64,1536]{2,1,0:T(8,128)(2,1)S(1)}, u32[]{:S(2)}, u32[]{:S(2)}) async-start(bf16[8,64,1536]{2,1,0:T(8,128)(2,1)} %bitcast.110), calls=%async_computation.3 | async-start | bytes 3145728 | tf_op jit(solution)/shard_map/all_to_all | solution.py:138
  205.2 181.8 %all-reduce.2.cloned.1.call-start = ((), (), s32[]{:S(2)}) async-start(), calls=%async_computation.11 | async-start | bytes 1179648 | tf_op jit(solution)/shard_map/psum | solution.py:171
  286.1 4.3 %copy-start.2 = (f32[128,4608]{1,0:T(8,128)S(1)}, f32[128,4608]{1,0:T(8,128)}, u32[]{:S(2)}) copy-start(f32[128,4608]{1,0:T(8,128)} %copy-done.1) | copy-start | bytes 7077892
  292.3 0.9 copy-start.4
Sparse Core Ops, SparseCore 0:
  9.6 13.3 all-gather.7
  27.4 12.9 all-gather.5
  68.3 12.7 all-gather.3
  148.6 9.8 reduce-scatter.13
  175.1 9.7 reduce-scatter.9
  195.9 9.7 reduce-scatter.11
  294.8 92.1 all-reduce.1
where the time goes:
time: 399 us; the launch traced here: 396 us
  waiting for transfers between devices  132 us (33%)
  local copies, waits for them, and re-layouts  95.7 us (24%)
  blocking collectives  83.3 us (21%)
  matrix products  40.8 us (10%)
  starting transfers between devices  19.6 us (5%)
  between operations  14.5 us (4%)
  other arithmetic  9.79 us (2%)
    unnamed x38, local copies, waits for them, and re-layouts  75.7 us
    psum x1, blocking collectives, local(): lax.psum((table_part, router_part), ('expert', 'dp'))  75.6 us
    psum x1, waiting for transfers between devices, local(): lax.psum((table_part, router_part), ('expert', 'dp'))  69.8 us
    all_to_all x1, waiting for transfers between devices, local(): lax.all_to_all(send_rows.reshape(experts, capacity, model_width), 'expert...  31.6 us
    all_to_all x1, waiting for transfers between devices, local(): lax.all_to_all(send_cot.reshape(experts, capacity, model_width), 'expert'...  21.1 us
  transfers between devices with their start and end apart: 11, of which 5 were waited for; matrix products, arithmetic and copies ran while one was open for 29% of the time, Pallas kernels for 0%

commit v1 on v0

v1 whole, which is shorter than its diff:
```python
import functools

import jax
import jax.numpy as jnp
from jax import lax
from jax.experimental import pallas as pl
from jax.experimental.pallas import tpu as pltpu
from jax.sharding import PartitionSpec as P

epsilon = 1e-06
f32 = jnp.float32
bf16 = jnp.bfloat16
LANES = 128
VMEM = pl.BlockSpec(memory_space=pltpu.VMEM)
SMEM = pl.BlockSpec(memory_space=pltpu.SMEM)
ANY = pl.BlockSpec(memory_space=pl.ANY)


def params(mib):
    return pltpu.CompilerParams(vmem_limit_bytes=mib * 1024 * 1024)


def cost(flops, moved):
    return pl.CostEstimate(flops=int(flops), bytes_accessed=int(moved), transcendentals=0)


def dot(a, b, dims=((1,), (0,))):
    return lax.dot_general(a, b, (dims, ((), ())), preferred_element_type=f32)


def routing(me, meta_ref, count, cap):
    toks = meta_ref.shape[1]
    height = max(8, count)
    wanted = jnp.bitwise_xor(me, lax.broadcasted_iota(jnp.int32, (height, toks), 0))
    member = jnp.logical_or(meta_ref[0:1, :] == wanted, meta_ref[1:2, :] == wanted)
    earlier = lax.broadcasted_iota(jnp.int32, (toks, toks), 0) < lax.broadcasted_iota(
        jnp.int32, (toks, toks), 1
    )
    slots = dot(member.astype(f32).astype(bf16), earlier.astype(f32).astype(bf16))
    slots = jnp.where(member, slots, -1.0).astype(jnp.int32)
    place = lax.broadcasted_iota(jnp.int32, (cap, toks), 0)
    return [(slots[k : k + 1, :] == place).astype(f32) for k in range(count)]


def split3(table):
    high = table.astype(bf16)
    rest = table - high.astype(f32)
    middle = rest.astype(bf16)
    low = (rest - middle.astype(f32)).astype(bf16)
    return jnp.concatenate([high, middle, low], axis=0)


def pick3(column, conditions):
    lane = lax.broadcasted_iota(jnp.int32, (column.shape[0], 3 * conditions), 1)
    return (lax.rem(lane, conditions) + 1 == column.astype(jnp.int32)).astype(f32).astype(bf16)


def own_row(me, router_ref):
    table = router_ref[...].astype(f32)
    place = lax.broadcasted_iota(jnp.int32, table.shape, 0)
    return jnp.sum(jnp.where(place == me, table, 0.0), axis=0, keepdims=True)


def normalize(values):
    mean = jnp.mean(values, axis=-1, keepdims=True)
    centred = values - mean
    inverse = lax.rsqrt(jnp.mean(centred * centred, axis=-1, keepdims=True) + epsilon)
    return mean, inverse, centred * inverse


def pack_kernel(count, cap, stamps, me_ref, meta_ref, *refs):
    arrays, outs = refs[: len(stamps)], refs[len(stamps) :]
    picks = routing(me_ref[0], meta_ref, count, cap)
    whole = jnp.concatenate(picks, axis=0).astype(bf16)
    for index, stamped in enumerate(stamps):
        rows = dot(whole, arrays[index][...]).astype(bf16)
        width = rows.shape[1]
        for k in range(count):
            out = outs[index * count + k]
            out[:, :width] = rows[k * cap : (k + 1) * cap]
            if stamped:
                marks = picks[k] * (meta_ref[2:3, :] + 1).astype(f32)
                column = jnp.sum(marks, axis=1, keepdims=True)
                out[:, width:] = jnp.broadcast_to(column, (cap, LANES)).astype(bf16)


def pack(me, meta, arrays, stamps, count, cap):
    width = arrays[0].shape[1]
    outs = [
        jax.ShapeDtypeStruct((cap, width + LANES if stamped else width), bf16)
        for stamped in stamps
        for _ in range(count)
    ]
    outs = pl.pallas_call(
        functools.partial(pack_kernel, count, cap, stamps),
        out_shape=outs,
        in_specs=[SMEM] + [VMEM] * (1 + len(arrays)),
        out_specs=[VMEM] * len(outs),
        compiler_params=params(24),
        cost_estimate=cost(4e9, 2e6),
        name="pack",
    )(me, meta, *arrays)
    return [outs[i * count : (i + 1) * count] for i in range(len(arrays))]


def forward_kernel(count, me_ref, *refs):
    blocks, refs = refs[:count], refs[count:]
    table_ref, router_ref, gate_a, up_a, gate_b, up_b = refs[:6]
    mod_ref, stats_ref, act_ref, fac_ref, hid_ref = refs[6:11]
    weights, sems = refs[11:15], refs[15]
    copies = [
        pltpu.make_async_copy(source, target, sems.at[i])
        for i, (source, target) in enumerate(zip((gate_a, up_a, gate_b, up_b), weights))
    ]
    for copy in copies:
        copy.start()
    cap, width = blocks[0].shape[0], mod_ref.shape[1]
    half = weights[0].shape[1]
    conditions = table_ref.shape[1]
    shift_parts, scale_parts = split3(table_ref[0]), split3(table_ref[1])
    router_row = own_row(me_ref[0], router_ref)
    lane = lax.broadcasted_iota(jnp.int32, (cap, LANES), 1)
    for k in range(count):
        mean, inverse, normed = normalize(blocks[k][:, :width].astype(f32))
        mark = blocks[k][:, width : width + 1].astype(f32)
        pick = pick3(mark, conditions)
        rows = (normed * (1.0 + dot(pick, scale_parts)) + dot(pick, shift_parts)).astype(bf16)
        mod_ref[k * cap : (k + 1) * cap, :] = rows
        logit = jnp.sum(rows.astype(f32) * router_row, axis=1, keepdims=True)
        prob = jax.nn.sigmoid(logit)
        stats_ref[k * cap : (k + 1) * cap, :] = jnp.where(
            lane == 0, mean, jnp.where(lane == 1, inverse, jnp.where(lane == 2, prob, mark))
        )
    for part in range(2):
        copies[2 * part].wait()
        pre_gate = dot(mod_ref[...], weights[2 * part][...])
        copies[2 * part + 1].wait()
        pre_up = dot(mod_ref[...], weights[2 * part + 1][...])
        sig = jax.nn.sigmoid(pre_gate)
        active = pre_gate * sig
        columns = slice(part * half, (part + 1) * half)
        act_ref[:, columns] = active
        fac_ref[:, columns] = pre_up * sig * (1.0 + pre_gate * (1.0 - sig))
        hid_ref[:, columns] = (active * pre_up).astype(bf16)


def forward(me, blocks, table, router, gates, ups):
    count, cap, wide = len(blocks), *blocks[0].shape
    width, half = gates[0].shape
    rows = count * cap
    return pl.pallas_call(
        functools.partial(forward_kernel, count),
        out_shape=[
            jax.ShapeDtypeStruct((rows, width), bf16),
            jax.ShapeDtypeStruct((rows, LANES), f32),
            jax.ShapeDtypeStruct((rows, 2 * half), f32),
            jax.ShapeDtypeStruct((rows, 2 * half), f32),
            jax.ShapeDtypeStruct((rows, 2 * half), bf16),
        ],
        in_specs=[SMEM] + [VMEM] * (count + 2) + [ANY] * 4,
        out_specs=[VMEM] * 5,
        scratch_shapes=[pltpu.VMEM((width, half), bf16)] * 4 + [pltpu.SemaphoreType.DMA((4,))],
        compiler_params=params(40),
        cost_estimate=cost(8 * rows * width * half, 4 * 2 * width * half + rows * 12000),
        name="expert_in",
    )(me, *blocks, table, router, gates[0], ups[0], gates[1], ups[1])


def backward_kernel(count, me_ref, *refs):
    blocks, refs = refs[:count], refs[count:]
    table_ref, router_ref, stats_ref, act_ref, fac_ref, hid_ref = refs[:6]
    sources, refs = refs[6:12], refs[12:]
    backs, refs = refs[:count], refs[count:]
    og_ref, gg_ref, ug_ref, lg_ref = refs[:4]
    up_ref, weights, sems = refs[4], refs[5:11], refs[11]
    copies = [
        pltpu.make_async_copy(source, target, sems.at[i])
        for i, (source, target) in enumerate(zip(sources, weights))
    ]
    for copy in copies:
        copy.start()
    cap, width = blocks[0].shape
    half = weights[0].shape[1]
    conditions = table_ref.shape[1]
    gate_parts = split3(table_ref[2])
    prob = stats_ref[:, 2:3]
    for k in range(count):
        rows = slice(k * cap, (k + 1) * cap)
        pick = pick3(stats_ref[rows, 3:4], conditions)
        upstream = (dot(pick, gate_parts) * blocks[k][...].astype(f32)).astype(bf16)
        up_ref[rows, :] = upstream
        og_ref[rows, :] = (stats_ref[rows, 2:3] * upstream.astype(f32)).astype(bf16)
    prob_grad = jnp.zeros((count * cap, 1), f32)
    total = None
    for part in range(2):
        down, gate, up = (weights[3 * part + i] for i in range(3))
        columns = slice(part * half, (part + 1) * half)
        copies[3 * part].wait()
        raw = dot(up_ref[...], down[...])
        prob_grad += jnp.sum(hid_ref[:, columns].astype(f32) * raw, axis=1, keepdims=True)
        hidden_grad = prob * raw
        gate_grad = (hidden_grad * fac_ref[:, columns]).astype(bf16)
        up_grad = (hidden_grad * act_ref[:, columns]).astype(bf16)
        gg_ref[:, columns] = gate_grad
        ug_ref[:, columns] = up_grad
        copies[3 * part + 1].wait()
        term = dot(gate_grad, gate[...], ((1,), (1,)))
        copies[3 * part + 2].wait()
        term += dot(up_grad, up[...], ((1,), (1,)))
        total = term if total is None else total + term
    logit_grad = prob_grad * prob * (1.0 - prob)
    lg_ref[...] = jnp.broadcast_to(logit_grad, lg_ref.shape)
    router_row = own_row(me_ref[0], router_ref)
    total += logit_grad * router_row
    for k in range(count):
        backs[k][...] = total[k * cap : (k + 1) * cap].astype(bf16)


def backward(me, blocks, table, router, stats, act, fac, hid, weights):
    count, cap, width = len(blocks), *blocks[0].shape
    half = weights[0].shape[1]
    rows = count * cap
    outs = pl.pallas_call(
        functools.partial(backward_kernel, count),
        out_shape=[jax.ShapeDtypeStruct((cap, width), bf16)] * count
        + [
            jax.ShapeDtypeStruct((rows, width), bf16),
            jax.ShapeDtypeStruct((rows, 2 * half), bf16),
            jax.ShapeDtypeStruct((rows, 2 * half), bf16),
            jax.ShapeDtypeStruct((rows, LANES), f32),
        ],
        in_specs=[SMEM] + [VMEM] * (count + 6) + [ANY] * 6,
        out_specs=[VMEM] * (count + 4),
        scratch_shapes=[pltpu.VMEM((rows, width), bf16)]
        + [pltpu.VMEM((width, half), bf16)] * 6
        + [pltpu.SemaphoreType.DMA((6,))],
        compiler_params=params(40),
        cost_estimate=cost(12 * rows * width * half, 6 * 2 * width * half + rows * 16000),
        name="expert_back",
    )(me, *blocks, table, router, stats, act, fac, hid, *weights)
    return outs[:count], *outs[count:]


def sums_kernel(count, tall, me_ref, *refs):
    blocks, refs = refs[: 2 * count], refs[2 * count :]
    backs, refs = refs[: 2 * count], refs[2 * count :]
    mods, refs = refs[:2], refs[2:]
    stats, refs = refs[:2], refs[2:]
    lgs, refs = refs[:2], refs[2:]
    meta_ref, cot_ref, mix_ref, out_ref = refs
    cap, width = backs[0].shape
    conditions, experts = tall
    zero = ((0,), (0,))
    shift_sum = jnp.zeros((conditions, width), f32)
    scale_sum = jnp.zeros((conditions, width), f32)
    router_sum = jnp.zeros((1, width), f32)
    for index in range(2 * count):
        q, k = divmod(index, count)
        rows = slice(k * cap, (k + 1) * cap)
        lane = lax.broadcasted_iota(jnp.int32, (cap, conditions), 1)
        mark = stats[q][rows, 3:4].astype(jnp.int32)
        pick = (lane + 1 == mark).astype(f32).astype(bf16)
        back = backs[index][...]
        mean, inverse = stats[q][rows, 0:1], stats[q][rows, 1:2]
        normed = (blocks[index][:, :width].astype(f32) - mean) * inverse
        product = back.astype(f32) * normed
        high = product.astype(bf16)
        low = (product - high.astype(f32)).astype(bf16)
        shift_sum += dot(pick, back, zero)
        scale_sum += dot(pick, high, zero) + dot(pick, low, zero)
        weighted = lgs[q][rows, 0:1] * mods[q][rows, :].astype(f32)
        router_sum += jnp.sum(weighted, axis=0, keepdims=True)
    toks = cot_ref.shape[0]
    wanted = lax.broadcasted_iota(jnp.int32, (conditions, toks), 0)
    pick = (meta_ref[2:3, :] == wanted).astype(f32).astype(bf16)
    product = cot_ref[...].astype(f32) * mix_ref[...].astype(f32)
    high = product.astype(bf16)
    low = (product - high.astype(f32)).astype(bf16)
    out_ref[0:conditions, :] = shift_sum
    out_ref[conditions : 2 * conditions, :] = scale_sum
    out_ref[2 * conditions : 3 * conditions, :] = dot(pick, high) + dot(pick, low)
    place = lax.broadcasted_iota(jnp.int32, (out_ref.shape[0] - 3 * conditions, width), 0)
    out_ref[3 * conditions :, :] = jnp.where(place == me_ref[0], router_sum, 0.0)


def sums(me, blocks, backs, mods, stats, lgs, meta, cot, mix, conditions, experts):
    height = -(-(3 * conditions + experts) // 128) * 128
    width = cot.shape[1]
    count = len(blocks) // 2
    return pl.pallas_call(
        functools.partial(sums_kernel, count, (conditions, experts)),
        out_shape=jax.ShapeDtypeStruct((height, width), f32),
        in_specs=[SMEM] + [VMEM] * (4 * count + 9),
        out_specs=VMEM,
        compiler_params=params(40),
        cost_estimate=cost(4e9, 8e6),
        name="table_sums",
    )(me, *blocks, *backs, *mods, *stats, *lgs, meta, cot, mix)


def grads_kernel(*refs):
    mods, ogs, ggs, ugs, hids = (refs[2 * i : 2 * i + 2] for i in range(5))
    mine_ref, other_ref = refs[10:]
    half = mine_ref.shape[2]
    zero = ((0,), (0,))
    for index, (left, right) in enumerate(((mods, ggs), (mods, ugs), (ogs, hids))):
        total = dot(left[0][...], right[0][...], zero) + dot(left[1][...], right[1][...], zero)
        mine_ref[index] = total[:, :half].astype(bf16)
        other_ref[index] = total[:, half:].astype(bf16)


def grads(mods, ogs, ggs, ugs, hids):
    rows, width = mods[0].shape
    full = ggs[0].shape[1]
    step = 256
    left = pl.BlockSpec((rows, step), lambda i: (0, i))
    right = pl.BlockSpec((rows, full), lambda i: (0, 0))
    out = pl.BlockSpec((3, step, full // 2), lambda i: (0, i, 0))
    return pl.pallas_call(
        grads_kernel,
        grid=(width // step,),
        out_shape=[jax.ShapeDtypeStruct((3, width, full // 2), bf16)] * 2,
        in_specs=[left] * 4 + [right] * 6,
        out_specs=[out] * 2,
        compiler_params=params(40),
        cost_estimate=cost(12 * rows * width * full, 12e6),
        name="weight_grads",
    )(*mods, *ogs, *ggs, *ugs, *hids)


def final_kernel(count, cap, me_ref, meta_ref, stamp_ref, tok_ref, cot_ref, table_ref, *refs):
    backs, out_ref = refs[:count], refs[count]
    picks = jnp.concatenate(routing(me_ref[0], meta_ref, count, cap), axis=0).astype(bf16)
    rows = jnp.concatenate([back[...] for back in backs], axis=0)
    mod_grad = dot(picks, rows, ((0,), (0,)))
    conditions = table_ref.shape[1]
    _, inverse, normed = normalize(tok_ref[...].astype(f32))
    pick = pick3((stamp_ref[:, 0:1] + 1).astype(f32), conditions)
    d_normed = mod_grad * (1.0 + dot(pick, split3(table_ref[1])))
    d_input = inverse * (
        d_normed
        - jnp.mean(d_normed, axis=-1, keepdims=True)
        - normed * jnp.mean(d_normed * normed, axis=-1, keepdims=True)
    )
    out_ref[...] = (cot_ref[...].astype(f32) + d_input).astype(bf16)


def final(me, meta, stamp_column, tokens, cot, table, backs, cap):
    count = len(backs)
    return pl.pallas_call(
        functools.partial(final_kernel, count, cap),
        out_shape=jax.ShapeDtypeStruct(tokens.shape, bf16),
        in_specs=[SMEM] + [VMEM] * (5 + count),
        out_specs=VMEM,
        compiler_params=params(40),
        cost_estimate=cost(1e9, 4e6),
        name="final",
    )(me, meta, stamp_column, tokens, cot, table, *backs)


def reduce_table(table, axes):
    steps = []
    for name, size in axes:
        bit = 1
        while bit < size:
            steps.append((name, size, bit))
            bit *= 2
    for name, size, bit in steps:
        pairs = [(i, i ^ bit) for i in range(size)]
        high = (lax.axis_index(name) & bit) != 0
        rows = table.shape[0] // 2
        low_half, high_half = table[:rows], table[rows:]
        away = jnp.where(high, low_half, high_half).astype(bf16)
        table = jnp.where(high, high_half, low_half)
        table = table + lax.ppermute(away, name, pairs).astype(f32)
    table = table.astype(bf16)
    for name, size, bit in reversed(steps):
        pairs = [(i, i ^ bit) for i in range(size)]
        high = (lax.axis_index(name) & bit) != 0
        other = lax.ppermute(table, name, pairs)
        table = jnp.concatenate(
            [jnp.where(high, other, table), jnp.where(high, table, other)], axis=0
        )
    return table.astype(f32)


def local(experts_axis, dp_axis, tokens, cotangent, mixture, stamp, expert_ids, modulation, router, w_gate, w_up, w_down):
    toks, width = tokens.shape
    conditions = modulation.shape[1]
    experts = experts_axis
    cap = min(toks, 4 * toks // experts)
    half = experts // 2
    me = lax.axis_index("expert").astype(jnp.int32)[None]

    def hop(array, k):
        return lax.ppermute(array, "expert", [(e, e ^ k) for e in range(experts)])

    def swap(array):
        return lax.ppermute(array, "dp", [(i, dp_axis - 1 - i) for i in range(dp_axis)])

    meta = jnp.concatenate(
        [expert_ids.T, stamp[None], jnp.zeros((5, toks), jnp.int32)], axis=0
    )
    far_meta = hop(meta, half)
    far_tokens = hop(tokens, half)
    far_cot = hop(cotangent, half)
    (near_rows, near_cots) = pack(me, meta, [tokens, cotangent], (True, False), half, cap)
    near_rows = [near_rows[0]] + [hop(near_rows[k], k) for k in range(1, half)]
    near_cots = [near_cots[0]] + [hop(near_cots[k], k) for k in range(1, half)]
    gates = [w_gate[0], swap(w_gate[0])]
    ups = [w_up[0], swap(w_up[0])]
    downs = [w_down[0], swap(w_down[0])]
    weights = [downs[0], gates[0], ups[0], downs[1], gates[1], ups[1]]
    (far_rows,) = pack(me, far_meta, [far_tokens], (True,), half, cap)
    far_rows = [far_rows[0]] + [hop(far_rows[k], k) for k in range(1, half)]
    (far_cots,) = pack(me, far_meta, [far_cot], (False,), half, cap)
    far_cots = [far_cots[0]] + [hop(far_cots[k], k) for k in range(1, half)]

    mods, stats, backs, ogs, ggs, ugs, lgs, hids = ([] for _ in range(8))
    for rows, cots in ((near_rows, near_cots), (far_rows, far_cots)):
        mod, stat, act, fac, hid = forward(me, rows, modulation, router, gates, ups)
        back, og, gg, ug, lg = backward(
            me, cots, modulation, router, stat, act, fac, hid, weights
        )
        for group, item in zip(
            (mods, stats, ogs, ggs, ugs, lgs, hids), (mod, stat, og, gg, ug, lg, hid)
        ):
            group.append(item)
        backs += list(back)
    returned = [backs[0]] + [hop(backs[k], k) for k in range(1, experts)]
    table = sums(
        me, list(near_rows) + list(far_rows), backs, mods, stats, lgs,
        meta, cotangent, mixture, conditions, experts,
    )
    mine, other = grads(mods, ogs, ggs, ugs, hids)
    other = swap(other)
    table = reduce_table(table, (("dp", dp_axis), ("expert", experts)))
    total = (mine.astype(f32) + other.astype(f32)).astype(bf16)
    d_tokens = final(me, meta, stamp[:, None], tokens, cotangent, modulation, returned, cap)
    d_modulation = table[: 3 * conditions].reshape(3, conditions, width)
    d_router = table[3 * conditions : 3 * conditions + experts]
    return (d_tokens, total[0:1], total[1:2], total[2:3], d_router, d_modulation)


def solution(mesh):
    return jax.shard_map(
        functools.partial(local, mesh.shape["expert"], mesh.shape["dp"]),
        mesh=mesh,
        in_specs=(
            P(("groups", "expert", "dp"), None),
            P(("groups", "expert", "dp"), None),
            P(("groups", "expert", "dp"), None),
            P(("groups", "expert", "dp")),
            P(("groups", "expert", "dp"), None),
            P(),
            P(),
            P("expert", None, "dp"),
            P("expert", None, "dp"),
            P("expert", None, "dp"),
        ),
        out_specs=(
            P(("groups", "expert", "dp"), None),
            P(("groups", "expert"), None, "dp"),
            P(("groups", "expert"), None, "dp"),
            P(("groups", "expert"), None, "dp"),
            P("groups", None),
            P(None, "groups", None),
        ),
        check_vma=False,
    )
```

time: 399 us -> 193 us (0.48)
  the two profiles are of different devices: /device:TPU:1 before, /device:TPU:11 now
where the time goes in v1:
time: 193 us; the launch traced here: 192 us
  waiting for transfers between devices  64.3 us (33%)
  starting transfers between devices  50.8 us (26%)
  Pallas kernels  39.5 us (20%)
  local copies, waits for them, and re-layouts  27.1 us (14%)
  other arithmetic  9.29 us (5%)
    ppermute x22, waiting for transfers between devices, hop(): return lax.ppermute(array, 'expert', [(e, e ^ k) for e in range(experts)])  52.3 us
    ppermute x22, starting transfers between devices, hop(): return lax.ppermute(array, 'expert', [(e, e ^ k) for e in range(experts)])  33.4 us
    unnamed x146, local copies, waits for them, and re-layouts  25 us
    pallas_call x2, Pallas kernels, backward(): pl.pallas_call(functools.partial(backward_kernel, count), out_shape=[jax....  12.5 us
    ppermute x4, starting transfers between devices, reduce_table(): table = table + lax.ppermute(away, name, pairs).astype(f32)  10.4 us
    pallas_call x2, Pallas kernels, forward(): pl.pallas_call(functools.partial(forward_kernel, count), out_shape=[jax.S...  9.86 us
    pallas_call x1, Pallas kernels, grads(): pl.pallas_call(grads_kernel, grid=(width // step,), out_shape=[jax.ShapeD...  6.35 us
    ppermute x4, waiting for transfers between devices, reduce_table(): other = lax.ppermute(table, name, pairs)  6.33 us
  transfers between devices with their start and end apart: 34, of which 14 were waited for; matrix products, arithmetic and copies ran while one was open for 2% of the time, Pallas kernels for 15%

profile of v1, /device:TPU:11, one launch (start us, length us, event | category | flops | bytes accessed | tf_op | source)
XLA Modules:
  0.0 192.4 jit_solution(16901958315603422463)
XLA Ops:
  0.6 2.4 %collective-permute-start.17 = (bf16[128,1536]{1,0:T(8,128)(2,1)}, bf16[128,1536]{1,0:T(8,128)(2,1)S(1)}, u32[]{:S(2)}, u32[]{:S(2)}) collective-permute-start(bf16[128,1536]{1,0:T(8,128)(2,1)} %tok_ref.1), channel_id=1, source_target_pairs={{0,8},{2,10},{4,12},{6,14},{8,0},{10,2},{12,4},{14,6},{1,9},{3,11}... | collective-permute-start | bytes 1179656 | tf_op jit(solution)/shard_map/ppermute | solution.py:396
  5.8 2.2 %pack.3 = (bf16[64,1664]{1,0:T(8,128)(2,1)S(1)}, bf16[64,1664]{1,0:T(8,128)(2,1)S(1)}, bf16[64,1664]{1,0:T(8,128)(2,1)S(1)}, bf16[64,1664]{1,0:T(8,128)(2,1)}, b...) custom-call(s32[1]{0:T(128)} %bitcast.me_ref, ...), custom_call_target="tpu_custom_call" | custom-call | flops 4000000000 | bytes 2000000 | tf_op jit(solution)/shard_map/pack/pallas_call | solution.py:94
  11.4 1.2 collective-permute-start.3
  13.0 7.5 %collective-permute-done.12.meta_ref = s32[8,128]{1,0:T(8,128)S(1)} collective-permute-done((s32[8,128]{1,0:T(8,128)S(1)}, s32[8,128]{1,0:T(8,128)S(1)}, u32[]{:S(2)}, u32[]{:S(2)}) %collective-permute-start.12) | collective-permute-done | bytes 4128 | tf_op jit(solution)/shard_map/ppermute | solution.py:396
  20.6 3.1 %collective-permute-start.13 = (bf16[128,1536]{1,0:T(8,128)(2,1)}, bf16[128,1536]{1,0:T(8,128)(2,1)S(1)}, u32[]{:S(2)}, u32[]{:S(2)}) collective-permute-start(bf16[128,1536]{1,0:T(8,128)(2,1)} %refs_23_.1), channel_id=1, source_target_pairs={{0,8},{2,10},{4,12},{6,14},{8,0},{10,2},{12,4},{14,6},{1,9},{3,11}... | collective-permute-start | bytes 1179656 | tf_op jit(solution)/shard_map/ppermute | solution.py:396
  26.3 7.0 %collective-permute-done.4.refs_2_ = bf16[64,1664]{1,0:T(8,128)(2,1)S(1)} collective-permute-done((bf16[64,1664]{1,0:T(8,128)(2,1)S(1)}, bf16[64,1664]{1,0:T(8,128)(2,1)S(1)}, u32[]{:S(2)}, u32[]{:S(2)}) %collective-permute-start.4) | collective-permute-done | bytes 213024 | tf_op jit(solution)/shard_map/ppermute | solution.py:396
  33.3 1.2 collective-permute-start.18
  34.5 3.3 %collective-permute-done.13.refs_0_ = bf16[128,1536]{1,0:T(8,128)(2,1)S(1)} collective-permute-done((bf16[128,1536]{1,0:T(8,128)(2,1)}, bf16[128,1536]{1,0:T(8,128)(2,1)S(1)}, u32[]{:S(2)}, u32[]{:S(2)}) %collective-permute-start.13) | collective-permute-done | bytes 393248 | tf_op jit(solution)/shard_map/ppermute | solution.py:396
  37.9 1.3 collective-permute-start.19
  39.9 1.1 collective-permute-start.5
  41.0 1.6 collective-permute-done.19.refs_2_.refs_6_
  43.3 2.3 %collective-permute-start.20 = (bf16[64,1664]{1,0:T(8,128)(2,1)S(1)}, bf16[64,1664]{1,0:T(8,128)(2,1)S(1)}, u32[]{:S(2)}, u32[]{:S(2)}) collective-permute-start(bf16[64,1664]{1,0:T(8,128)(2,1)S(1)} %get-tuple-element.73), channel_id=1, source_target_pairs={{0,6},{2,4},{4,2},{6,0},{8,14},{10,12},{12,10},{14,8},{1,7},{3,5},... | collective-permute-start | bytes 638984 | tf_op jit(solution)/shard_map/ppermute | solution.py:396
  45.6 1.2 pack.4
  48.1 4.7 %collective-permute-done.20.refs_3_.refs_7_ = bf16[64,1664]{1,0:T(8,128)(2,1)S(1)} collective-permute-done((bf16[64,1664]{1,0:T(8,128)(2,1)S(1)}, bf16[64,1664]{1,0:T(8,128)(2,1)S(1)}, u32[]{:S(2)}, u32[]{:S(2)}) %collective-permute-start.20) | collective-permute-done | bytes 213024 | tf_op jit(solution)/shard_map/ppermute | solution.py:396
  54.9 1.3 collective-permute-start.16
  61.7 4.5 %expert_in.3 = (bf16[256,1536]{1,0:T(8,128)(2,1)S(1)}, f32[256,128]{1,0:T(8,128)S(1)}, f32[256,768]{1,0:T(8,128)S(1)}, f32[256,768]{1,0:T(8,128)S(1)}, bf16[256,768]{1,0:T(8,128)(2,1)S(1)}) custom-call(s32[1]{0:T(128)} %bitcast.me_ref, bf16[64,1664]{1,0:T(8,128)(2,1)S(1)} %copy-done.20, bf16[64,1664]{1,0:T(8,128)(2,1)S(1)} %copy-done.23, ...), custom_call_target="tpu_custom_call" | custom-call | flops 1207959552 | bytes 7790592 | tf_op jit(solution)/shard_map/expert_in/pallas_call | solution.py:151
  66.7 1.1 collective-permute-start.1
  67.8 1.3 collective-permute-start.2
  69.1 5.3 %expert_in.2 = (bf16[256,1536]{1,0:T(8,128)(2,1)S(1)}, f32[256,128]{1,0:T(8,128)S(1)}, f32[256,768]{1,0:T(8,128)S(1)}, f32[256,768]{1,0:T(8,128)S(1)}, bf16[256,768]{1,0:T(8,128)(2,1)S(1)}) custom-call(s32[1]{0:T(128)} %bitcast.me_ref, bf16[64,1664]{1,0:T(8,128)(2,1)S(1)} %copy-done.14, bf16[64,1664]{1,0:T(8,128)(2,1)S(1)} %copy-done.16, ...), custom_call_target="tpu_custom_call" | custom-call | flops 1207959552 | bytes 7790592 | tf_op jit(solution)/shard_map/expert_in/pallas_call | solution.py:151
  74.5 6.4 %expert_back.3 = (bf16[64,1536]{1,0:T(8,128)(2,1)S(1)}, bf16[64,1536]{1,0:T(8,128)(2,1)S(1)}, bf16[64,1536]{1,0:T(8,128)(2,1)S(1)}, bf16[64,1536]{1,0:T(8,128)(2...) custom-call(s32[1]{0:T(128)} %bitcast.me_ref, ...), custom_call_target="tpu_custom_call" | custom-call | flops 1811939328 | bytes 11173888 | tf_op jit(solution)/shard_map/expert_back/pallas_call | solution.py:223
  83.4 6.1 %expert_back.2 = (bf16[64,1536]{1,0:T(8,128)(2,1)S(1)}, bf16[64,1536]{1,0:T(8,128)(2,1)}, bf16[64,1536]{1,0:T(8,128)(2,1)}, bf16[64,1536]{1,0:T(8,128)(2,1)}, bf...) custom-call(s32[1]{0:T(128)} %bitcast.me_ref, ...), custom_call_target="tpu_custom_call" | custom-call | flops 1811939328 | bytes 11173888 | tf_op jit(solution)/shard_map/expert_back/pallas_call | solution.py:223
  89.7 3.9 %table_sums.1 = f32[128,1536]{1,0:T(8,128)S(1)} custom-call(s32[1]{0:T(128)} %bitcast.me_ref, bf16[64,1664]{1,0:T(8,128)(2,1)S(1)} %copy-done.14, bf16[64,1664]{1,0:T(8,128)(2,1)S(1)} %copy-done.16, bf16[64,1664]{1,0:T(8,128)(2,1)S(1)} %copy-done.18, bf16[64,1664]{1,0:T(8,128)(2,1)} %collective-permute-done.5.refs_3_, bf16[64,1664]{1,0:T(8,128)(2,1)S(1)} %copy-done.21, ...), custom_call_target="tpu_custom_call" | custom-call | flops 4000000000 | bytes 8000000 | tf_op jit(solution)/shard_map/table_sums/pallas_call | solution.py:290
  94.4 4.5 %collective-permute-start.26 = (bf16[64,1536]{1,0:T(8,128)(2,1)}, bf16[64,1536]{1,0:T(8,128)(2,1)}, u32[]{:S(2)}, u32[]{:S(2)}) collective-permute-start(bf16[64,1536]{1,0:T(8,128)(2,1)} %select_convert_fusion), channel_id=1, source_target_pairs={{0,1},{1,0},{2,3},{3,2},{4,5},{5,4},{6,7},{7,6},{8,9},{9,8},{10,11... | collective-permute-start | bytes 589832 | tf_op jit(solution)/shard_map/ppermute | solution.py:375
  98.9 1.4 collective-permute-done.26
  102.1 1.3 collective-permute-start.27
  103.4 2.8 %collective-permute-done.27 = bf16[32,1536]{1,0:T(8,128)(2,1)S(1)} collective-permute-done((bf16[32,1536]{1,0:T(8,128)(2,1)S(1)}, bf16[32,1536]{1,0:T(8,128)(2,1)S(1)}, u32[]{:S(2)}, u32[]{:S(2)}) %collective-permute-start.27) | collective-permute-done | bytes 98336 | tf_op jit(solution)/shard_map/ppermute | solution.py:375
  107.2 1.5 collective-permute-start.28
  108.8 1.5 collective-permute-done.28
  110.3 3.0 %collective-permute-start.29 = (bf16[8,1536]{1,0:T(8,128)(2,1)S(1)}, bf16[8,1536]{1,0:T(8,128)(2,1)S(1)}, u32[]{:S(2)}, u32[]{:S(2)}) collective-permute-start(bf16[8,1536]{1,0:T(8,128)(2,1)S(1)} %select_convert_fusion.3), channel_id=1, source_target_pairs={{0,8},{2,10},{4,12},{6,14},{8,0},{10,2},{12,4},{14,6},{1,9},{3,11}... | collective-permute-start | bytes 73736 | tf_op jit(solution)/shard_map/ppermute | solution.py:375
  113.4 1.1 copy-done.40
  114.5 1.1 copy-done.42
  118.6 6.4 %weight_grads.1 = (bf16[3,1536,384]{2,1,0:T(8,128)(2,1)S(1)}, bf16[3,1536,384]{2,1,0:T(8,128)(2,1)}) custom-call(bf16[256,1536]{1,0:T(8,128)(2,1)S(1)} %copy-done.38, bf16[256,1536]{1,0:T(8,128)(2,1)S(1)} %copy-done.36, bf16[256,1536]{1,0:T(8,128)(2,1)S(1)} %copy-done.42, bf16[256,1536]{1,0:T(8,128)(2,1)S(1)} %copy-done.40, bf16[256,768]{1,0:T(8,128)(2,1)S(1)} %copy-done.51, ...), custom_call_target="tpu_custom_call" | custom-call | flops 3623878656 | bytes 12000000 | tf_op jit(solution)/shard_map/weight_grads/pallas_call | solution.py:319
  125.0 1.7 copy-done.5
  126.7 2.7 %collective-permute-start.25 = (bf16[3,1536,384]{2,1,0:T(8,128)(2,1)}, bf16[3,1536,384]{2,1,0:T(8,128)(2,1)}, u32[]{:S(2)}, u32[]{:S(2)}) collective-permute-start(bf16[3,1536,384]{2,1,0:T(8,128)(2,1)} %get-tuple-element.91), channel_id=1, source_target_pairs={{0,1},{1,0},{2,3},{3,2},{4,5},{5,4},{6,7},{7,6},{8,9},{9,8},{10,11... | collective-permute-start | bytes 10616840 | tf_op jit(solution)/shard_map/ppermute | solution.py:399
  129.5 3.6 %collective-permute-done.30 = bf16[8,1536]{1,0:T(8,128)(2,1)S(1)} collective-permute-done((bf16[8,1536]{1,0:T(8,128)(2,1)S(1)}, bf16[8,1536]{1,0:T(8,128)(2,1)S(1)}, u32[]{:S(2)}, u32[]{:S(2)}) %collective-permute-start.30) | collective-permute-done | bytes 24608 | tf_op jit(solution)/shard_map/ppermute | solution.py:380
  133.4 2.8 %collective-permute-done.31 = bf16[16,1536]{1,0:T(8,128)(2,1)S(1)} collective-permute-done((bf16[16,1536]{1,0:T(8,128)(2,1)S(1)}, bf16[16,1536]{1,0:T(8,128)(2,1)S(1)}, u32[]{:S(2)}, u32[]{:S(2)}) %collective-permute-start.31) | collective-permute-done | bytes 49184 | tf_op jit(solution)/shard_map/ppermute | solution.py:380
  137.1 2.7 %collective-permute-start.22 = (bf16[64,1536]{1,0:T(8,128)(2,1)S(1)}, bf16[64,1536]{1,0:T(8,128)(2,1)S(1)}, u32[]{:S(2)}, u32[]{:S(2)}) collective-permute-start(bf16[64,1536]{1,0:T(8,128)(2,1)S(1)} %copy-done.61), channel_id=1, source_target_pairs={{0,10},{2,8},{4,14},{6,12},{8,2},{10,0},{12,6},{14,4},{1,11},{3,9}... | collective-permute-start | bytes 589832 | tf_op jit(solution)/shard_map/ppermute | solution.py:396
  139.8 2.0 %collective-permute-start.24 = (bf16[64,1536]{1,0:T(8,128)(2,1)S(1)}, bf16[64,1536]{1,0:T(8,128)(2,1)S(1)}, u32[]{:S(2)}, u32[]{:S(2)}) collective-permute-start(bf16[64,1536]{1,0:T(8,128)(2,1)S(1)} %copy-done.55), channel_id=1, source_target_pairs={{0,14},{2,12},{4,10},{6,8},{8,6},{10,4},{12,2},{14,0},{1,15},{3,13... | collective-permute-start | bytes 589832 | tf_op jit(solution)/shard_map/ppermute | solution.py:396
  141.8 15.5 %collective-permute-done.21.refs_4_ = bf16[64,1536]{1,0:T(8,128)(2,1)S(1)} collective-permute-done((bf16[64,1536]{1,0:T(8,128)(2,1)S(1)}, bf16[64,1536]{1,0:T(8,128)(2,1)S(1)}, u32[]{:S(2)}, u32[]{:S(2)}) %collective-permute-start.21) | collective-permute-done | bytes 196640 | tf_op jit(solution)/shard_map/ppermute | solution.py:396
  157.3 5.5 %collective-permute-start.10 = (bf16[64,1536]{1,0:T(8,128)(2,1)}, bf16[64,1536]{1,0:T(8,128)(2,1)S(1)}, u32[]{:S(2)}, u32[]{:S(2)}) collective-permute-start(bf16[64,1536]{1,0:T(8,128)(2,1)} %get-tuple-element.64.refs_10_), channel_id=1, source_target_pairs={{0,4},{2,6},{4,0},{6,2},{8,12},{10,14},{12,8},{14,10},{1,5},{3,7},... | collective-permute-start | bytes 589832 | tf_op jit(solution)/shard_map/ppermute | solution.py:396
  162.8 5.1 %collective-permute-start.11 = (bf16[64,1536]{1,0:T(8,128)(2,1)}, bf16[64,1536]{1,0:T(8,128)(2,1)S(1)}, u32[]{:S(2)}, u32[]{:S(2)}) collective-permute-start(bf16[64,1536]{1,0:T(8,128)(2,1)} %get-tuple-element.65.refs_11_), channel_id=1, source_target_pairs={{0,6},{2,4},{4,2},{6,0},{8,14},{10,12},{12,10},{14,8},{1,7},{3,5},... | collective-permute-start | bytes 589832 | tf_op jit(solution)/shard_map/ppermute | solution.py:396
  167.9 2.1 %collective-permute-done.23.refs_6_ = bf16[64,1536]{1,0:T(8,128)(2,1)S(1)} collective-permute-done((bf16[64,1536]{1,0:T(8,128)(2,1)S(1)}, bf16[64,1536]{1,0:T(8,128)(2,1)S(1)}, u32[]{:S(2)}, u32[]{:S(2)}) %collective-permute-start.23) | collective-permute-done | bytes 196640 | tf_op jit(solution)/shard_map/ppermute | solution.py:396
  170.1 7.1 %collective-permute-done.24.refs_7_ = bf16[64,1536]{1,0:T(8,128)(2,1)S(1)} collective-permute-done((bf16[64,1536]{1,0:T(8,128)(2,1)S(1)}, bf16[64,1536]{1,0:T(8,128)(2,1)S(1)}, u32[]{:S(2)}, u32[]{:S(2)}) %collective-permute-start.24) | collective-permute-done | bytes 196640 | tf_op jit(solution)/shard_map/ppermute | solution.py:396
  177.1 1.2 collective-permute-start.33
  178.4 3.5 %collective-permute-done.9.refs_1_ = bf16[64,1536]{1,0:T(8,128)(2,1)S(1)} collective-permute-done((bf16[64,1536]{1,0:T(8,128)(2,1)}, bf16[64,1536]{1,0:T(8,128)(2,1)S(1)}, u32[]{:S(2)}, u32[]{:S(2)}) %collective-permute-start.9) | collective-permute-done | bytes 196640 | tf_op jit(solution)/shard_map/ppermute | solution.py:396
  181.9 2.9 %final.1 = bf16[128,1536]{1,0:T(8,128)(2,1)} custom-call(s32[1]{0:T(128)} %bitcast.me_ref, s32[8,128]{1,0:T(8,128)S(1)} %add_add_fusion.meta_ref.refs_22_, s32[128,1]{1,0:T(8,128)S(1)} %copy.16.stamp_ref, bf16[128,1536]{1,0:T(8,128)(2,1)S(1)} %copy-done.45, bf16[128,1536]{1,0:T(8,128)(2,1)} %refs_23_.1, f32[3,32,1536]{2,1,0:T(8,128)S(1)} %copy-done.4, ...), custom_call_target="tpu_custom_call" | custom-call | flops 1000000000 | bytes 4000000 | tf_op jit(solution)/shard_map/final/pallas_call | solution.py:350
  187.3 3.1 %add_convert_fusion = bf16[3,1536,384]{2,1,0:T(8,128)(2,1)S(1)} fusion(bf16[3,1536,384]{2,1,0:T(8,128)(2,1)} %collective-permute-done.25, bf16[3,1536,384]{2,1,0:T(8,128)(2,1)S(1)} %copy-done.6), kind=kLoop, calls=%fused_computation | loop fusion | flops 7077888 | bytes 10616832 | tf_op jit(solution)/shard_map/convert_element_type | solution.py:438
  190.5 1.9 fusion.1
  (199 shorter events, 32.9 us)
Async XLA Ops:
  0.6 24.5 %collective-permute-start.17 = (bf16[128,1536]{1,0:T(8,128)(2,1)}, bf16[128,1536]{1,0:T(8,128)(2,1)S(1)}, u32[]{:S(2)}, u32[]{:S(2)}) collective-permute-start(bf16[128,1536]{1,0:T(8,128)(2,1)} %tok_ref.1), channel_id=1, source_target_pairs={{0,8},{2,10},{4,12},{6,14},{8,0},{10,2},{12,4},{14,6},{1,9},{3,11}... | collective-permute-start | bytes 1179656 | tf_op jit(solution)/shard_map/ppermute | solution.py:396
  3.0 50.8 %collective-permute-start.6 = (bf16[1536,384]{1,0:T(8,128)(2,1)}, bf16[1536,384]{1,0:T(8,128)(2,1)S(1)}, u32[]{:S(2)}, u32[]{:S(2)}) collective-permute-start(bf16[1536,384]{1,0:T(8,128)(2,1)} %bitcast.8), channel_id=1, source_target_pairs={{0,1},{1,0},{2,3},{3,2},{4,5},{5,4},{6,7},{7,6},{8,9},{9,8},{10,11... | collective-permute-start | bytes 3538952 | tf_op jit(solution)/shard_map/ppermute | solution.py:399
  11.4 12.2 %collective-permute-start.3 = (bf16[64,1664]{1,0:T(8,128)(2,1)S(1)}, bf16[64,1664]{1,0:T(8,128)(2,1)S(1)}, u32[]{:S(2)}, u32[]{:S(2)}) collective-permute-start(bf16[64,1664]{1,0:T(8,128)(2,1)S(1)} %get-tuple-element.55), channel_id=1, source_target_pairs={{0,2},{2,0},{4,6},{6,4},{8,10},{10,8},{12,14},{14,12},{1,3},{3,1},... | collective-permute-start | bytes 638984 | tf_op jit(solution)/shard_map/ppermute | solution.py:396
  12.7 42.2 %collective-permute-start.7 = (bf16[1536,384]{1,0:T(8,128)(2,1)S(1)}, bf16[1536,384]{1,0:T(8,128)(2,1)}, u32[]{:S(2)}, u32[]{:S(2)}) collective-permute-start(bf16[1536,384]{1,0:T(8,128)(2,1)S(1)} %bitcast.13), channel_id=1, source_target_pairs={{0,1},{1,0},{2,3},{3,2},{4,5},{5,4},{6,7},{7,6},{8,9},{9,8},{10,11... | collective-permute-start | bytes 3538952 | tf_op jit(solution)/shard_map/ppermute | solution.py:399
  13.0 7.6 %collective-permute-start.12 = (s32[8,128]{1,0:T(8,128)S(1)}, s32[8,128]{1,0:T(8,128)S(1)}, u32[]{:S(2)}, u32[]{:S(2)}) collective-permute-start(s32[8,128]{1,0:T(8,128)S(1)} %add_add_fusion.meta_ref.refs_22_), channel_id=1, source_target_pairs={{0,8},{2,10},{4,12},{6,14},{8,0},{10,2},{12,4},{14,6},{1,9},{3,11}... | collective-permute-start | bytes 12296 | tf_op jit(solution)/shard_map/ppermute | solution.py:396
  20.6 17.3 %collective-permute-start.13 = (bf16[128,1536]{1,0:T(8,128)(2,1)}, bf16[128,1536]{1,0:T(8,128)(2,1)S(1)}, u32[]{:S(2)}, u32[]{:S(2)}) collective-permute-start(bf16[128,1536]{1,0:T(8,128)(2,1)} %refs_23_.1), channel_id=1, source_target_pairs={{0,8},{2,10},{4,12},{6,14},{8,0},{10,2},{12,4},{14,6},{1,9},{3,11}... | collective-permute-start | bytes 1179656 | tf_op jit(solution)/shard_map/ppermute | solution.py:396
  24.3 50.1 %collective-permute-start.8 = (bf16[1536,384]{1,0:T(8,128)(2,1)}, bf16[1536,384]{1,0:T(8,128)(2,1)}, u32[]{:S(2)}, u32[]{:S(2)}) collective-permute-start(bf16[1536,384]{1,0:T(8,128)(2,1)} %bitcast.6.refs_10_), channel_id=1, source_target_pairs={{0,1},{1,0},{2,3},{3,2},{4,5},{5,4},{6,7},{7,6},{8,9},{9,8},{10,11... | collective-permute-start | bytes 3538952 | tf_op jit(solution)/shard_map/ppermute | solution.py:399
  25.1 8.2 %collective-permute-start.4 = (bf16[64,1664]{1,0:T(8,128)(2,1)S(1)}, bf16[64,1664]{1,0:T(8,128)(2,1)S(1)}, u32[]{:S(2)}, u32[]{:S(2)}) collective-permute-start(bf16[64,1664]{1,0:T(8,128)(2,1)S(1)} %get-tuple-element.56), channel_id=1, source_target_pairs={{0,4},{2,6},{4,0},{6,2},{8,12},{10,14},{12,8},{14,10},{1,5},{3,7},... | collective-permute-start | bytes 638984 | tf_op jit(solution)/shard_map/ppermute | solution.py:396
  33.3 5.9 %collective-permute-start.18 = (bf16[64,1664]{1,0:T(8,128)(2,1)S(1)}, bf16[64,1664]{1,0:T(8,128)(2,1)S(1)}, u32[]{:S(2)}, u32[]{:S(2)}) collective-permute-start(bf16[64,1664]{1,0:T(8,128)(2,1)S(1)} %get-tuple-element.71), channel_id=1, source_target_pairs={{0,2},{2,0},{4,6},{6,4},{8,10},{10,8},{12,14},{14,12},{1,3},{3,1},... | collective-permute-start | bytes 638984 | tf_op jit(solution)/shard_map/ppermute | solution.py:396
  37.9 4.7 %collective-permute-start.19 = (bf16[64,1664]{1,0:T(8,128)(2,1)S(1)}, bf16[64,1664]{1,0:T(8,128)(2,1)S(1)}, u32[]{:S(2)}, u32[]{:S(2)}) collective-permute-start(bf16[64,1664]{1,0:T(8,128)(2,1)S(1)} %get-tuple-element.72), channel_id=1, source_target_pairs={{0,4},{2,6},{4,0},{6,2},{8,12},{10,14},{12,8},{14,10},{1,5},{3,7},... | collective-permute-start | bytes 638984 | tf_op jit(solution)/shard_map/ppermute | solution.py:396
  39.9 26.4 %collective-permute-start.5 = (bf16[64,1664]{1,0:T(8,128)(2,1)}, bf16[64,1664]{1,0:T(8,128)(2,1)}, u32[]{:S(2)}, u32[]{:S(2)}) collective-permute-start(bf16[64,1664]{1,0:T(8,128)(2,1)} %get-tuple-element.57), channel_id=1, source_target_pairs={{0,6},{2,4},{4,2},{6,0},{8,14},{10,12},{12,10},{14,8},{1,7},{3,5},... | collective-permute-start | bytes 638984 | tf_op jit(solution)/shard_map/ppermute | solution.py:396
  43.3 9.5 %collective-permute-start.20 = (bf16[64,1664]{1,0:T(8,128)(2,1)S(1)}, bf16[64,1664]{1,0:T(8,128)(2,1)S(1)}, u32[]{:S(2)}, u32[]{:S(2)}) collective-permute-start(bf16[64,1664]{1,0:T(8,128)(2,1)S(1)} %get-tuple-element.73), channel_id=1, source_target_pairs={{0,6},{2,4},{4,2},{6,0},{8,14},{10,12},{12,10},{14,8},{1,7},{3,5},... | collective-permute-start | bytes 638984 | tf_op jit(solution)/shard_map/ppermute | solution.py:396
  53.5 13.2 %collective-permute-start.14 = (bf16[64,1536]{1,0:T(8,128)(2,1)}, bf16[64,1536]{1,0:T(8,128)(2,1)}, u32[]{:S(2)}, u32[]{:S(2)}) collective-permute-start(bf16[64,1536]{1,0:T(8,128)(2,1)} %get-tuple-element.67), channel_id=1, source_target_pairs={{0,2},{2,0},{4,6},{6,4},{8,10},{10,8},{12,14},{14,12},{1,3},{3,1},... | collective-permute-start | bytes 589832 | tf_op jit(solution)/shard_map/ppermute | solution.py:396
  53.8 14.0 %collective-permute-start.15 = (bf16[64,1536]{1,0:T(8,128)(2,1)}, bf16[64,1536]{1,0:T(8,128)(2,1)}, u32[]{:S(2)}, u32[]{:S(2)}) collective-permute-start(bf16[64,1536]{1,0:T(8,128)(2,1)} %get-tuple-element.68), channel_id=1, source_target_pairs={{0,4},{2,6},{4,0},{6,2},{8,12},{10,14},{12,8},{14,10},{1,5},{3,7},... | collective-permute-start | bytes 589832 | tf_op jit(solution)/shard_map/ppermute | solution.py:396
  54.9 19.6 %collective-permute-start.16 = (bf16[64,1536]{1,0:T(8,128)(2,1)}, bf16[64,1536]{1,0:T(8,128)(2,1)S(1)}, u32[]{:S(2)}, u32[]{:S(2)}) collective-permute-start(bf16[64,1536]{1,0:T(8,128)(2,1)} %copy-done.70), channel_id=1, source_target_pairs={{0,6},{2,4},{4,2},{6,0},{8,14},{10,12},{12,10},{14,8},{1,7},{3,5},... | collective-permute-start | bytes 589832 | tf_op jit(solution)/shard_map/ppermute | solution.py:396
  66.3 23.3 %copy-start.35 = (bf16[256,1536]{1,0:T(8,128)(2,1)}, bf16[256,1536]{1,0:T(8,128)(2,1)S(1)}, u32[]{:S(2)}) copy-start(bf16[256,1536]{1,0:T(8,128)(2,1)S(1)} %get-tuple-element.83.refs_1_.refs_17_) | copy-start | bytes 2359300
  66.3 17.0 %collective-permute-start = (bf16[64,1536]{1,0:T(8,128)(2,1)S(1)}, bf16[64,1536]{1,0:T(8,128)(2,1)S(1)}, u32[]{:S(2)}, u32[]{:S(2)}) collective-permute-start(bf16[64,1536]{1,0:T(8,128)(2,1)S(1)} %copy-done.69), channel_id=1, source_target_pairs={{0,2},{2,0},{4,6},{6,4},{8,10},{10,8},{12,14},{14,12},{1,3},{3,1},... | collective-permute-start | bytes 589832 | tf_op jit(solution)/shard_map/ppermute | solution.py:396
  66.7 16.7 %collective-permute-start.1 = (bf16[64,1536]{1,0:T(8,128)(2,1)S(1)}, bf16[64,1536]{1,0:T(8,128)(2,1)S(1)}, u32[]{:S(2)}, u32[]{:S(2)}) collective-permute-start(bf16[64,1536]{1,0:T(8,128)(2,1)S(1)} %copy-done.67), channel_id=1, source_target_pairs={{0,4},{2,6},{4,0},{6,2},{8,12},{10,14},{12,8},{14,10},{1,5},{3,7},... | collective-permute-start | bytes 589832 | tf_op jit(solution)/shard_map/ppermute | solution.py:396
  67.8 15.6 %collective-permute-start.2 = (bf16[64,1536]{1,0:T(8,128)(2,1)S(1)}, bf16[64,1536]{1,0:T(8,128)(2,1)S(1)}, u32[]{:S(2)}, u32[]{:S(2)}) collective-permute-start(bf16[64,1536]{1,0:T(8,128)(2,1)S(1)} %copy-done.65), channel_id=1, source_target_pairs={{0,6},{2,4},{4,2},{6,0},{8,14},{10,12},{12,10},{14,8},{1,7},{3,5},... | collective-permute-start | bytes 589832 | tf_op jit(solution)/shard_map/ppermute | solution.py:396
  74.4 15.2 %copy-start.37 = (bf16[256,1536]{1,0:T(8,128)(2,1)}, bf16[256,1536]{1,0:T(8,128)(2,1)S(1)}, u32[]{:S(2)}) copy-start(bf16[256,1536]{1,0:T(8,128)(2,1)S(1)} %get-tuple-element.82.refs_0_.refs_16_) | copy-start | bytes 2359300
  94.4 5.9 %collective-permute-start.26 = (bf16[64,1536]{1,0:T(8,128)(2,1)}, bf16[64,1536]{1,0:T(8,128)(2,1)}, u32[]{:S(2)}, u32[]{:S(2)}) collective-permute-start(bf16[64,1536]{1,0:T(8,128)(2,1)} %select_convert_fusion), channel_id=1, source_target_pairs={{0,1},{1,0},{2,3},{3,2},{4,5},{5,4},{6,7},{7,6},{8,9},{9,8},{10,11... | collective-permute-start | bytes 589832 | tf_op jit(solution)/shard_map/ppermute | solution.py:375
  98.9 14.4 %copy-start.12 = (bf16[256,768]{1,0:T(8,128)(2,1)S(1)}, bf16[256,768]{1,0:T(8,128)(2,1)}, u32[]{:S(2)}) copy-start(bf16[256,768]{1,0:T(8,128)(2,1)} %copy-done.11) | copy-start | bytes 1179652
  98.9 14.4 %copy-start.36 = (bf16[256,1536]{1,0:T(8,128)(2,1)S(1)}, bf16[256,1536]{1,0:T(8,128)(2,1)}, u32[]{:S(2)}) copy-start(bf16[256,1536]{1,0:T(8,128)(2,1)} %copy-done.35) | copy-start | bytes 2359300
  98.9 14.4 %copy-start.38 = (bf16[256,1536]{1,0:T(8,128)(2,1)S(1)}, bf16[256,1536]{1,0:T(8,128)(2,1)}, u32[]{:S(2)}) copy-start(bf16[256,1536]{1,0:T(8,128)(2,1)} %copy-done.37) | copy-start | bytes 2359300
  98.9 14.4 %copy-start.47 = (bf16[256,768]{1,0:T(8,128)(2,1)S(1)}, bf16[256,768]{1,0:T(8,128)(2,1)}, u32[]{:S(2)}) copy-start(bf16[256,768]{1,0:T(8,128)(2,1)} %copy-done.46) | copy-start | bytes 1179652
  102.1 4.1 %collective-permute-start.27 = (bf16[32,1536]{1,0:T(8,128)(2,1)S(1)}, bf16[32,1536]{1,0:T(8,128)(2,1)S(1)}, u32[]{:S(2)}, u32[]{:S(2)}) collective-permute-start(bf16[32,1536]{1,0:T(8,128)(2,1)S(1)} %select_convert_fusion.1), channel_id=1, source_target_pairs={{0,2},{2,0},{4,6},{6,4},{8,10},{10,8},{12,14},{14,12},{1,3},{3,1},... | collective-permute-start | bytes 294920 | tf_op jit(solution)/shard_map/ppermute | solution.py:375
  107.2 3.0 %collective-permute-start.28 = (bf16[16,1536]{1,0:T(8,128)(2,1)S(1)}, bf16[16,1536]{1,0:T(8,128)(2,1)S(1)}, u32[]{:S(2)}, u32[]{:S(2)}) collective-permute-start(bf16[16,1536]{1,0:T(8,128)(2,1)S(1)} %select_convert_fusion.2), channel_id=1, source_target_pairs={{0,4},{2,6},{4,0},{6,2},{8,12},{10,14},{12,8},{14,10},{1,5},{3,7},... | collective-permute-start | bytes 147464 | tf_op jit(solution)/shard_map/ppermute | solution.py:375
  110.3 19.1 %collective-permute-start.29 = (bf16[8,1536]{1,0:T(8,128)(2,1)S(1)}, bf16[8,1536]{1,0:T(8,128)(2,1)S(1)}, u32[]{:S(2)}, u32[]{:S(2)}) collective-permute-start(bf16[8,1536]{1,0:T(8,128)(2,1)S(1)} %select_convert_fusion.3), channel_id=1, source_target_pairs={{0,8},{2,10},{4,12},{6,14},{8,0},{10,2},{12,4},{14,6},{1,9},{3,11}... | collective-permute-start | bytes 73736 | tf_op jit(solution)/shard_map/ppermute | solution.py:375
  118.6 18.4 %copy-start.63 = (bf16[64,1536]{1,0:T(8,128)(2,1)S(1)}, bf16[64,1536]{1,0:T(8,128)(2,1)}, u32[]{:S(2)}) copy-start(bf16[64,1536]{1,0:T(8,128)(2,1)} %copy-done.62) | copy-start | bytes 589828
  118.6 18.4 %copy-start.61 = (bf16[64,1536]{1,0:T(8,128)(2,1)S(1)}, bf16[64,1536]{1,0:T(8,128)(2,1)}, u32[]{:S(2)}) copy-start(bf16[64,1536]{1,0:T(8,128)(2,1)} %copy-done.60) | copy-start | bytes 589828
  118.6 21.2 %copy-start.59 = (bf16[64,1536]{1,0:T(8,128)(2,1)S(1)}, bf16[64,1536]{1,0:T(8,128)(2,1)}, u32[]{:S(2)}) copy-start(bf16[64,1536]{1,0:T(8,128)(2,1)} %copy-done.58) | copy-start | bytes 589828
  118.6 21.2 %copy-start.55 = (bf16[64,1536]{1,0:T(8,128)(2,1)S(1)}, bf16[64,1536]{1,0:T(8,128)(2,1)}, u32[]{:S(2)}) copy-start(bf16[64,1536]{1,0:T(8,128)(2,1)} %copy-done.54) | copy-start | bytes 589828
  126.7 51.6 %copy-start.72 = (s32[128]{0:T(128)S(1)}, s32[128]{0:T(128)}, u32[]{:S(2)}) copy-start(s32[128]{0:T(128)} %param.13) | copy-start | bytes 1540
  126.7 55.2 %copy-start.4 = (f32[3,32,1536]{2,1,0:T(8,128)S(1)}, f32[3,32,1536]{2,1,0:T(8,128)}, u32[]{:S(2)}) copy-start(f32[3,32,1536]{2,1,0:T(8,128)} %table_ref.1) | copy-start | bytes 1769476
  126.7 55.2 %copy-start.45 = (bf16[128,1536]{1,0:T(8,128)(2,1)S(1)}, bf16[128,1536]{1,0:T(8,128)(2,1)}, u32[]{:S(2)}) copy-start(bf16[128,1536]{1,0:T(8,128)(2,1)} %tok_ref.1) | copy-start | bytes 1179652
  126.7 55.2 %copy-start.57 = (bf16[64,1536]{1,0:T(8,128)(2,1)S(1)}, bf16[64,1536]{1,0:T(8,128)(2,1)}, u32[]{:S(2)}) copy-start(bf16[64,1536]{1,0:T(8,128)(2,1)} %copy-done.56) | copy-start | bytes 589828
  126.7 60.6 %collective-permute-start.25 = (bf16[3,1536,384]{2,1,0:T(8,128)(2,1)}, bf16[3,1536,384]{2,1,0:T(8,128)(2,1)}, u32[]{:S(2)}, u32[]{:S(2)}) collective-permute-start(bf16[3,1536,384]{2,1,0:T(8,128)(2,1)} %get-tuple-element.91), channel_id=1, source_target_pairs={{0,1},{1,0},{2,3},{3,2},{4,5},{5,4},{6,7},{7,6},{8,9},{9,8},{10,11... | collective-permute-start | bytes 10616840 | tf_op jit(solution)/shard_map/ppermute | solution.py:399
  129.5 3.6 %collective-permute-start.30 = (bf16[8,1536]{1,0:T(8,128)(2,1)S(1)}, bf16[8,1536]{1,0:T(8,128)(2,1)S(1)}, u32[]{:S(2)}, u32[]{:S(2)}) collective-permute-start(bf16[8,1536]{1,0:T(8,128)(2,1)S(1)} %add_convert_fusion.1), channel_id=1, source_target_pairs={{0,8},{2,10},{4,12},{6,14},{8,0},{10,2},{12,4},{14,6},{1,9},{3,11}... | collective-permute-start | bytes 73736 | tf_op jit(solution)/shard_map/ppermute | solution.py:380
  133.1 3.0 %collective-permute-start.31 = (bf16[16,1536]{1,0:T(8,128)(2,1)S(1)}, bf16[16,1536]{1,0:T(8,128)(2,1)S(1)}, u32[]{:S(2)}, u32[]{:S(2)}) collective-permute-start(bf16[16,1536]{1,0:T(8,128)(2,1)S(1)} %pad_maximum_fusion.3), channel_id=1, source_target_pairs={{0,4},{2,6},{4,0},{6,2},{8,12},{10,14},{12,8},{14,10},{1,5},{3,7},... | collective-permute-start | bytes 147464 | tf_op jit(solution)/shard_map/ppermute | solution.py:380
  136.2 3.6 %collective-permute-start.32 = (bf16[32,1536]{1,0:T(8,128)(2,1)S(1)}, bf16[32,1536]{1,0:T(8,128)(2,1)S(1)}, u32[]{:S(2)}, u32[]{:S(2)}) collective-permute-start(bf16[32,1536]{1,0:T(8,128)(2,1)S(1)} %pad_maximum_fusion.2), channel_id=1, source_target_pairs={{0,2},{2,0},{4,6},{6,4},{8,10},{10,8},{12,14},{14,12},{1,3},{3,1},... | collective-permute-start | bytes 294920 | tf_op jit(solution)/shard_map/ppermute | solution.py:380
  137.1 20.2 %collective-permute-start.21 = (bf16[64,1536]{1,0:T(8,128)(2,1)S(1)}, bf16[64,1536]{1,0:T(8,128)(2,1)S(1)}, u32[]{:S(2)}, u32[]{:S(2)}) collective-permute-start(bf16[64,1536]{1,0:T(8,128)(2,1)S(1)} %copy-done.63), channel_id=1, source_target_pairs={{0,8},{2,10},{4,12},{6,14},{8,0},{10,2},{12,4},{14,6},{1,9},{3,11}... | collective-permute-start | bytes 589832 | tf_op jit(solution)/shard_map/ppermute | solution.py:396
  137.1 25.8 %collective-permute-start.22 = (bf16[64,1536]{1,0:T(8,128)(2,1)S(1)}, bf16[64,1536]{1,0:T(8,128)(2,1)S(1)}, u32[]{:S(2)}, u32[]{:S(2)}) collective-permute-start(bf16[64,1536]{1,0:T(8,128)(2,1)S(1)} %copy-done.61), channel_id=1, source_target_pairs={{0,10},{2,8},{4,14},{6,12},{8,2},{10,0},{12,6},{14,4},{1,11},{3,9}... | collective-permute-start | bytes 589832 | tf_op jit(solution)/shard_map/ppermute | solution.py:396
  139.8 30.3 %collective-permute-start.23 = (bf16[64,1536]{1,0:T(8,128)(2,1)S(1)}, bf16[64,1536]{1,0:T(8,128)(2,1)S(1)}, u32[]{:S(2)}, u32[]{:S(2)}) collective-permute-start(bf16[64,1536]{1,0:T(8,128)(2,1)S(1)} %copy-done.59), channel_id=1, source_target_pairs={{0,12},{2,14},{4,8},{6,10},{8,4},{10,6},{12,0},{14,2},{1,13},{3,15... | collective-permute-start | bytes 589832 | tf_op jit(solution)/shard_map/ppermute | solution.py:396
  139.8 37.3 %collective-permute-start.24 = (bf16[64,1536]{1,0:T(8,128)(2,1)S(1)}, bf16[64,1536]{1,0:T(8,128)(2,1)S(1)}, u32[]{:S(2)}, u32[]{:S(2)}) collective-permute-start(bf16[64,1536]{1,0:T(8,128)(2,1)S(1)} %copy-done.55), channel_id=1, source_target_pairs={{0,14},{2,12},{4,10},{6,8},{8,6},{10,4},{12,2},{14,0},{1,15},{3,13... | collective-permute-start | bytes 589832 | tf_op jit(solution)/shard_map/ppermute | solution.py:396
  157.3 21.1 %collective-permute-start.10 = (bf16[64,1536]{1,0:T(8,128)(2,1)}, bf16[64,1536]{1,0:T(8,128)(2,1)S(1)}, u32[]{:S(2)}, u32[]{:S(2)}) collective-permute-start(bf16[64,1536]{1,0:T(8,128)(2,1)} %get-tuple-element.64.refs_10_), channel_id=1, source_target_pairs={{0,4},{2,6},{4,0},{6,2},{8,12},{10,14},{12,8},{14,10},{1,5},{3,7},... | collective-permute-start | bytes 589832 | tf_op jit(solution)/shard_map/ppermute | solution.py:396
  162.8 15.6 %collective-permute-start.11 = (bf16[64,1536]{1,0:T(8,128)(2,1)}, bf16[64,1536]{1,0:T(8,128)(2,1)S(1)}, u32[]{:S(2)}, u32[]{:S(2)}) collective-permute-start(bf16[64,1536]{1,0:T(8,128)(2,1)} %get-tuple-element.65.refs_11_), channel_id=1, source_target_pairs={{0,6},{2,4},{4,2},{6,0},{8,14},{10,12},{12,10},{14,8},{1,7},{3,5},... | collective-permute-start | bytes 589832 | tf_op jit(solution)/shard_map/ppermute | solution.py:396
  170.1 11.9 %collective-permute-start.9 = (bf16[64,1536]{1,0:T(8,128)(2,1)}, bf16[64,1536]{1,0:T(8,128)(2,1)S(1)}, u32[]{:S(2)}, u32[]{:S(2)}) collective-permute-start(bf16[64,1536]{1,0:T(8,128)(2,1)} %get-tuple-element.63.refs_9_), channel_id=1, source_target_pairs={{0,2},{2,0},{4,6},{6,4},{8,10},{10,8},{12,14},{14,12},{1,3},{3,1},... | collective-permute-start | bytes 589832 | tf_op jit(solution)/shard_map/ppermute | solution.py:396
  177.1 7.7 %collective-permute-start.33 = (bf16[64,1536]{1,0:T(8,128)(2,1)S(1)}, bf16[64,1536]{1,0:T(8,128)(2,1)}, u32[]{:S(2)}, u32[]{:S(2)}) collective-permute-start(bf16[64,1536]{1,0:T(8,128)(2,1)S(1)} %pad_maximum_fusion.1), channel_id=1, source_target_pairs={{0,1},{1,0},{2,3},{3,2},{4,5},{5,4},{6,7},{7,6},{8,9},{9,8},{10,11... | collective-permute-start | bytes 589832 | tf_op jit(solution)/shard_map/ppermute | solution.py:380
  (59 other events, 234.9 us)

commit v2 on v1

v2 whole, which is shorter than its diff:
```python
import functools

import jax
import jax.numpy as jnp
from jax import lax
from jax.experimental import pallas as pl
from jax.experimental.pallas import tpu as pltpu
from jax.sharding import PartitionSpec as P

epsilon = 1e-06
f32 = jnp.float32
bf16 = jnp.bfloat16
LANES = 128
VMEM = pl.BlockSpec(memory_space=pltpu.VMEM)
SMEM = pl.BlockSpec(memory_space=pltpu.SMEM)


def params(mib):
    return pltpu.CompilerParams(vmem_limit_bytes=mib * 1024 * 1024)


def cost(flops, moved):
    return pl.CostEstimate(flops=int(flops), bytes_accessed=int(moved), transcendentals=0)


def dot(a, b, dims=((1,), (0,))):
    return lax.dot_general(a, b, (dims, ((), ())), preferred_element_type=f32)


def routing(base, flip, meta_ref, count, cap):
    toks = meta_ref.shape[1]
    height = max(8, count)
    wanted = base + jnp.bitwise_xor(
        flip, lax.broadcasted_iota(jnp.int32, (height, toks), 0)
    )
    member = jnp.logical_or(meta_ref[0:1, :] == wanted, meta_ref[1:2, :] == wanted)
    earlier = lax.broadcasted_iota(jnp.int32, (toks, toks), 0) < lax.broadcasted_iota(
        jnp.int32, (toks, toks), 1
    )
    slots = dot(member.astype(f32).astype(bf16), earlier.astype(f32).astype(bf16))
    slots = jnp.where(member, slots, -1.0).astype(jnp.int32)
    place = lax.broadcasted_iota(jnp.int32, (cap, toks), 0)
    picks = [(slots[k : k + 1, :] == place).astype(f32) for k in range(count)]
    return jnp.concatenate(picks, axis=0)


def split3(table):
    high = table.astype(bf16)
    rest = table - high.astype(f32)
    middle = rest.astype(bf16)
    low = (rest - middle.astype(f32)).astype(bf16)
    return jnp.concatenate([high, middle, low], axis=0)


def pick3(column, conditions):
    lane = lax.broadcasted_iota(jnp.int32, (column.shape[0], 3 * conditions), 1)
    return (lax.rem(lane, conditions) + 1 == column.astype(jnp.int32)).astype(f32).astype(bf16)


def own_row(me, router_ref):
    table = router_ref[...].astype(f32)
    place = lax.broadcasted_iota(jnp.int32, table.shape, 0)
    return jnp.sum(jnp.where(place == me, table, 0.0), axis=0, keepdims=True)


def normalize(values):
    mean = jnp.mean(values, axis=-1, keepdims=True)
    centred = values - mean
    inverse = lax.rsqrt(jnp.mean(centred * centred, axis=-1, keepdims=True) + epsilon)
    return mean, inverse, centred * inverse


def piece(refs, start, size, columns):
    height = refs[0].shape[0]
    if size <= height:
        block, row = divmod(start, height)
        return refs[block][row : row + size, columns]
    parts = [refs[start // height + i][:, columns] for i in range(size // height)]
    return jnp.concatenate(parts, axis=0)


def put(refs, start, values, columns):
    height = refs[0].shape[0]
    size = values.shape[0]
    if size <= height:
        block, row = divmod(start, height)
        refs[block][row : row + size, columns] = values
    else:
        for i in range(size // height):
            refs[start // height + i][:, columns] = values[i * height : (i + 1) * height]


def pack_kernel(count, cap, number, flipped, stamped, me_ref, meta_ref, *refs):
    arrays, outs = refs[:number], refs[number:]
    flip = me_ref[0] - me_ref[1] if flipped else 0
    picks = routing(me_ref[1], flip, meta_ref, count, cap)
    whole = picks.astype(bf16)
    total = count * cap
    width = arrays[0].shape[1]
    put(outs, 0, dot(whole, arrays[0][...]).astype(bf16), slice(0, width))
    at = width
    if stamped:
        column = jnp.sum(picks * (meta_ref[2:3, :] + 1).astype(f32), axis=1, keepdims=True)
        put(outs, 0, jnp.broadcast_to(column, (total, LANES)).astype(bf16), slice(at, at + LANES))
        at += LANES
    for array in arrays[1:]:
        put(outs, 0, dot(whole, array[...]).astype(bf16), slice(at, at + width))
        at += width


def pack(me, meta, arrays, stamped, flipped, count, cap):
    width = arrays[0].shape[1] * len(arrays) + (LANES if stamped else 0)
    shape = (cap, width) if flipped else (count * cap, width)
    number = count if flipped else 1
    return pl.pallas_call(
        functools.partial(pack_kernel, count, cap, len(arrays), flipped, stamped),
        out_shape=[jax.ShapeDtypeStruct(shape, bf16)] * number,
        in_specs=[SMEM] + [VMEM] * (1 + len(arrays)),
        out_specs=[VMEM] * number,
        compiler_params=params(8),
        cost_estimate=cost(1e9, 4e6),
        name="pack",
    )(me, meta, *arrays)


def late_views(late_ref, width, full):
    edges = [0, width, 2 * width, 2 * width + full, 2 * width + 2 * full, 2 * width + 3 * full]
    return [late_ref.at[:, low:high] for low, high in zip(edges, edges[1:])]


def forward_body(me_ref, ins, table_ref, router_ref, gate_ref, up_ref, mod_ref, stats_ref, act_ref, fac_ref, hid_ref):
    count, width = mod_ref.shape
    full = gate_ref.shape[1]
    conditions = table_ref.shape[1]
    chunk = 64
    shift_parts, scale_parts = split3(table_ref[0]), split3(table_ref[1])
    router_row = own_row(me_ref[0], router_ref)
    lane = lax.broadcasted_iota(jnp.int32, (chunk, LANES), 1)
    for start in range(0, count, chunk):
        part = slice(start, start + chunk)
        mean, inverse, normed = normalize(piece(ins, start, chunk, slice(0, width)).astype(f32))
        mark = piece(ins, start, chunk, slice(width, width + 1)).astype(f32)
        pick = pick3(mark, conditions)
        rows = (normed * (1.0 + dot(pick, scale_parts)) + dot(pick, shift_parts)).astype(bf16)
        mod_ref[part, :] = rows
        logit = jnp.sum(rows.astype(f32) * router_row, axis=1, keepdims=True)
        prob = jax.nn.sigmoid(logit)
        stats_ref[part, :] = jnp.where(
            lane == 0, mean, jnp.where(lane == 1, inverse, jnp.where(lane == 2, prob, mark))
        )
    step = 256
    for start in range(0, full, step):
        columns = slice(start, start + step)
        pre_gate = dot(mod_ref[...], gate_ref[:, columns])
        pre_up = dot(mod_ref[...], up_ref[:, columns])
        sig = jax.nn.sigmoid(pre_gate)
        active = pre_gate * sig
        act_ref[:, columns] = active
        fac_ref[:, columns] = pre_up * sig * (1.0 + pre_gate * (1.0 - sig))
        hid_ref[:, columns] = (active * pre_up).astype(bf16)


def backward_body(offset, me_ref, cots, table_ref, router_ref, stats_ref, act_ref, fac_ref, hid_ref, down_ref, gate_ref, up_ref, backs, og_ref, gg_ref, ug_ref, lg_ref, ups_ref):
    count, width = og_ref.shape
    full = gate_ref.shape[1]
    conditions = table_ref.shape[1]
    gate_parts = split3(table_ref[2])
    prob = stats_ref[:, 2:3]
    chunk = 64
    for start in range(0, count, chunk):
        part = slice(start, start + chunk)
        pick = pick3(stats_ref[part, 3:4], conditions)
        cot = piece(cots, start, chunk, slice(offset, offset + width)).astype(f32)
        upstream = (dot(pick, gate_parts) * cot).astype(bf16)
        ups_ref[part, :] = upstream
        og_ref[part, :] = (stats_ref[part, 2:3] * upstream.astype(f32)).astype(bf16)
    prob_grad = jnp.zeros((count, 1), f32)
    step = 256
    for start in range(0, full, step):
        columns = slice(start, start + step)
        raw = dot(ups_ref[...], down_ref[:, columns])
        prob_grad += jnp.sum(hid_ref[:, columns].astype(f32) * raw, axis=1, keepdims=True)
        hidden_grad = prob * raw
        gg_ref[:, columns] = (hidden_grad * fac_ref[:, columns]).astype(bf16)
        ug_ref[:, columns] = (hidden_grad * act_ref[:, columns]).astype(bf16)
    logit_grad = prob_grad * prob * (1.0 - prob)
    lane = lax.broadcasted_iota(jnp.int32, stats_ref.shape, 1)
    lg_ref[...] = jnp.where(lane == 4, logit_grad, stats_ref[...])
    router_row = own_row(me_ref[0], router_ref)
    for start in range(0, width, step):
        part = slice(start, start + step)
        total = dot(gg_ref[...], gate_ref[part, :], ((1,), (1,)))
        total += dot(ug_ref[...], up_ref[part, :], ((1,), (1,)))
        put(backs, 0, (total + logit_grad * router_row[:, part]).astype(bf16), part)


def forward_kernel(number, me_ref, *refs):
    forward_body(me_ref, refs[:number], *refs[number:])


def forward(me, blocks, table, router, gate, up):
    count = sum(block.shape[0] for block in blocks)
    width, full = gate.shape
    wide = jax.ShapeDtypeStruct((count, full), f32)
    return pl.pallas_call(
        functools.partial(forward_kernel, len(blocks)),
        out_shape=[
            jax.ShapeDtypeStruct((count, width), bf16),
            jax.ShapeDtypeStruct((count, LANES), f32),
            wide,
            wide,
            jax.ShapeDtypeStruct((count, full), bf16),
        ],
        in_specs=[SMEM] + [VMEM] * (len(blocks) + 4),
        out_specs=[VMEM] * 5,
        compiler_params=params(12),
        cost_estimate=cost(4 * count * width * full, 4 * width * full + count * 12000),
        name="expert_in",
    )(me, *blocks, table, router, gate, up)


def backward_shapes(blocks, width, full):
    count = sum(block.shape[0] for block in blocks)
    return [jax.ShapeDtypeStruct((block.shape[0], width), bf16) for block in blocks] + [
        jax.ShapeDtypeStruct((count, 2 * width + 3 * full), bf16),
        jax.ShapeDtypeStruct((count, LANES), f32),
    ]


def backward_kernel(number, me_ref, *refs):
    cots, refs = refs[:number], refs[number:]
    table_ref, router_ref, seen_ref, stats_ref, act_ref, fac_ref, hid_ref, down_ref, gate_ref, up_ref = refs[:10]
    backs, (late_ref, lg_ref, ups_ref) = refs[10 : 10 + number], refs[10 + number :]
    mod, og, gg, ug, hid = late_views(late_ref, *gate_ref.shape)
    backward_body(0, me_ref, cots, table_ref, router_ref, stats_ref, act_ref, fac_ref, hid_ref, down_ref, gate_ref, up_ref, backs, og, gg, ug, lg_ref, ups_ref)
    mod[...] = seen_ref[...]
    hid[...] = hid_ref[...]


def backward(me, blocks, table, router, mod, stats, act, fac, hid, down, gate, up):
    count = sum(block.shape[0] for block in blocks)
    width, full = gate.shape
    number = len(blocks)
    outs = pl.pallas_call(
        functools.partial(backward_kernel, number),
        out_shape=backward_shapes(blocks, width, full),
        in_specs=[SMEM] + [VMEM] * (number + 10),
        out_specs=[VMEM] * (number + 2),
        scratch_shapes=[pltpu.VMEM((count, width), bf16)],
        compiler_params=params(12),
        cost_estimate=cost(6 * count * width * full, 6 * width * full + count * 16000),
        name="expert_back",
    )(me, *blocks, table, router, mod, stats, act, fac, hid, down, gate, up)
    return outs[:number], *outs[number:]


def whole_kernel(number, me_ref, *refs):
    blocks, refs = refs[:number], refs[number:]
    table_ref, router_ref, down_ref, gate_ref, up_ref = refs[:5]
    backs, refs = refs[5 : 5 + number], refs[5 + number :]
    late_ref, lg_ref, stats_ref, act_ref, fac_ref, ups_ref = refs
    mod, og, gg, ug, hid = late_views(late_ref, *gate_ref.shape)
    forward_body(me_ref, blocks, table_ref, router_ref, gate_ref, up_ref, mod, stats_ref, act_ref, fac_ref, hid)
    backward_body(mod.shape[1] + LANES, me_ref, blocks, table_ref, router_ref, stats_ref, act_ref, fac_ref, hid, down_ref, gate_ref, up_ref, backs, og, gg, ug, lg_ref, ups_ref)


def whole(me, blocks, table, router, down, gate, up):
    count = sum(block.shape[0] for block in blocks)
    width, full = gate.shape
    number = len(blocks)
    outs = pl.pallas_call(
        functools.partial(whole_kernel, number),
        out_shape=backward_shapes(blocks, width, full),
        in_specs=[SMEM] + [VMEM] * (number + 5),
        out_specs=[VMEM] * (number + 2),
        scratch_shapes=[pltpu.VMEM((count, LANES), f32)]
        + [pltpu.VMEM((count, full), f32)] * 2
        + [pltpu.VMEM((count, width), bf16)],
        compiler_params=params(16),
        cost_estimate=cost(10 * count * width * full, 6 * width * full + count * 16000),
        name="expert_whole",
    )(me, *blocks, table, router, down, gate, up)
    return outs[:number], *outs[number:]


def sums_kernel(numbers, tall, me_ref, *refs):
    rows, backs = [], []
    for group in (rows, backs):
        for number in numbers:
            group.append(refs[:number])
            refs = refs[number:]
    lates, stats = refs[:2], refs[2:4]
    meta_ref, cot_ref, mix_ref, out_ref = refs[4:]
    count, width = lates[0].shape[0], cot_ref.shape[1]
    conditions, experts = tall
    zero = ((0,), (0,))
    shift_sum = jnp.zeros((conditions, width), f32)
    scale_sum = jnp.zeros((conditions, width), f32)
    router_sum = jnp.zeros((1, width), f32)
    chunk = 128
    for q in range(2):
        for start in range(0, count, chunk):
            part = slice(start, start + chunk)
            lane = lax.broadcasted_iota(jnp.int32, (chunk, conditions), 1)
            mark = stats[q][part, 3:4].astype(jnp.int32)
            pick = (lane + 1 == mark).astype(f32).astype(bf16)
            back = piece(backs[q], start, chunk, slice(0, width))
            mean, inverse = stats[q][part, 0:1], stats[q][part, 1:2]
            values = piece(rows[q], start, chunk, slice(0, width)).astype(f32)
            normed = (values - mean) * inverse
            product = back.astype(f32) * normed
            high = product.astype(bf16)
            low = (product - high.astype(f32)).astype(bf16)
            shift_sum += dot(pick, back, zero)
            scale_sum += dot(pick, high, zero) + dot(pick, low, zero)
            weighted = stats[q][part, 4:5] * lates[q][part, :width].astype(f32)
            router_sum += jnp.sum(weighted, axis=0, keepdims=True)
    toks = cot_ref.shape[0]
    wanted = lax.broadcasted_iota(jnp.int32, (conditions, toks), 0)
    pick = (meta_ref[2:3, :] == wanted).astype(f32).astype(bf16)
    product = cot_ref[...].astype(f32) * mix_ref[...].astype(f32)
    high = product.astype(bf16)
    low = (product - high.astype(f32)).astype(bf16)
    out_ref[0:conditions, :] = shift_sum
    out_ref[conditions : 2 * conditions, :] = scale_sum
    out_ref[2 * conditions : 3 * conditions, :] = dot(pick, high) + dot(pick, low)
    place = lax.broadcasted_iota(jnp.int32, (out_ref.shape[0] - 3 * conditions, width), 0)
    out_ref[3 * conditions :, :] = jnp.where(place == me_ref[0], router_sum, 0.0)


def sums(me, rows, backs, lates, stats, meta, cot, mix, conditions, experts):
    numbers = [len(blocks) for blocks in rows]
    height = -(-(3 * conditions + experts) // 128) * 128
    width = cot.shape[1]
    return pl.pallas_call(
        functools.partial(sums_kernel, numbers, (conditions, experts)),
        out_shape=jax.ShapeDtypeStruct((height, width), f32),
        in_specs=[SMEM] + [VMEM] * (2 * sum(numbers) + 7),
        out_specs=VMEM,
        compiler_params=params(12),
        cost_estimate=cost(1e6, 1e4),
        name="table_sums",
    )(me, *rows[0], *rows[1], *backs[0], *backs[1], *lates, *stats, meta, cot, mix)


def grads_kernel(me_ref, near_ref, far_ref, *outs):
    width, half = outs[0].shape
    other_ref = outs[3]
    zero = ((0,), (0,))
    second = me_ref[2] != 0
    step = 256
    near, far = (late_views(ref, width, 2 * half) for ref in (near_ref, far_ref))
    for start in range(0, width, step):
        part = slice(start, start + step)
        for index, (left, right) in enumerate(((0, 2), (0, 3), (1, 4))):
            total = dot(near[left][:, part], near[right][...], zero)
            total += dot(far[left][:, part], far[right][...], zero)
            low, high = total[:, :half], total[:, half:]
            outs[index][part, :] = jnp.where(second, high, low).astype(bf16)
            other_ref[index, part, :] = jnp.where(second, low, high).astype(bf16)


def grads(me, lates, width, full):
    outs = pl.pallas_call(
        grads_kernel,
        out_shape=[jax.ShapeDtypeStruct((width, full // 2), bf16)] * 3
        + [jax.ShapeDtypeStruct((3, width, full // 2), bf16)],
        in_specs=[SMEM] + [VMEM] * 2,
        out_specs=[VMEM] * 4,
        compiler_params=params(12),
        cost_estimate=cost(1e6, 1e4),
        name="weight_grads",
    )(me, *lates)
    return outs[:3], outs[3]


def merge_kernel(count, cap, me_ref, meta_ref, *refs):
    picks = routing(me_ref[1], me_ref[0] - me_ref[1], meta_ref, count, cap).astype(bf16)
    rows = piece(refs[:-1], 0, count * cap, slice(None))
    refs[-1][...] = dot(picks, rows, ((0,), (0,))).astype(bf16)


def merge(me, meta, backs, cap):
    return pl.pallas_call(
        functools.partial(merge_kernel, len(backs), cap),
        out_shape=jax.ShapeDtypeStruct((meta.shape[1], backs[0].shape[1]), bf16),
        in_specs=[SMEM] + [VMEM] * (1 + len(backs)),
        out_specs=VMEM,
        compiler_params=params(8),
        cost_estimate=cost(1e9, 2e6),
        name="merge",
    )(me, meta, *backs)


def final_kernel(count, cap, me_ref, meta_ref, stamp_ref, tok_ref, cot_ref, table_ref, near_ref, far_ref, out_ref):
    picks = routing(me_ref[1], 0, meta_ref, count, cap).astype(bf16)
    mod_grad = dot(picks, near_ref[...], ((0,), (0,))) + far_ref[...].astype(f32)
    conditions = table_ref.shape[1]
    _, inverse, normed = normalize(tok_ref[...].astype(f32))
    pick = pick3((stamp_ref[:, 0:1] + 1).astype(f32), conditions)
    d_normed = mod_grad * (1.0 + dot(pick, split3(table_ref[1])))
    d_input = inverse * (
        d_normed
        - jnp.mean(d_normed, axis=-1, keepdims=True)
        - normed * jnp.mean(d_normed * normed, axis=-1, keepdims=True)
    )
    out_ref[...] = (cot_ref[...].astype(f32) + d_input).astype(bf16)


def final(me, meta, stamp_column, tokens, cot, table, near, far, count, cap):
    return pl.pallas_call(
        functools.partial(final_kernel, count, cap),
        out_shape=jax.ShapeDtypeStruct(tokens.shape, bf16),
        in_specs=[SMEM] + [VMEM] * 7,
        out_specs=VMEM,
        compiler_params=params(12),
        cost_estimate=cost(1e9, 4e6),
        name="final",
    )(me, meta, stamp_column, tokens, cot, table, near, far)


def rounded(values):
    return lax.reduce_precision(values, 8, 7)


def flip(values, name, size, bit):
    return lax.ppermute(values.astype(bf16), name, [(i, i ^ bit) for i in range(size)])


def scattered_axes(dp_axis, experts):
    return ([("dp", dp_axis, 1)] if dp_axis > 1 else []) + [("expert", experts, 1)]


def scatter_table(table, dp_axis, experts):
    for name, size, bit in scattered_axes(dp_axis, experts):
        high = (lax.axis_index(name) & bit) != 0
        rows = table.shape[0] // 2
        low_half, high_half = table[:rows], table[rows:]
        away = jnp.where(high, low_half, high_half)
        table = jnp.where(high, high_half, low_half)
        table = table + flip(away, name, size, bit).astype(f32)
    bit = 2
    while bit < experts:
        table = rounded(table)
        table = table + flip(table, "expert", experts, bit).astype(f32)
        bit *= 2
    return rounded(table).astype(bf16)


def gather_table(table, dp_axis, experts):
    for name, size, bit in reversed(scattered_axes(dp_axis, experts)):
        high = (lax.axis_index(name) & bit) != 0
        other = flip(table, name, size, bit)
        table = jnp.concatenate(
            [jnp.where(high, other, table), jnp.where(high, table, other)], axis=0
        )
    return table.astype(f32)


def local(experts, dp_axis, tokens, cotangent, mixture, stamp, expert_ids, modulation, router, w_gate, w_up, w_down):
    toks, width = tokens.shape
    conditions = modulation.shape[1]
    cap = min(toks, 4 * toks // experts)
    half = experts // 2
    index = lax.axis_index("expert").astype(jnp.int32)
    me = jnp.stack([index, index // half * half, lax.axis_index("dp").astype(jnp.int32)])
    halves = [list(range(half)), list(range(half, experts))]
    across = [(e, (e + half) % experts) for e in range(experts)]

    def hop(array):
        return lax.ppermute(array, "expert", across)

    def trade(array):
        blocks = array.reshape(half, cap, array.shape[1])
        blocks = lax.all_to_all(
            blocks, "expert", split_axis=0, concat_axis=0, tiled=True, axis_index_groups=halves
        )
        return blocks.reshape(array.shape)

    def fan(blocks):
        return [blocks[0]] + [
            lax.ppermute(blocks[k], "expert", [(e, e ^ k) for e in range(experts)])
            for k in range(1, half)
        ]

    def after(array, *others):
        return lax.optimization_barrier((array,) + others)[0]

    meta = jnp.concatenate(
        [expert_ids.T, stamp[None], jnp.zeros((5, toks), jnp.int32)], axis=0
    )
    gate, up, down = (
        lax.all_gather(w[0], "dp", axis=1, tiled=True) for w in (w_gate, w_up, w_down)
    )
    far_tokens = hop(tokens)
    far_meta = hop(meta)
    (near,) = pack(me, after(meta, far_meta), [tokens, cotangent], True, False, half, cap)
    near = trade(near)
    far_cot = hop(after(cotangent, far_tokens))
    far = fan(pack(me, far_meta, [far_tokens], True, True, half, cap))
    far_cots = fan(pack(me, far_meta, [far_cot], False, True, half, cap))

    near_backs, near_late, near_stats = whole(me, [near], modulation, router, down, gate, up)
    near_late, far = lax.optimization_barrier((near_late, far))
    far_in = forward(me, far, modulation, router, gate, up)
    far_backs, far_late, far_stats = backward(
        me, far_cots, modulation, router, *far_in, down, gate, up
    )
    far_back = fan(far_backs)
    lates = [near_late, far_late]
    table = sums(
        me, [[near], far], [near_backs, far_backs], lates, [near_stats, far_stats],
        meta, cotangent, mixture, conditions, experts,
    )
    mine, other = grads(me, lates, *gate.shape)
    merged = merge(me, far_meta, far_back, cap)
    merged, table, other, near_back = lax.optimization_barrier(
        (merged, table, other, near_backs[0])
    )
    far_grad = hop(merged)
    near_back = trade(near_back)
    other = lax.ppermute(other, "dp", [(i, dp_axis - 1 - i) for i in range(dp_axis)])
    table = scatter_table(table, dp_axis, experts)
    d_gate, d_up, d_down = (
        (mine[i].astype(f32) + other[i].astype(f32)).astype(bf16)[None] for i in range(3)
    )
    table, near_back, far_grad, d_gate, d_up, d_down = lax.optimization_barrier(
        (table, near_back, far_grad, d_gate, d_up, d_down)
    )
    table = gather_table(table, dp_axis, experts)
    d_modulation = table[: 3 * conditions].reshape(3, conditions, width)
    d_router = table[3 * conditions : 3 * conditions + experts]
    d_tokens = final(
        me, meta, stamp[:, None], tokens, cotangent, modulation, near_back, far_grad, half, cap
    )
    return (d_tokens, d_gate, d_up, d_down, d_router, d_modulation)


def solution(mesh):
    return jax.shard_map(
        functools.partial(local, mesh.shape["expert"], mesh.shape["dp"]),
        mesh=mesh,
        in_specs=(
            P(("groups", "expert", "dp"), None),
            P(("groups", "expert", "dp"), None),
            P(("groups", "expert", "dp"), None),
            P(("groups", "expert", "dp")),
            P(("groups", "expert", "dp"), None),
            P(),
            P(),
            P("expert", None, "dp"),
            P("expert", None, "dp"),
            P("expert", None, "dp"),
        ),
        out_specs=(
            P(("groups", "expert", "dp"), None),
            P(("groups", "expert"), None, "dp"),
            P(("groups", "expert"), None, "dp"),
            P(("groups", "expert"), None, "dp"),
            P("groups", None),
            P(None, "groups", None),
        ),
        check_vma=False,
    )
```

time: 193 us -> 165 us (0.85)
  the two profiles are of different devices: /device:TPU:11 before, /device:TPU:1 now
where the time goes in v2:
time: 165 us
  waiting for transfers between devices  66 us (40%)
  starting transfers between devices  38.6 us (23%)
  Pallas kernels  34.3 us (21%)
  between operations  14.2 us (9%)
  other arithmetic  6.64 us (4%)
  local copies, waits for them, and re-layouts  5.28 us (3%)
    ppermute x4, waiting for transfers between devices, hop(): return lax.ppermute(array, 'expert', across)  42.2 us
    ppermute x6, waiting for transfers between devices, flip(): lax.ppermute(values.astype(bf16), name, [(i, i ^ bit) for i in range(size)])  21.6 us
    ppermute x4, starting transfers between devices, hop(): return lax.ppermute(array, 'expert', across)  10.9 us
    ppermute x6, starting transfers between devices, flip(): lax.ppermute(values.astype(bf16), name, [(i, i ^ bit) for i in range(size)])  8.73 us
    ppermute x9, starting transfers between devices, fan(): lax.ppermute(blocks[k], 'expert', [(e, e ^ k) for e in range(experts)])  8 us
    all_to_all x2, starting transfers between devices, trade(): lax.all_to_all(blocks, 'expert', split_axis=0, concat_axis=0, tiled=True,...  7.8 us
    pallas_call x3, Pallas kernels, pack(): pl.pallas_call(functools.partial(pack_kernel, count, cap, len(arrays), fl...  6.49 us
    pallas_call x1, Pallas kernels, grads(): pl.pallas_call(grads_kernel, out_shape=[jax.ShapeDtypeStruct((width, full...  6.39 us
  transfers between devices with their start and end apart: 25, of which 9 were waited for; matrix products, arithmetic and copies ran while one was open for 3% of the time, Pallas kernels for 18%

profile of v2, /device:TPU:1, one launch (start us, length us, event | category | flops | bytes accessed | tf_op | source)
XLA Modules:
  0.0 165.0 jit_solution(16175982610859671437)
XLA Ops:
  7.2 0.7 all-gather.11.cloned.1.call-update
  8.0 0.7 all-gather.9.cloned.1.call-update
  8.8 3.1 %collective-permute-start = (s32[8,128]{1,0:T(8,128)S(1)}, s32[8,128]{1,0:T(8,128)S(1)}, u32[]{:S(2)}, u32[]{:S(2)}) collective-permute-start(s32[8,128]{1,0:T(8,128)S(1)} %add_add_fusion.meta_ref.refs_14_), channel_id=1, source_target_pairs={{0,8},{2,10},{4,12},{6,14},{8,0},{10,2},{12,4},{14,6},{1,9},{3,11}... | collective-permute-start | bytes 12296 | tf_op jit(solution)/shard_map/ppermute | solution.py:471
  12.0 0.1 pad_add_fusion.me_ref
  12.1 0.9 collective-permute-done.meta_ref
  13.0 3.0 %pack.4 = bf16[256,3200]{1,0:T(8,128)(2,1)} custom-call(s32[3]{0:T(128)S(1)} %pad_add_fusion.me_ref, s32[8,128]{1,0:T(8,128)S(1)} %add_add_fusion.meta_ref.refs_14_, bf16[128,1536]{1,0:T(8,128)(2,1)S(1)} %copy-done.18, bf16[128,1536]{1,0:T(8,128)(2,1)} %cot_ref.1), custom_call_target="tpu_custom_call" | custom-call | flops 1000000000 | bytes 4000000 | tf_op jit(solution)/shard_map/pack/pallas_call | solution.py:115
  15.9 3.6 %all-to-all-start = ((bf16[4,64,3200]{2,1,0:T(8,128)(2,1)}), bf16[4,64,3200]{2,1,0:T(8,128)(2,1)S(1)}, u32[]{:S(2)}, u32[]{:S(2)}) async-start(bf16[4,64,3200]{2,1,0:T(8,128)(2,1)} %bitcast.6), calls=%async_computation | async-start | bytes 3276800 | tf_op jit(solution)/shard_map/all_to_all | solution.py:475
  19.6 0.7 all-gather.7.cloned.1.call-update
  20.3 2.4 %collective-permute-start.1 = (bf16[128,1536]{1,0:T(8,128)(2,1)S(1)}, bf16[128,1536]{1,0:T(8,128)(2,1)S(1)}, u32[]{:S(2)}, u32[]{:S(2)}) collective-permute-start(bf16[128,1536]{1,0:T(8,128)(2,1)S(1)} %copy-done.18), channel_id=1, source_target_pairs={{0,8},{2,10},{4,12},{6,14},{8,0},{10,2},{12,4},{14,6},{1,9},{3,11}... | collective-permute-start | bytes 1179656 | tf_op jit(solution)/shard_map/ppermute | solution.py:471
  22.7 21.3 %collective-permute-done.1.refs_0_ = bf16[128,1536]{1,0:T(8,128)(2,1)S(1)} collective-permute-done((bf16[128,1536]{1,0:T(8,128)(2,1)S(1)}, bf16[128,1536]{1,0:T(8,128)(2,1)S(1)}, u32[]{:S(2)}, u32[]{:S(2)}) %collective-permute-start.1) | collective-permute-done | bytes 393248 | tf_op jit(solution)/shard_map/ppermute | solution.py:471
  44.0 3.1 %collective-permute-start.2 = (bf16[128,1536]{1,0:T(8,128)(2,1)}, bf16[128,1536]{1,0:T(8,128)(2,1)S(1)}, u32[]{:S(2)}, u32[]{:S(2)}) collective-permute-start(bf16[128,1536]{1,0:T(8,128)(2,1)} %cot_ref.1), channel_id=1, source_target_pairs={{0,8},{2,10},{4,12},{6,14},{8,0},{10,2},{12,4},{14,6},{1,9},{3,11}... | collective-permute-start | bytes 1179656 | tf_op jit(solution)/shard_map/ppermute | solution.py:471
  47.1 1.8 %pack.5 = (bf16[64,1664]{1,0:T(8,128)(2,1)S(1)}, bf16[64,1664]{1,0:T(8,128)(2,1)S(1)}, bf16[64,1664]{1,0:T(8,128)(2,1)}, bf16[64,1664]{1,0:T(8,128)(2,1)}) custom-call(s32[3]{0:T(128)S(1)} %pad_add_fusion.me_ref, s32[8,128]{1,0:T(8,128)S(1)} %collective-permute-done.meta_ref, bf16[128,1536]{1,0:T(8,128)(2,1)S(1)} %collective-permute-done.1.refs_0_), custom_call_target="tpu_custom_call" | custom-call | flops 1000000000 | bytes 4000000 | tf_op jit(solution)/shard_map/pack/pallas_call | solution.py:115
  48.9 1.1 collective-permute-start.6
  50.0 1.2 collective-permute-start.7
  51.2 0.3 collective-permute-start.8
  51.5 15.0 %collective-permute-done.2.refs_0_ = bf16[128,1536]{1,0:T(8,128)(2,1)S(1)} collective-permute-done((bf16[128,1536]{1,0:T(8,128)(2,1)}, bf16[128,1536]{1,0:T(8,128)(2,1)S(1)}, u32[]{:S(2)}, u32[]{:S(2)}) %collective-permute-start.2) | collective-permute-done | bytes 393248 | tf_op jit(solution)/shard_map/ppermute | solution.py:471
  66.5 1.8 %pack.3 = (bf16[64,1536]{1,0:T(8,128)(2,1)S(1)}, bf16[64,1536]{1,0:T(8,128)(2,1)}, bf16[64,1536]{1,0:T(8,128)(2,1)}, bf16[64,1536]{1,0:T(8,128)(2,1)}) custom-call(s32[3]{0:T(128)S(1)} %pad_add_fusion.me_ref, s32[8,128]{1,0:T(8,128)S(1)} %collective-permute-done.meta_ref, bf16[128,1536]{1,0:T(8,128)(2,1)S(1)} %collective-permute-done.2.refs_0_), custom_call_target="tpu_custom_call" | custom-call | flops 1000000000 | bytes 4000000 | tf_op jit(solution)/shard_map/pack/pallas_call | solution.py:115
  68.3 0.9 collective-permute-start.3
  69.2 1.7 %collective-permute-start.5 = (bf16[64,1536]{1,0:T(8,128)(2,1)}, bf16[64,1536]{1,0:T(8,128)(2,1)}, u32[]{:S(2)}, u32[]{:S(2)}) collective-permute-start(bf16[64,1536]{1,0:T(8,128)(2,1)} %get-tuple-element.53), channel_id=1, source_target_pairs={{0,6},{2,4},{4,2},{6,0},{8,14},{10,12},{12,10},{14,8},{1,7},{3,5},... | collective-permute-start | bytes 589832 | tf_op jit(solution)/shard_map/ppermute | solution.py:482
  71.0 1.7 %copy-done = bf16[1,1536,768]{2,1,0:T(8,128)(2,1)S(1)} copy-done((bf16[1,1536,768]{2,1,0:T(8,128)(2,1)S(1)}, bf16[1,1536,768]{2,1,0:T(8,128)(2,1)}, u32[]{:S(2)}) %copy-start) | copy-done | bytes 2359320
  72.6 1.7 %copy-done.2 = bf16[1,1536,768]{2,1,0:T(8,128)(2,1)S(1)} copy-done((bf16[1,1536,768]{2,1,0:T(8,128)(2,1)S(1)}, bf16[1,1536,768]{2,1,0:T(8,128)(2,1)}, u32[]{:S(2)}) %copy-start.2) | copy-done | bytes 2359320
  74.3 1.7 %copy-done.5 = bf16[1,1536,768]{2,1,0:T(8,128)(2,1)S(1)} copy-done((bf16[1,1536,768]{2,1,0:T(8,128)(2,1)S(1)}, bf16[1,1536,768]{2,1,0:T(8,128)(2,1)}, u32[]{:S(2)}) %copy-start.5) | copy-done | bytes 2359320
  76.0 6.3 %expert_whole.1 = (bf16[256,1536]{1,0:T(8,128)(2,1)}, bf16[256,5376]{1,0:T(8,128)(2,1)S(1)}, f32[256,128]{1,0:T(8,128)S(1)}) custom-call(s32[3]{0:T(128)S(1)} %pad_add_fusion.me_ref, bf16[256,3200]{1,0:T(8,128)(2,1)S(1)} %bitcast.41, f32[3,32,1536]{2,1,0:T(8,128)S(1)} %copy-done.4, bf16[8,1536]{1,0:T(8,128)(2,1)S(1)} %copy-done.17, ...), custom_call_target="tpu_custom_call" | custom-call | flops 3019898880 | bytes 11173888 | tf_op jit(solution)/shard_map/expert_whole/pallas_call | solution.py:271
  82.3 2.9 %expert_in.1 = (bf16[256,1536]{1,0:T(8,128)(2,1)S(1)}, f32[256,128]{1,0:T(8,128)S(1)}, f32[256,768]{1,0:T(8,128)S(1)}, f32[256,768]{1,0:T(8,128)S(1)}, bf16[256,768]{1,0:T(8,128)(2,1)S(1)}) custom-call(s32[3]{0:T(128)S(1)} %pad_add_fusion.me_ref, bf16[64,1664]{1,0:T(8,128)(2,1)S(1)} %get-tuple-element.60.refs_0_.refs_1_, ...), custom_call_target="tpu_custom_call" | custom-call | flops 1207959552 | bytes 7790592 | tf_op jit(solution)/shard_map/expert_in/pallas_call | solution.py:205
  85.3 3.5 %expert_back.1 = (bf16[64,1536]{1,0:T(8,128)(2,1)S(1)}, bf16[64,1536]{1,0:T(8,128)(2,1)S(1)}, bf16[64,1536]{1,0:T(8,128)(2,1)S(1)}, bf16[64,1536]{1,0:T(8,128)(2...) custom-call(s32[3]{0:T(128)S(1)} %pad_add_fusion.me_ref, bf16[64,1536]{1,0:T(8,128)(2,1)S(1)} %get-tuple-element.50.refs_0_, ...), custom_call_target="tpu_custom_call" | custom-call | flops 1811939328 | bytes 11173888 | tf_op jit(solution)/shard_map/expert_back/pallas_call | solution.py:244
  89.0 2.1 %collective-permute-start.11 = (bf16[64,1536]{1,0:T(8,128)(2,1)S(1)}, bf16[64,1536]{1,0:T(8,128)(2,1)S(1)}, u32[]{:S(2)}, u32[]{:S(2)}) collective-permute-start(bf16[64,1536]{1,0:T(8,128)(2,1)S(1)} %get-tuple-element.72.refs_9_), channel_id=1, source_target_pairs={{0,6},{2,4},{4,2},{6,0},{8,14},{10,12},{12,10},{14,8},{1,7},{3,5},... | collective-permute-start | bytes 589832 | tf_op jit(solution)/shard_map/ppermute | solution.py:482
  91.1 0.5 collective-permute-start.9
  91.6 6.4 %weight_grads.1 = (bf16[1536,384]{1,0:T(8,128)(2,1)S(1)}, bf16[1536,384]{1,0:T(8,128)(2,1)S(1)}, bf16[1536,384]{1,0:T(8,128)(2,1)S(1)}, bf16[3,1536,384]{2,1,0:T(8,128)(2,1)}) custom-call(s32[3]{0:T(128)S(1)} %pad_add_fusion.me_ref, bf16[256,5376]{1,0:T(8,128)(2,1)S(1)} %get-tuple-element.74.refs_10_.near_ref, ...), custom_call_target="tpu_custom_call" | custom-call | flops 1000000 | bytes 10000 | tf_op jit(solution)/shard_map/weight_grads/pallas_call | solution.py:364
  98.0 3.9 %table_sums.1 = f32[128,1536]{1,0:T(8,128)S(1)} custom-call(s32[3]{0:T(128)S(1)} %pad_add_fusion.me_ref, bf16[256,3200]{1,0:T(8,128)(2,1)S(1)} %bitcast.42, bf16[64,1664]{1,0:T(8,128)(2,1)S(1)} %get-tuple-element.60.refs_0_.refs_1_, bf16[64,1664]{1,0:T(8,128)(2,1)S(1)} %collective-permute-done.6.refs_1_.refs_2_, bf16[64,1664]{1,0:T(8,128)(2,1)S(1)} %copy-done.13, ...), custom_call_target="tpu_custom_call" | custom-call | flops 1000000 | bytes 10000 | tf_op jit(solution)/shard_map/table_sums/pallas_call | solution.py:335
  102.0 1.7 %merge.1 = bf16[128,1536]{1,0:T(8,128)(2,1)} custom-call(s32[3]{0:T(128)S(1)} %pad_add_fusion.me_ref, s32[8,128]{1,0:T(8,128)S(1)} %collective-permute-done.meta_ref, bf16[64,1536]{1,0:T(8,128)(2,1)S(1)} %get-tuple-element.69.refs_0_.refs_6_, bf16[64,1536]{1,0:T(8,128)(2,1)S(1)} %collective-permute-done.9.refs_1_, ...), custom_call_target="tpu_custom_call" | custom-call | flops 1000000000 | bytes 2000000 | tf_op jit(solution)/shard_map/merge/pallas_call | solution.py:384
  103.7 3.1 %collective-permute-start.17 = (bf16[3,1536,384]{2,1,0:T(8,128)(2,1)}, bf16[3,1536,384]{2,1,0:T(8,128)(2,1)}, u32[]{:S(2)}, u32[]{:S(2)}) collective-permute-start(bf16[3,1536,384]{2,1,0:T(8,128)(2,1)} %get-tuple-element.83), channel_id=1, source_target_pairs={{0,1},{1,0},{2,3},{3,2},{4,5},{5,4},{6,7},{7,6},{8,9},{9,8},{10,11... | collective-permute-start | bytes 10616840 | tf_op jit(solution)/shard_map/ppermute | solution.py:522
  106.9 5.9 %collective-permute-done.12 = bf16[64,1536]{1,0:T(8,128)(2,1)S(1)} collective-permute-done((bf16[64,1536]{1,0:T(8,128)(2,1)S(1)}, bf16[64,1536]{1,0:T(8,128)(2,1)S(1)}, u32[]{:S(2)}, u32[]{:S(2)}) %collective-permute-start.12) | collective-permute-done | bytes 196640 | tf_op jit(solution)/shard_map/ppermute | solution.py:427
  112.9 1.3 collective-permute-start.13
  114.2 3.1 %collective-permute-done.13 = bf16[32,1536]{1,0:T(8,128)(2,1)S(1)} collective-permute-done((bf16[32,1536]{1,0:T(8,128)(2,1)S(1)}, bf16[32,1536]{1,0:T(8,128)(2,1)S(1)}, u32[]{:S(2)}, u32[]{:S(2)}) %collective-permute-start.13) | collective-permute-done | bytes 98336 | tf_op jit(solution)/shard_map/ppermute | solution.py:427
  117.4 3.5 %collective-permute-done.14 = bf16[32,1536]{1,0:T(8,128)(2,1)S(1)} collective-permute-done((bf16[32,1536]{1,0:T(8,128)(2,1)S(1)}, bf16[32,1536]{1,0:T(8,128)(2,1)S(1)}, u32[]{:S(2)}, u32[]{:S(2)}) %collective-permute-start.14) | collective-permute-done | bytes 98336 | tf_op jit(solution)/shard_map/ppermute | solution.py:427
  120.9 0.2 collective-permute-start.15
  121.0 2.3 %collective-permute-start.16 = (bf16[128,1536]{1,0:T(8,128)(2,1)}, bf16[128,1536]{1,0:T(8,128)(2,1)}, u32[]{:S(2)}, u32[]{:S(2)}) collective-permute-start(bf16[128,1536]{1,0:T(8,128)(2,1)} %merge.1), channel_id=1, source_target_pairs={{0,8},{2,10},{4,12},{6,14},{8,0},{10,2},{12,4},{14,6},{1,9},{3,11}... | collective-permute-start | bytes 1179656 | tf_op jit(solution)/shard_map/ppermute | solution.py:471
  123.3 4.2 %all-to-all-start.1 = ((bf16[4,64,1536]{2,1,0:T(8,128)(2,1)}), bf16[4,64,1536]{2,1,0:T(8,128)(2,1)}, u32[]{:S(2)}, u32[]{:S(2)}) async-start(bf16[4,64,1536]{2,1,0:T(8,128)(2,1)} %bitcast.11), calls=%async_computation.1 | async-start | bytes 1572864 | tf_op jit(solution)/shard_map/all_to_all | solution.py:475
  127.5 7.3 %collective-permute-done.15 = bf16[32,1536]{1,0:T(8,128)(2,1)S(1)} collective-permute-done((bf16[32,1536]{1,0:T(8,128)(2,1)S(1)}, bf16[32,1536]{1,0:T(8,128)(2,1)S(1)}, u32[]{:S(2)}, u32[]{:S(2)}) %collective-permute-start.15) | collective-permute-done | bytes 98336 | tf_op jit(solution)/shard_map/ppermute | solution.py:427
  134.8 4.7 %fusion.5 = (bf16[1,1536,384]{2,1,0:T(8,128)(2,1)}, bf16[1,1536,384]{2,1,0:T(8,128)(2,1)}, bf16[1,1536,384]{2,1,0:T(8,128)(2,1)}) fusion(bf16[1536,384]{1,0:T(8,128)(2,1)} %copy-done.11, bf16[3,1536,384]{2,1,0:T(8,128)(2,1)} %collective-permute-done.17, bf16[1536,384]{1,0:T(8,128)(2,1)S(1)} %copy-done.10, bf16[1536,384]{1,0:T(8,128)(2,1)S(1)} %copy-done.8), kind=kLoop, calls=%fused_computation.8 | loop fusion | flops 7077888 | bytes 10616832 | tf_op jit(solution)/shard_map/broadcast_in_dim | solution.py:525
  139.5 5.1 %collective-permute-done.16.far_ref = bf16[128,1536]{1,0:T(8,128)(2,1)} collective-permute-done((bf16[128,1536]{1,0:T(8,128)(2,1)}, bf16[128,1536]{1,0:T(8,128)(2,1)}, u32[]{:S(2)}, u32[]{:S(2)}) %collective-permute-start.16) | collective-permute-done | bytes 393248 | tf_op jit(solution)/shard_map/ppermute | solution.py:471
  144.6 2.2 %collective-permute-start.18 = (bf16[32,1536]{1,0:T(8,128)(2,1)S(1)}, bf16[32,1536]{1,0:T(8,128)(2,1)S(1)}, u32[]{:S(2)}, u32[]{:S(2)}) collective-permute-start(bf16[32,1536]{1,0:T(8,128)(2,1)S(1)} %reduce-precision_convert_fusion), channel_id=1, source_target_pairs={{0,2},{2,0},{4,6},{6,4},{8,10},{10,8},{12,14},{14,12},{1,3},{3,1},... | collective-permute-start | bytes 294920 | tf_op jit(solution)/shard_map/ppermute | solution.py:427
  146.7 2.0 %collective-permute-done.18 = bf16[32,1536]{1,0:T(8,128)(2,1)S(1)} collective-permute-done((bf16[32,1536]{1,0:T(8,128)(2,1)S(1)}, bf16[32,1536]{1,0:T(8,128)(2,1)S(1)}, u32[]{:S(2)}, u32[]{:S(2)}) %collective-permute-start.18) | collective-permute-done | bytes 98336 | tf_op jit(solution)/shard_map/ppermute | solution.py:427
  148.8 5.0 %collective-permute-start.19 = (bf16[64,1536]{1,0:T(8,128)(2,1)S(1)}, bf16[64,1536]{1,0:T(8,128)(2,1)S(1)}, u32[]{:S(2)}, u32[]{:S(2)}) collective-permute-start(bf16[64,1536]{1,0:T(8,128)(2,1)S(1)} %pad_maximum_fusion.1), channel_id=1, source_target_pairs={{0,1},{1,0},{2,3},{3,2},{4,5},{5,4},{6,7},{7,6},{8,9},{9,8},{10,11... | collective-permute-start | bytes 589832 | tf_op jit(solution)/shard_map/ppermute | solution.py:427
  153.8 0.1 copy.16.stamp_ref
  153.9 3.0 %final.1 = bf16[128,1536]{1,0:T(8,128)(2,1)} custom-call(s32[3]{0:T(128)S(1)} %pad_add_fusion.me_ref, s32[8,128]{1,0:T(8,128)S(1)} %add_add_fusion.meta_ref.refs_14_, s32[128,1]{1,0:T(8,128)S(1)} %copy.16.stamp_ref, bf16[128,1536]{1,0:T(8,128)(2,1)S(1)} %copy-done.19, bf16[128,1536]{1,0:T(8,128)(2,1)} %cot_ref.1, f32[3,32,1536]{2,1,0:T(8,128)S(1)} %copy-done.4, ...), custom_call_target="tpu_custom_call" | custom-call | flops 1000000000 | bytes 4000000 | tf_op jit(solution)/shard_map/final/pallas_call | solution.py:411
  157.0 0.9 fusion.6
  157.8 0.6 maximum_convert_fusion
  (80 shorter events, 0.9 us)
Async XLA Ops:
  7.2 1.6 copy-start.23
  7.2 5.8 %copy-start.18 = (bf16[128,1536]{1,0:T(8,128)(2,1)S(1)}, bf16[128,1536]{1,0:T(8,128)(2,1)}, u32[]{:S(2)}) copy-start(bf16[128,1536]{1,0:T(8,128)(2,1)} %tok_ref.1) | copy-start | bytes 1179652
  7.2 63.7 %all-gather.11.cloned.1.call-start = ((), (), s32[]{:S(2)}) async-start(), calls=%async_computation.4 | async-start | bytes 3538944 | tf_op jit(solution)/shard_map/all_gather | solution.py:493
  7.9 63.0 %all-gather.9.cloned.1.call-start = ((), (), s32[]{:S(2)}) async-start(), calls=%async_computation.3 | async-start | bytes 3538944 | tf_op jit(solution)/shard_map/all_gather | solution.py:493
  8.8 4.1 %collective-permute-start = (s32[8,128]{1,0:T(8,128)S(1)}, s32[8,128]{1,0:T(8,128)S(1)}, u32[]{:S(2)}, u32[]{:S(2)}) collective-permute-start(s32[8,128]{1,0:T(8,128)S(1)} %add_add_fusion.meta_ref.refs_14_), channel_id=1, source_target_pairs={{0,8},{2,10},{4,12},{6,14},{8,0},{10,2},{12,4},{14,6},{1,9},{3,11}... | collective-permute-start | bytes 12296 | tf_op jit(solution)/shard_map/ppermute | solution.py:471
  15.9 55.0 %all-to-all-start = ((bf16[4,64,3200]{2,1,0:T(8,128)(2,1)}), bf16[4,64,3200]{2,1,0:T(8,128)(2,1)S(1)}, u32[]{:S(2)}, u32[]{:S(2)}) async-start(bf16[4,64,3200]{2,1,0:T(8,128)(2,1)} %bitcast.6), calls=%async_computation | async-start | bytes 3276800 | tf_op jit(solution)/shard_map/all_to_all | solution.py:475
  19.6 51.4 %all-gather.7.cloned.1.call-start = ((), (), s32[]{:S(2)}) async-start(), calls=%async_computation.2 | async-start | bytes 3538944 | tf_op jit(solution)/shard_map/all_gather | solution.py:493
  20.3 23.7 %collective-permute-start.1 = (bf16[128,1536]{1,0:T(8,128)(2,1)S(1)}, bf16[128,1536]{1,0:T(8,128)(2,1)S(1)}, u32[]{:S(2)}, u32[]{:S(2)}) collective-permute-start(bf16[128,1536]{1,0:T(8,128)(2,1)S(1)} %copy-done.18), channel_id=1, source_target_pairs={{0,8},{2,10},{4,12},{6,14},{8,0},{10,2},{12,4},{14,6},{1,9},{3,11}... | collective-permute-start | bytes 1179656 | tf_op jit(solution)/shard_map/ppermute | solution.py:471
  44.0 22.5 %collective-permute-start.2 = (bf16[128,1536]{1,0:T(8,128)(2,1)}, bf16[128,1536]{1,0:T(8,128)(2,1)S(1)}, u32[]{:S(2)}, u32[]{:S(2)}) collective-permute-start(bf16[128,1536]{1,0:T(8,128)(2,1)} %cot_ref.1), channel_id=1, source_target_pairs={{0,8},{2,10},{4,12},{6,14},{8,0},{10,2},{12,4},{14,6},{1,9},{3,11}... | collective-permute-start | bytes 1179656 | tf_op jit(solution)/shard_map/ppermute | solution.py:471
  48.9 20.4 %collective-permute-start.6 = (bf16[64,1664]{1,0:T(8,128)(2,1)S(1)}, bf16[64,1664]{1,0:T(8,128)(2,1)S(1)}, u32[]{:S(2)}, u32[]{:S(2)}) collective-permute-start(bf16[64,1664]{1,0:T(8,128)(2,1)S(1)} %get-tuple-element.57), channel_id=1, source_target_pairs={{0,2},{2,0},{4,6},{6,4},{8,10},{10,8},{12,14},{14,12},{1,3},{3,1},... | collective-permute-start | bytes 638984 | tf_op jit(solution)/shard_map/ppermute | solution.py:482
  50.0 32.3 %collective-permute-start.7 = (bf16[64,1664]{1,0:T(8,128)(2,1)}, bf16[64,1664]{1,0:T(8,128)(2,1)S(1)}, u32[]{:S(2)}, u32[]{:S(2)}) collective-permute-start(bf16[64,1664]{1,0:T(8,128)(2,1)} %get-tuple-element.58), channel_id=1, source_target_pairs={{0,4},{2,6},{4,0},{6,2},{8,12},{10,14},{12,8},{14,10},{1,5},{3,7},... | collective-permute-start | bytes 638984 | tf_op jit(solution)/shard_map/ppermute | solution.py:482
  51.2 19.7 %copy-start.4 = (f32[3,32,1536]{2,1,0:T(8,128)S(1)}, f32[3,32,1536]{2,1,0:T(8,128)}, u32[]{:S(2)}) copy-start(f32[3,32,1536]{2,1,0:T(8,128)} %table_ref.1) | copy-start | bytes 1769476
  51.2 19.7 %copy-start.17 = (bf16[8,1536]{1,0:T(8,128)(2,1)S(1)}, bf16[8,1536]{1,0:T(8,128)(2,1)}, u32[]{:S(2)}) copy-start(bf16[8,1536]{1,0:T(8,128)(2,1)} %refs_5_.3) | copy-start | bytes 73732
  51.2 31.0 %collective-permute-start.8 = (bf16[64,1664]{1,0:T(8,128)(2,1)}, bf16[64,1664]{1,0:T(8,128)(2,1)S(1)}, u32[]{:S(2)}, u32[]{:S(2)}) collective-permute-start(bf16[64,1664]{1,0:T(8,128)(2,1)} %get-tuple-element.59), channel_id=1, source_target_pairs={{0,6},{2,4},{4,2},{6,0},{8,14},{10,12},{12,10},{14,8},{1,7},{3,5},... | collective-permute-start | bytes 638984 | tf_op jit(solution)/shard_map/ppermute | solution.py:482
  68.3 17.0 %collective-permute-start.3 = (bf16[64,1536]{1,0:T(8,128)(2,1)}, bf16[64,1536]{1,0:T(8,128)(2,1)}, u32[]{:S(2)}, u32[]{:S(2)}) collective-permute-start(bf16[64,1536]{1,0:T(8,128)(2,1)} %get-tuple-element.51), channel_id=1, source_target_pairs={{0,2},{2,0},{4,6},{6,4},{8,10},{10,8},{12,14},{14,12},{1,3},{3,1},... | collective-permute-start | bytes 589832 | tf_op jit(solution)/shard_map/ppermute | solution.py:482
  69.2 16.1 %collective-permute-start.4 = (bf16[64,1536]{1,0:T(8,128)(2,1)}, bf16[64,1536]{1,0:T(8,128)(2,1)}, u32[]{:S(2)}, u32[]{:S(2)}) collective-permute-start(bf16[64,1536]{1,0:T(8,128)(2,1)} %get-tuple-element.52), channel_id=1, source_target_pairs={{0,4},{2,6},{4,0},{6,2},{8,12},{10,14},{12,8},{14,10},{1,5},{3,7},... | collective-permute-start | bytes 589832 | tf_op jit(solution)/shard_map/ppermute | solution.py:482
  69.2 16.1 %collective-permute-start.5 = (bf16[64,1536]{1,0:T(8,128)(2,1)}, bf16[64,1536]{1,0:T(8,128)(2,1)}, u32[]{:S(2)}, u32[]{:S(2)}) collective-permute-start(bf16[64,1536]{1,0:T(8,128)(2,1)} %get-tuple-element.53), channel_id=1, source_target_pairs={{0,6},{2,4},{4,2},{6,0},{8,14},{10,12},{12,10},{14,8},{1,7},{3,5},... | collective-permute-start | bytes 589832 | tf_op jit(solution)/shard_map/ppermute | solution.py:482
  71.0 1.7 %copy-start = (bf16[1,1536,768]{2,1,0:T(8,128)(2,1)S(1)}, bf16[1,1536,768]{2,1,0:T(8,128)(2,1)}, u32[]{:S(2)}) copy-start(bf16[1,1536,768]{2,1,0:T(8,128)(2,1)} %all-gather.11.cloned.1.call-done) | copy-start | bytes 7077892
  72.6 1.7 %copy-start.2 = (bf16[1,1536,768]{2,1,0:T(8,128)(2,1)S(1)}, bf16[1,1536,768]{2,1,0:T(8,128)(2,1)}, u32[]{:S(2)}) copy-start(bf16[1,1536,768]{2,1,0:T(8,128)(2,1)} %all-gather.9.cloned.1.call-done) | copy-start | bytes 7077892
  74.3 1.7 %copy-start.5 = (bf16[1,1536,768]{2,1,0:T(8,128)(2,1)S(1)}, bf16[1,1536,768]{2,1,0:T(8,128)(2,1)}, u32[]{:S(2)}) copy-start(bf16[1,1536,768]{2,1,0:T(8,128)(2,1)} %all-gather.7.cloned.1.call-done) | copy-start | bytes 7077892
  76.0 6.3 %copy-start.3 = (bf16[1,1536,768]{2,1,0:T(8,128)(2,1)S(1)}, bf16[1,1536,768]{2,1,0:T(8,128)(2,1)}, u32[]{:S(2)}) copy-start(bf16[1,1536,768]{2,1,0:T(8,128)(2,1)} %all-gather.9.cloned.1.call-done) | copy-start | bytes 7077892
  82.3 3.0 %copy-start.12 = (bf16[64,1664]{1,0:T(8,128)(2,1)}, bf16[64,1664]{1,0:T(8,128)(2,1)S(1)}, u32[]{:S(2)}) copy-start(bf16[64,1664]{1,0:T(8,128)(2,1)S(1)} %collective-permute-done.7.refs_2_.refs_3_) | copy-start | bytes 638980
  82.3 3.0 %copy-start.14 = (bf16[64,1664]{1,0:T(8,128)(2,1)}, bf16[64,1664]{1,0:T(8,128)(2,1)S(1)}, u32[]{:S(2)}) copy-start(bf16[64,1664]{1,0:T(8,128)(2,1)S(1)} %collective-permute-done.8.refs_3_.refs_4_) | copy-start | bytes 638980
  82.3 3.0 %copy-start.1 = (bf16[1,1536,768]{2,1,0:T(8,128)(2,1)S(1)}, bf16[1,1536,768]{2,1,0:T(8,128)(2,1)}, u32[]{:S(2)}) copy-start(bf16[1,1536,768]{2,1,0:T(8,128)(2,1)} %all-gather.11.cloned.1.call-done) | copy-start | bytes 7077892
  82.3 3.0 %copy-start.6 = (bf16[1,1536,768]{2,1,0:T(8,128)(2,1)S(1)}, bf16[1,1536,768]{2,1,0:T(8,128)(2,1)}, u32[]{:S(2)}) copy-start(bf16[1,1536,768]{2,1,0:T(8,128)(2,1)} %all-gather.7.cloned.1.call-done) | copy-start | bytes 7077892
  88.9 13.1 %collective-permute-start.10 = (bf16[64,1536]{1,0:T(8,128)(2,1)S(1)}, bf16[64,1536]{1,0:T(8,128)(2,1)S(1)}, u32[]{:S(2)}, u32[]{:S(2)}) collective-permute-start(bf16[64,1536]{1,0:T(8,128)(2,1)S(1)} %get-tuple-element.71.refs_8_), channel_id=1, source_target_pairs={{0,4},{2,6},{4,0},{6,2},{8,12},{10,14},{12,8},{14,10},{1,5},{3,7},... | collective-permute-start | bytes 589832 | tf_op jit(solution)/shard_map/ppermute | solution.py:482
  89.0 13.0 %collective-permute-start.11 = (bf16[64,1536]{1,0:T(8,128)(2,1)S(1)}, bf16[64,1536]{1,0:T(8,128)(2,1)S(1)}, u32[]{:S(2)}, u32[]{:S(2)}) collective-permute-start(bf16[64,1536]{1,0:T(8,128)(2,1)S(1)} %get-tuple-element.72.refs_9_), channel_id=1, source_target_pairs={{0,6},{2,4},{4,2},{6,0},{8,14},{10,12},{12,10},{14,8},{1,7},{3,5},... | collective-permute-start | bytes 589832 | tf_op jit(solution)/shard_map/ppermute | solution.py:482
  91.1 10.9 %collective-permute-start.9 = (bf16[64,1536]{1,0:T(8,128)(2,1)S(1)}, bf16[64,1536]{1,0:T(8,128)(2,1)S(1)}, u32[]{:S(2)}, u32[]{:S(2)}) collective-permute-start(bf16[64,1536]{1,0:T(8,128)(2,1)S(1)} %get-tuple-element.70.refs_7_), channel_id=1, source_target_pairs={{0,2},{2,0},{4,6},{6,4},{8,10},{10,8},{12,14},{14,12},{1,3},{3,1},... | collective-permute-start | bytes 589832 | tf_op jit(solution)/shard_map/ppermute | solution.py:482
  91.6 6.4 %copy-start.13 = (bf16[64,1664]{1,0:T(8,128)(2,1)S(1)}, bf16[64,1664]{1,0:T(8,128)(2,1)}, u32[]{:S(2)}) copy-start(bf16[64,1664]{1,0:T(8,128)(2,1)} %copy-done.12) | copy-start | bytes 638980
  91.6 6.4 %copy-start.15 = (bf16[64,1664]{1,0:T(8,128)(2,1)S(1)}, bf16[64,1664]{1,0:T(8,128)(2,1)}, u32[]{:S(2)}) copy-start(bf16[64,1664]{1,0:T(8,128)(2,1)} %copy-done.14) | copy-start | bytes 638980
  91.6 6.4 %copy-start.16 = (bf16[128,1536]{1,0:T(8,128)(2,1)S(1)}, bf16[128,1536]{1,0:T(8,128)(2,1)}, u32[]{:S(2)}) copy-start(bf16[128,1536]{1,0:T(8,128)(2,1)} %refs_16_.1) | copy-start | bytes 1179652
  98.0 4.0 %copy-start.7 = (bf16[1536,384]{1,0:T(8,128)(2,1)}, bf16[1536,384]{1,0:T(8,128)(2,1)S(1)}, u32[]{:S(2)}) copy-start(bf16[1536,384]{1,0:T(8,128)(2,1)S(1)} %get-tuple-element.82) | copy-start | bytes 3538948
  98.0 4.0 %copy-start.9 = (bf16[1536,384]{1,0:T(8,128)(2,1)}, bf16[1536,384]{1,0:T(8,128)(2,1)S(1)}, u32[]{:S(2)}) copy-start(bf16[1536,384]{1,0:T(8,128)(2,1)S(1)} %get-tuple-element.84) | copy-start | bytes 3538948
  98.0 4.0 %copy-start.11 = (bf16[1536,384]{1,0:T(8,128)(2,1)}, bf16[1536,384]{1,0:T(8,128)(2,1)S(1)}, u32[]{:S(2)}) copy-start(bf16[1536,384]{1,0:T(8,128)(2,1)S(1)} %get-tuple-element.85) | copy-start | bytes 3538948
  103.7 31.1 %collective-permute-start.17 = (bf16[3,1536,384]{2,1,0:T(8,128)(2,1)}, bf16[3,1536,384]{2,1,0:T(8,128)(2,1)}, u32[]{:S(2)}, u32[]{:S(2)}) collective-permute-start(bf16[3,1536,384]{2,1,0:T(8,128)(2,1)} %get-tuple-element.83), channel_id=1, source_target_pairs={{0,1},{1,0},{2,3},{3,2},{4,5},{5,4},{6,7},{7,6},{8,9},{9,8},{10,11... | collective-permute-start | bytes 10616840 | tf_op jit(solution)/shard_map/ppermute | solution.py:522
  106.8 6.0 %collective-permute-start.12 = (bf16[64,1536]{1,0:T(8,128)(2,1)S(1)}, bf16[64,1536]{1,0:T(8,128)(2,1)S(1)}, u32[]{:S(2)}, u32[]{:S(2)}) collective-permute-start(bf16[64,1536]{1,0:T(8,128)(2,1)S(1)} %select_convert_fusion), channel_id=1, source_target_pairs={{0,1},{1,0},{2,3},{3,2},{4,5},{5,4},{6,7},{7,6},{8,9},{9,8},{10,11... | collective-permute-start | bytes 589832 | tf_op jit(solution)/shard_map/ppermute | solution.py:427
  112.9 21.9 %copy-start.8 = (bf16[1536,384]{1,0:T(8,128)(2,1)S(1)}, bf16[1536,384]{1,0:T(8,128)(2,1)}, u32[]{:S(2)}) copy-start(bf16[1536,384]{1,0:T(8,128)(2,1)} %copy-done.7) | copy-start | bytes 3538948
  112.9 21.9 %copy-start.10 = (bf16[1536,384]{1,0:T(8,128)(2,1)S(1)}, bf16[1536,384]{1,0:T(8,128)(2,1)}, u32[]{:S(2)}) copy-start(bf16[1536,384]{1,0:T(8,128)(2,1)} %copy-done.9) | copy-start | bytes 3538948
  112.9 4.3 %collective-permute-start.13 = (bf16[32,1536]{1,0:T(8,128)(2,1)S(1)}, bf16[32,1536]{1,0:T(8,128)(2,1)S(1)}, u32[]{:S(2)}, u32[]{:S(2)}) collective-permute-start(bf16[32,1536]{1,0:T(8,128)(2,1)S(1)} %select_convert_fusion.1), channel_id=1, source_target_pairs={{0,2},{2,0},{4,6},{6,4},{8,10},{10,8},{12,14},{14,12},{1,3},{3,1},... | collective-permute-start | bytes 294920 | tf_op jit(solution)/shard_map/ppermute | solution.py:427
  117.3 3.5 %copy-start.20 = (f32[32,1536]{1,0:T(8,128)}, f32[32,1536]{1,0:T(8,128)S(1)}, u32[]{:S(2)}) copy-start(f32[32,1536]{1,0:T(8,128)S(1)} %get-tuple-element.93) | copy-start | bytes 589828
  117.3 3.5 %collective-permute-start.14 = (bf16[32,1536]{1,0:T(8,128)(2,1)S(1)}, bf16[32,1536]{1,0:T(8,128)(2,1)S(1)}, u32[]{:S(2)}, u32[]{:S(2)}) collective-permute-start(bf16[32,1536]{1,0:T(8,128)(2,1)S(1)} %get-tuple-element.92), channel_id=1, source_target_pairs={{0,4},{2,6},{4,0},{6,2},{8,12},{10,14},{12,8},{14,10},{1,5},{3,7},... | collective-permute-start | bytes 294920 | tf_op jit(solution)/shard_map/ppermute | solution.py:427
  120.8 13.9 %copy-start.21 = (f32[32,1536]{1,0:T(8,128)S(1)}, f32[32,1536]{1,0:T(8,128)}, u32[]{:S(2)}) copy-start(f32[32,1536]{1,0:T(8,128)} %copy-done.20) | copy-start | bytes 589828
  120.9 13.9 %collective-permute-start.15 = (bf16[32,1536]{1,0:T(8,128)(2,1)S(1)}, bf16[32,1536]{1,0:T(8,128)(2,1)S(1)}, u32[]{:S(2)}, u32[]{:S(2)}) collective-permute-start(bf16[32,1536]{1,0:T(8,128)(2,1)S(1)} %fusion.7), channel_id=1, source_target_pairs={{0,8},{2,10},{4,12},{6,14},{8,0},{10,2},{12,4},{14,6},{1,9},{3,11}... | collective-permute-start | bytes 294920 | tf_op jit(solution)/shard_map/ppermute | solution.py:427
  121.0 23.5 %collective-permute-start.16 = (bf16[128,1536]{1,0:T(8,128)(2,1)}, bf16[128,1536]{1,0:T(8,128)(2,1)}, u32[]{:S(2)}, u32[]{:S(2)}) collective-permute-start(bf16[128,1536]{1,0:T(8,128)(2,1)} %merge.1), channel_id=1, source_target_pairs={{0,8},{2,10},{4,12},{6,14},{8,0},{10,2},{12,4},{14,6},{1,9},{3,11}... | collective-permute-start | bytes 1179656 | tf_op jit(solution)/shard_map/ppermute | solution.py:471
  123.3 21.3 %all-to-all-start.1 = ((bf16[4,64,1536]{2,1,0:T(8,128)(2,1)}), bf16[4,64,1536]{2,1,0:T(8,128)(2,1)}, u32[]{:S(2)}, u32[]{:S(2)}) async-start(bf16[4,64,1536]{2,1,0:T(8,128)(2,1)} %bitcast.11), calls=%async_computation.1 | async-start | bytes 1572864 | tf_op jit(solution)/shard_map/all_to_all | solution.py:475
  134.8 19.1 %copy-start.19 = (bf16[128,1536]{1,0:T(8,128)(2,1)S(1)}, bf16[128,1536]{1,0:T(8,128)(2,1)}, u32[]{:S(2)}) copy-start(bf16[128,1536]{1,0:T(8,128)(2,1)} %tok_ref.1) | copy-start | bytes 1179652
  144.6 4.2 %collective-permute-start.18 = (bf16[32,1536]{1,0:T(8,128)(2,1)S(1)}, bf16[32,1536]{1,0:T(8,128)(2,1)S(1)}, u32[]{:S(2)}, u32[]{:S(2)}) collective-permute-start(bf16[32,1536]{1,0:T(8,128)(2,1)S(1)} %reduce-precision_convert_fusion), channel_id=1, source_target_pairs={{0,2},{2,0},{4,6},{6,4},{8,10},{10,8},{12,14},{14,12},{1,3},{3,1},... | collective-permute-start | bytes 294920 | tf_op jit(solution)/shard_map/ppermute | solution.py:427
  148.8 8.1 %collective-permute-start.19 = (bf16[64,1536]{1,0:T(8,128)(2,1)S(1)}, bf16[64,1536]{1,0:T(8,128)(2,1)S(1)}, u32[]{:S(2)}, u32[]{:S(2)}) collective-permute-start(bf16[64,1536]{1,0:T(8,128)(2,1)S(1)} %pad_maximum_fusion.1), channel_id=1, source_target_pairs={{0,1},{1,0},{2,3},{3,2},{4,5},{5,4},{6,7},{7,6},{8,9},{9,8},{10,11... | collective-permute-start | bytes 589832 | tf_op jit(solution)/shard_map/ppermute | solution.py:427
  (1 other events, 1.6 us)
Sparse Core Ops, SparseCore 0:
  9.6 13.3 all-gather.10
  24.5 12.0 all-gather.8
  38.2 12.0 all-gather.6

commit v3 on v2

--- a/solution.py
+++ b/solution.py
@@ -439,12 +439,39 @@
         away = jnp.where(high, low_half, high_half)
         table = jnp.where(high, high_half, low_half)
         table = table + flip(away, name, size, bit).astype(f32)
-    bit = 2
-    while bit < experts:
+    return table
+
+
+def exchange_table(table, experts, first, last):
+    bit = first
+    while bit < last:
         table = rounded(table)
         table = table + flip(table, "expert", experts, bit).astype(f32)
         bit *= 2
-    return rounded(table).astype(bf16)
+    return table
+
+
+def add_kernel(other_ref, *refs):
+    number = len(refs) // 2
+    for i in range(number):
+        total = refs[i][...].astype(f32) + other_ref[i].astype(f32)
+        refs[number + i][0] = total.astype(bf16)
+
+
+def add(mine, other):
+    width, half = mine[0].shape
+    step = 256
+    part = pl.BlockSpec((step, half), lambda i: (i, 0))
+    return pl.pallas_call(
+        add_kernel,
+        grid=(width // step,),
+        out_shape=[jax.ShapeDtypeStruct((1, width, half), bf16)] * len(mine),
+        in_specs=[pl.BlockSpec((len(mine), step, half), lambda i: (0, i, 0))] + [part] * len(mine),
+        out_specs=[pl.BlockSpec((1, step, half), lambda i: (0, i, 0))] * len(mine),
+        compiler_params=params(12),
+        cost_estimate=cost(1e6, 1e4),
+        name="add",
+    )(other, *mine)
 
 
 def gather_table(table, dp_axis, experts):
@@ -454,7 +481,7 @@
         table = jnp.concatenate(
             [jnp.where(high, other, table), jnp.where(high, table, other)], axis=0
         )
-    return table.astype(f32)
+    return table
 
 
 def local(experts, dp_axis, tokens, cotangent, mixture, stamp, expert_ids, modulation, router, w_gate, w_up, w_down):
@@ -494,7 +521,8 @@
     )
     far_tokens = hop(tokens)
     far_meta = hop(meta)
-    (near,) = pack(me, after(meta, far_meta), [tokens, cotangent], True, False, half, cap)
+    (near,) = pack(me, meta, [tokens, cotangent], True, False, half, cap)
+    far_tokens, near, far_meta = lax.optimization_barrier((far_tokens, near, far_meta))
     near = trade(near)
     far_cot = hop(after(cotangent, far_tokens))
     far = fan(pack(me, far_meta, [far_tokens], True, True, half, cap))
@@ -521,18 +549,20 @@
     near_back = trade(near_back)
     other = lax.ppermute(other, "dp", [(i, dp_axis - 1 - i) for i in range(dp_axis)])
     table = scatter_table(table, dp_axis, experts)
-    d_gate, d_up, d_down = (
-        (mine[i].astype(f32) + other[i].astype(f32)).astype(bf16)[None] for i in range(3)
-    )
+    table = exchange_table(table, experts, 2, 2)
+    d_gate, d_up, d_down = add(mine, other)
     table, near_back, far_grad, d_gate, d_up, d_down = lax.optimization_barrier(
         (table, near_back, far_grad, d_gate, d_up, d_down)
     )
+    table = rounded(exchange_table(table, experts, 2, experts)).astype(bf16)
     table = gather_table(table, dp_axis, experts)
+    d_tokens = final(
+        me, meta, stamp[:, None], tokens, cotangent, modulation, near_back, far_grad, half, cap
+    )
+    table, d_tokens = lax.optimization_barrier((table, d_tokens))
+    table = table.astype(f32)
     d_modulation = table[: 3 * conditions].reshape(3, conditions, width)
     d_router = table[3 * conditions : 3 * conditions + experts]
-    d_tokens = final(
-        me, meta, stamp[:, None], tokens, cotangent, modulation, near_back, far_grad, half, cap
-    )
     return (d_tokens, d_gate, d_up, d_down, d_router, d_modulation)
 
 

time: 165 us -> 160 us (0.970)
  other arithmetic: 6.64 us -> 0.5 us
  waiting for transfers between devices: 66 us -> 60.1 us
  Pallas kernels: 34.3 us -> 40.1 us
    pallas_call x0 -> x1, Pallas kernels: none -> 5.47 us  [add(): pl.pallas_call(add_kernel, grid=(width // step,), out_shape=[jax.ShapeDty...]
    ppermute x4, waiting for transfers between devices: 42.2 us -> 37.5 us  [hop(): return lax.ppermute(array, 'expert', across)]
    broadcast_in_dim x1 -> x0, other arithmetic: 4.69 us -> none  [local(): (mine[i].astype(f32) + other[i].astype(f32)).astype(bf16)[None]]
    ppermute x4, starting transfers between devices: 10.9 us -> 6.62 us  [hop(): return lax.ppermute(array, 'expert', across)]
    ppermute x9, starting transfers between devices: 8 us -> 11.8 us  [fan(): lax.ppermute(blocks[k], 'expert', [(e, e ^ k) for e in range(experts)])]
    ppermute x6, starting transfers between devices: 8.73 us -> 6.86 us  [flip(): lax.ppermute(values.astype(bf16), name, [(i, i ^ bit) for i in range(size)])]
    unnamed x48 -> x46, local copies, waits for them, and re-layouts: 5.09 us -> 5.08 us
  transfers between devices with their start and end apart: 25 -> 25, of which waited for: 9 -> 8; matrix products, arithmetic and copies ran while one was open for 3% -> 0% of each run, Pallas kernels for 18% -> 22%
where the time goes in v3:
time: 160 us; the launch traced here: 159 us
  waiting for transfers between devices  60.1 us (38%)
  Pallas kernels  40.1 us (25%)
  starting transfers between devices  37.6 us (24%)
  between operations  14.2 us (9%)
  local copies, waits for them, and re-layouts  6.76 us (4%)
    ppermute x4, waiting for transfers between devices, hop(): return lax.ppermute(array, 'expert', across)  37.5 us
    ppermute x6, waiting for transfers between devices, flip(): lax.ppermute(values.astype(bf16), name, [(i, i ^ bit) for i in range(size)])  20.5 us
    ppermute x9, starting transfers between devices, fan(): lax.ppermute(blocks[k], 'expert', [(e, e ^ k) for e in range(experts)])  11.8 us
    all_to_all x2, starting transfers between devices, trade(): lax.all_to_all(blocks, 'expert', split_axis=0, concat_axis=0, tiled=True,...  7.97 us
    ppermute x6, starting transfers between devices, flip(): lax.ppermute(values.astype(bf16), name, [(i, i ^ bit) for i in range(size)])  6.86 us
    ppermute x4, starting transfers between devices, hop(): return lax.ppermute(array, 'expert', across)  6.62 us
    pallas_call x3, Pallas kernels, pack(): pl.pallas_call(functools.partial(pack_kernel, count, cap, len(arrays), fl...  6.5 us
    pallas_call x1, Pallas kernels, grads(): pl.pallas_call(grads_kernel, out_shape=[jax.ShapeDtypeStruct((width, full...  6.49 us
  transfers between devices with their start and end apart: 25, of which 8 were waited for; matrix products, arithmetic and copies ran while one was open for 0% of the time, Pallas kernels for 22%

profile of v3, /device:TPU:1, one launch (start us, length us, event | category | flops | bytes accessed | tf_op | source)
XLA Modules:
  0.0 159.3 jit_solution(639686831730661018)
XLA Ops:
  7.2 0.7 all-gather.9.cloned.1.call-update
  8.0 0.7 all-gather.11.cloned.1.call-update
  8.7 3.2 %collective-permute-start = (bf16[128,1536]{1,0:T(8,128)(2,1)S(1)}, bf16[128,1536]{1,0:T(8,128)(2,1)S(1)}, u32[]{:S(2)}, u32[]{:S(2)}) collective-permute-start(bf16[128,1536]{1,0:T(8,128)(2,1)S(1)} %copy-done.19), channel_id=1, source_target_pairs={{0,8},{2,10},{4,12},{6,14},{8,0},{10,2},{12,4},{14,6},{1,9},{3,11}... | collective-permute-start | bytes 1179656 | tf_op jit(solution)/shard_map/ppermute | solution.py:498
  11.9 0.1 pad.6.clone
  12.1 0.1 pad_add_fusion.me_ref
  12.2 3.0 %pack.3 = bf16[256,3200]{1,0:T(8,128)(2,1)} custom-call(s32[3]{0:T(128)S(1)} %pad_add_fusion.me_ref, s32[8,128]{1,0:T(8,128)S(1)} %add_add_fusion.meta_ref.refs_14_, bf16[128,1536]{1,0:T(8,128)(2,1)S(1)} %copy-done.19, bf16[128,1536]{1,0:T(8,128)(2,1)} %cot_ref.1), custom_call_target="tpu_custom_call" | custom-call | flops 1000000000 | bytes 4000000 | tf_op jit(solution)/shard_map/pack/pallas_call | solution.py:115
  15.1 14.2 %collective-permute-done.1.meta_ref = s32[8,128]{1,0:T(8,128)S(1)} collective-permute-done((s32[8,128]{1,0:T(8,128)S(1)}, s32[8,128]{1,0:T(8,128)S(1)}, u32[]{:S(2)}, u32[]{:S(2)}) %collective-permute-start.1) | collective-permute-done | bytes 4128 | tf_op jit(solution)/shard_map/ppermute | solution.py:498
  29.3 3.6 %all-to-all-start = ((bf16[4,64,3200]{2,1,0:T(8,128)(2,1)}), bf16[4,64,3200]{2,1,0:T(8,128)(2,1)S(1)}, u32[]{:S(2)}, u32[]{:S(2)}) async-start(bf16[4,64,3200]{2,1,0:T(8,128)(2,1)} %bitcast.5), calls=%async_computation | async-start | bytes 3276800 | tf_op jit(solution)/shard_map/all_to_all | solution.py:502
  33.0 0.7 all-gather.7.cloned.1.call-update
  33.7 2.9 %collective-permute-start.2 = (bf16[128,1536]{1,0:T(8,128)(2,1)}, bf16[128,1536]{1,0:T(8,128)(2,1)S(1)}, u32[]{:S(2)}, u32[]{:S(2)}) collective-permute-start(bf16[128,1536]{1,0:T(8,128)(2,1)} %cot_ref.1), channel_id=1, source_target_pairs={{0,8},{2,10},{4,12},{6,14},{8,0},{10,2},{12,4},{14,6},{1,9},{3,11}... | collective-permute-start | bytes 1179656 | tf_op jit(solution)/shard_map/ppermute | solution.py:498
  36.6 1.8 %pack.5 = (bf16[64,1664]{1,0:T(8,128)(2,1)S(1)}, bf16[64,1664]{1,0:T(8,128)(2,1)S(1)}, bf16[64,1664]{1,0:T(8,128)(2,1)}, bf16[64,1664]{1,0:T(8,128)(2,1)}) custom-call(s32[3]{0:T(128)S(1)} %pad_add_fusion.me_ref, s32[8,128]{1,0:T(8,128)S(1)} %collective-permute-done.1.meta_ref, bf16[128,1536]{1,0:T(8,128)(2,1)S(1)} %collective-permute-done.refs_0_), custom_call_target="tpu_custom_call" | custom-call | flops 1000000000 | bytes 4000000 | tf_op jit(solution)/shard_map/pack/pallas_call | solution.py:115
  38.4 1.5 collective-permute-start.6
  39.8 1.2 collective-permute-start.7
  41.0 17.3 %collective-permute-done.2.refs_0_ = bf16[128,1536]{1,0:T(8,128)(2,1)S(1)} collective-permute-done((bf16[128,1536]{1,0:T(8,128)(2,1)}, bf16[128,1536]{1,0:T(8,128)(2,1)S(1)}, u32[]{:S(2)}, u32[]{:S(2)}) %collective-permute-start.2) | collective-permute-done | bytes 393248 | tf_op jit(solution)/shard_map/ppermute | solution.py:498
  58.3 1.8 %pack.4 = (bf16[64,1536]{1,0:T(8,128)(2,1)S(1)}, bf16[64,1536]{1,0:T(8,128)(2,1)}, bf16[64,1536]{1,0:T(8,128)(2,1)}, bf16[64,1536]{1,0:T(8,128)(2,1)}) custom-call(s32[3]{0:T(128)S(1)} %pad_add_fusion.me_ref, s32[8,128]{1,0:T(8,128)S(1)} %collective-permute-done.1.meta_ref, bf16[128,1536]{1,0:T(8,128)(2,1)S(1)} %collective-permute-done.2.refs_0_), custom_call_target="tpu_custom_call" | custom-call | flops 1000000000 | bytes 4000000 | tf_op jit(solution)/shard_map/pack/pallas_call | solution.py:115
  60.1 1.2 collective-permute-start.3
  61.3 5.3 %collective-permute-start.4 = (bf16[64,1536]{1,0:T(8,128)(2,1)}, bf16[64,1536]{1,0:T(8,128)(2,1)}, u32[]{:S(2)}, u32[]{:S(2)}) collective-permute-start(bf16[64,1536]{1,0:T(8,128)(2,1)} %get-tuple-element.61), channel_id=1, source_target_pairs={{0,4},{2,6},{4,0},{6,2},{8,12},{10,14},{12,8},{14,10},{1,5},{3,7},... | collective-permute-start | bytes 589832 | tf_op jit(solution)/shard_map/ppermute | solution.py:509
  66.6 1.7 %copy-done = bf16[1,1536,768]{2,1,0:T(8,128)(2,1)S(1)} copy-done((bf16[1,1536,768]{2,1,0:T(8,128)(2,1)S(1)}, bf16[1,1536,768]{2,1,0:T(8,128)(2,1)}, u32[]{:S(2)}) %copy-start) | copy-done | bytes 2359320
  68.3 1.7 %copy-done.2 = bf16[1,1536,768]{2,1,0:T(8,128)(2,1)S(1)} copy-done((bf16[1,1536,768]{2,1,0:T(8,128)(2,1)S(1)}, bf16[1,1536,768]{2,1,0:T(8,128)(2,1)}, u32[]{:S(2)}) %copy-start.2) | copy-done | bytes 2359320
  70.0 1.7 %copy-done.5 = bf16[1,1536,768]{2,1,0:T(8,128)(2,1)S(1)} copy-done((bf16[1,1536,768]{2,1,0:T(8,128)(2,1)S(1)}, bf16[1,1536,768]{2,1,0:T(8,128)(2,1)}, u32[]{:S(2)}) %copy-start.5) | copy-done | bytes 2359320
  71.6 6.4 %expert_whole.1 = (bf16[256,1536]{1,0:T(8,128)(2,1)}, bf16[256,5376]{1,0:T(8,128)(2,1)S(1)}, f32[256,128]{1,0:T(8,128)S(1)}) custom-call(s32[3]{0:T(128)S(1)} %pad_add_fusion.me_ref, bf16[256,3200]{1,0:T(8,128)(2,1)S(1)} %bitcast.20, f32[3,32,1536]{2,1,0:T(8,128)S(1)} %copy-done.4, bf16[8,1536]{1,0:T(8,128)(2,1)S(1)} %copy-done.18, ...), custom_call_target="tpu_custom_call" | custom-call | flops 3019898880 | bytes 11173888 | tf_op jit(solution)/shard_map/expert_whole/pallas_call | solution.py:271
  78.1 3.0 %expert_in.1 = (bf16[256,1536]{1,0:T(8,128)(2,1)S(1)}, f32[256,128]{1,0:T(8,128)S(1)}, f32[256,768]{1,0:T(8,128)S(1)}, f32[256,768]{1,0:T(8,128)S(1)}, bf16[256,768]{1,0:T(8,128)(2,1)S(1)}) custom-call(s32[3]{0:T(128)S(1)} %pad_add_fusion.me_ref, bf16[64,1664]{1,0:T(8,128)(2,1)S(1)} %get-tuple-element.69.refs_0_.refs_1_, ...), custom_call_target="tpu_custom_call" | custom-call | flops 1207959552 | bytes 7790592 | tf_op jit(solution)/shard_map/expert_in/pallas_call | solution.py:205
  81.2 3.6 %expert_back.1 = (bf16[64,1536]{1,0:T(8,128)(2,1)S(1)}, bf16[64,1536]{1,0:T(8,128)(2,1)S(1)}, bf16[64,1536]{1,0:T(8,128)(2,1)S(1)}, bf16[64,1536]{1,0:T(8,128)(2...) custom-call(s32[3]{0:T(128)S(1)} %pad_add_fusion.me_ref, bf16[64,1536]{1,0:T(8,128)(2,1)S(1)} %get-tuple-element.59.refs_0_, ...), custom_call_target="tpu_custom_call" | custom-call | flops 1811939328 | bytes 11173888 | tf_op jit(solution)/shard_map/expert_back/pallas_call | solution.py:244
  84.8 1.5 collective-permute-start.10
  86.3 1.0 collective-permute-start.11
  87.3 0.3 collective-permute-start.9
  87.5 6.5 %weight_grads.1 = (bf16[1536,384]{1,0:T(8,128)(2,1)S(1)}, bf16[1536,384]{1,0:T(8,128)(2,1)S(1)}, bf16[1536,384]{1,0:T(8,128)(2,1)S(1)}, bf16[3,1536,384]{2,1,0:T(8,128)(2,1)}) custom-call(s32[3]{0:T(128)S(1)} %pad_add_fusion.me_ref, bf16[256,5376]{1,0:T(8,128)(2,1)S(1)} %get-tuple-element.83.refs_10_.near_ref, ...), custom_call_target="tpu_custom_call" | custom-call | flops 1000000 | bytes 10000 | tf_op jit(solution)/shard_map/weight_grads/pallas_call | solution.py:364
  94.1 4.0 %table_sums.1 = f32[128,1536]{1,0:T(8,128)S(1)} custom-call(s32[3]{0:T(128)S(1)} %pad_add_fusion.me_ref, bf16[256,3200]{1,0:T(8,128)(2,1)S(1)} %bitcast.21, bf16[64,1664]{1,0:T(8,128)(2,1)S(1)} %get-tuple-element.69.refs_0_.refs_1_, bf16[64,1664]{1,0:T(8,128)(2,1)S(1)} %collective-permute-done.6.refs_1_.refs_2_, bf16[64,1664]{1,0:T(8,128)(2,1)S(1)} %copy-done.14, ...), custom_call_target="tpu_custom_call" | custom-call | flops 1000000 | bytes 10000 | tf_op jit(solution)/shard_map/table_sums/pallas_call | solution.py:335
  98.1 1.7 %merge.1 = bf16[128,1536]{1,0:T(8,128)(2,1)} custom-call(s32[3]{0:T(128)S(1)} %pad_add_fusion.me_ref, s32[8,128]{1,0:T(8,128)S(1)} %collective-permute-done.1.meta_ref, bf16[64,1536]{1,0:T(8,128)(2,1)S(1)} %get-tuple-element.78.refs_0_.refs_6_, bf16[64,1536]{1,0:T(8,128)(2,1)S(1)} %collective-permute-done.9.refs_1_, ...), custom_call_target="tpu_custom_call" | custom-call | flops 1000000000 | bytes 2000000 | tf_op jit(solution)/shard_map/merge/pallas_call | solution.py:384
  99.9 4.2 %collective-permute-start.15 = (bf16[3,1536,384]{2,1,0:T(8,128)(2,1)}, bf16[3,1536,384]{2,1,0:T(8,128)(2,1)}, u32[]{:S(2)}, u32[]{:S(2)}) collective-permute-start(bf16[3,1536,384]{2,1,0:T(8,128)(2,1)} %get-tuple-element.91), channel_id=1, source_target_pairs={{0,1},{1,0},{2,3},{3,2},{4,5},{5,4},{6,7},{7,6},{8,9},{9,8},{10,11... | collective-permute-start | bytes 10616840 | tf_op jit(solution)/shard_map/ppermute | solution.py:550
  104.1 0.1 collective-permute-start.12
  104.2 4.4 %all-to-all-start.1 = ((bf16[4,64,1536]{2,1,0:T(8,128)(2,1)}), bf16[4,64,1536]{2,1,0:T(8,128)(2,1)}, u32[]{:S(2)}, u32[]{:S(2)}) async-start(bf16[4,64,1536]{2,1,0:T(8,128)(2,1)} %bitcast.10), calls=%async_computation.1 | async-start | bytes 1572864 | tf_op jit(solution)/shard_map/all_to_all | solution.py:502
  108.6 1.5 collective-permute-done.12
  110.2 1.2 collective-permute-start.13
  111.4 0.5 collective-permute-start.14
  111.9 7.9 %collective-permute-done.13 = bf16[32,1536]{1,0:T(8,128)(2,1)S(1)} collective-permute-done((bf16[32,1536]{1,0:T(8,128)(2,1)S(1)}, bf16[32,1536]{1,0:T(8,128)(2,1)S(1)}, u32[]{:S(2)}, u32[]{:S(2)}) %collective-permute-start.13) | collective-permute-done | bytes 98336 | tf_op jit(solution)/shard_map/ppermute | solution.py:427
  119.8 5.5 %add.34 = (bf16[1,1536,384]{2,1,0:T(8,128)(2,1)}, bf16[1,1536,384]{2,1,0:T(8,128)(2,1)}, bf16[1,1536,384]{2,1,0:T(8,128)(2,1)}) custom-call(bf16[3,1536,384]{2,1,0:T(8,128)(2,1)} %collective-permute-done.15.other_ref, bf16[1536,384]{1,0:T(8,128)(2,1)S(1)} %copy-done.8, bf16[1536,384]{1,0:T(8,128)(2,1)S(1)} %copy-done.10, bf16[1536,384]{1,0:T(8,128)(2,1)S(1)} %copy-done.12), custom_call_target="tpu_custom_call" | custom-call | flops 1000000 | bytes 10000 | tf_op jit(solution)/shard_map/add/pallas_call | solution.py:465
  125.3 6.0 %collective-permute-done.14.far_ref = bf16[128,1536]{1,0:T(8,128)(2,1)S(1)} collective-permute-done((bf16[128,1536]{1,0:T(8,128)(2,1)}, bf16[128,1536]{1,0:T(8,128)(2,1)S(1)}, u32[]{:S(2)}, u32[]{:S(2)}) %collective-permute-start.14) | collective-permute-done | bytes 393248 | tf_op jit(solution)/shard_map/ppermute | solution.py:498
  131.4 3.5 %collective-permute-done.16 = bf16[32,1536]{1,0:T(8,128)(2,1)S(1)} collective-permute-done((bf16[32,1536]{1,0:T(8,128)(2,1)S(1)}, bf16[32,1536]{1,0:T(8,128)(2,1)S(1)}, u32[]{:S(2)}, u32[]{:S(2)}) %collective-permute-start.16) | collective-permute-done | bytes 98336 | tf_op jit(solution)/shard_map/ppermute | solution.py:427
  134.8 0.6 collective-permute-start.17
  135.5 4.6 %collective-permute-done.17 = bf16[32,1536]{1,0:T(8,128)(2,1)S(1)} collective-permute-done((bf16[32,1536]{1,0:T(8,128)(2,1)S(1)}, bf16[32,1536]{1,0:T(8,128)(2,1)S(1)}, u32[]{:S(2)}, u32[]{:S(2)}) %collective-permute-start.17) | collective-permute-done | bytes 98336 | tf_op jit(solution)/shard_map/ppermute | solution.py:427
  140.1 0.4 collective-permute-start.18
  140.5 3.2 %collective-permute-done.18 = bf16[32,1536]{1,0:T(8,128)(2,1)S(1)} collective-permute-done((bf16[32,1536]{1,0:T(8,128)(2,1)S(1)}, bf16[32,1536]{1,0:T(8,128)(2,1)S(1)}, u32[]{:S(2)}, u32[]{:S(2)}) %collective-permute-start.18) | collective-permute-done | bytes 98336 | tf_op jit(solution)/shard_map/ppermute | solution.py:427
  143.7 4.5 %collective-permute-start.19 = (bf16[64,1536]{1,0:T(8,128)(2,1)S(1)}, bf16[64,1536]{1,0:T(8,128)(2,1)S(1)}, u32[]{:S(2)}, u32[]{:S(2)}) collective-permute-start(bf16[64,1536]{1,0:T(8,128)(2,1)S(1)} %pad_maximum_fusion.1), channel_id=1, source_target_pairs={{0,1},{1,0},{2,3},{3,2},{4,5},{5,4},{6,7},{7,6},{8,9},{9,8},{10,11... | collective-permute-start | bytes 589832 | tf_op jit(solution)/shard_map/ppermute | solution.py:427
  148.2 0.1 copy.16.stamp_ref
  148.3 2.9 %final.1 = bf16[128,1536]{1,0:T(8,128)(2,1)} custom-call(s32[3]{0:T(128)S(1)} %pad_add_fusion.me_ref, s32[8,128]{1,0:T(8,128)S(1)} %add_add_fusion.meta_ref.refs_14_, s32[128,1]{1,0:T(8,128)S(1)} %copy.16.stamp_ref, bf16[128,1536]{1,0:T(8,128)(2,1)S(1)} %copy-done.20, bf16[128,1536]{1,0:T(8,128)(2,1)} %cot_ref.1, f32[3,32,1536]{2,1,0:T(8,128)S(1)} %copy-done.4, ...), custom_call_target="tpu_custom_call" | custom-call | flops 1000000000 | bytes 4000000 | tf_op jit(solution)/shard_map/final/pallas_call | solution.py:411
  151.3 0.9 slice.27
  152.2 0.6 slice.26
  (80 shorter events, 0.8 us)
Async XLA Ops:
  7.2 1.5 copy-start.19
  7.2 4.8 %copy-start.22 = (s32[128,2]{0,1:T(2,128)S(1)}, s32[128,2]{0,1:T(2,128)}, u32[]{:S(2)}) copy-start(s32[128,2]{0,1:T(2,128)} %param.14) | copy-start | bytes 3076
  7.2 4.8 %copy-start.21 = (s32[128]{0:T(128)S(1)}, s32[128]{0:T(128)}, u32[]{:S(2)}) copy-start(s32[128]{0:T(128)} %param.13) | copy-start | bytes 1540
  7.2 59.3 %all-gather.9.cloned.1.call-start = ((), (), s32[]{:S(2)}) async-start(), calls=%async_computation.3 | async-start | bytes 3538944 | tf_op jit(solution)/shard_map/all_gather | solution.py:520
  7.9 58.6 %all-gather.11.cloned.1.call-start = ((), (), s32[]{:S(2)}) async-start(), calls=%async_computation.4 | async-start | bytes 3538944 | tf_op jit(solution)/shard_map/all_gather | solution.py:520
  8.7 20.7 %collective-permute-start = (bf16[128,1536]{1,0:T(8,128)(2,1)S(1)}, bf16[128,1536]{1,0:T(8,128)(2,1)S(1)}, u32[]{:S(2)}, u32[]{:S(2)}) collective-permute-start(bf16[128,1536]{1,0:T(8,128)(2,1)S(1)} %copy-done.19), channel_id=1, source_target_pairs={{0,8},{2,10},{4,12},{6,14},{8,0},{10,2},{12,4},{14,6},{1,9},{3,11}... | collective-permute-start | bytes 1179656 | tf_op jit(solution)/shard_map/ppermute | solution.py:498
  12.1 17.3 %collective-permute-start.1 = (s32[8,128]{1,0:T(8,128)S(1)}, s32[8,128]{1,0:T(8,128)S(1)}, u32[]{:S(2)}, u32[]{:S(2)}) collective-permute-start(s32[8,128]{1,0:T(8,128)S(1)} %add_add_fusion.meta_ref.refs_14_), channel_id=1, source_target_pairs={{0,8},{2,10},{4,12},{6,14},{8,0},{10,2},{12,4},{14,6},{1,9},{3,11}... | collective-permute-start | bytes 12296 | tf_op jit(solution)/shard_map/ppermute | solution.py:498
  29.3 37.3 %all-to-all-start = ((bf16[4,64,3200]{2,1,0:T(8,128)(2,1)}), bf16[4,64,3200]{2,1,0:T(8,128)(2,1)S(1)}, u32[]{:S(2)}, u32[]{:S(2)}) async-start(bf16[4,64,3200]{2,1,0:T(8,128)(2,1)} %bitcast.5), calls=%async_computation | async-start | bytes 3276800 | tf_op jit(solution)/shard_map/all_to_all | solution.py:502
  33.0 33.6 %all-gather.7.cloned.1.call-start = ((), (), s32[]{:S(2)}) async-start(), calls=%async_computation.2 | async-start | bytes 3538944 | tf_op jit(solution)/shard_map/all_gather | solution.py:520
  33.7 24.6 %collective-permute-start.2 = (bf16[128,1536]{1,0:T(8,128)(2,1)}, bf16[128,1536]{1,0:T(8,128)(2,1)S(1)}, u32[]{:S(2)}, u32[]{:S(2)}) collective-permute-start(bf16[128,1536]{1,0:T(8,128)(2,1)} %cot_ref.1), channel_id=1, source_target_pairs={{0,8},{2,10},{4,12},{6,14},{8,0},{10,2},{12,4},{14,6},{1,9},{3,11}... | collective-permute-start | bytes 1179656 | tf_op jit(solution)/shard_map/ppermute | solution.py:498
  38.4 28.1 %collective-permute-start.6 = (bf16[64,1664]{1,0:T(8,128)(2,1)S(1)}, bf16[64,1664]{1,0:T(8,128)(2,1)S(1)}, u32[]{:S(2)}, u32[]{:S(2)}) collective-permute-start(bf16[64,1664]{1,0:T(8,128)(2,1)S(1)} %get-tuple-element.66), channel_id=1, source_target_pairs={{0,2},{2,0},{4,6},{6,4},{8,10},{10,8},{12,14},{14,12},{1,3},{3,1},... | collective-permute-start | bytes 638984 | tf_op jit(solution)/shard_map/ppermute | solution.py:509
  39.8 38.2 %collective-permute-start.7 = (bf16[64,1664]{1,0:T(8,128)(2,1)}, bf16[64,1664]{1,0:T(8,128)(2,1)S(1)}, u32[]{:S(2)}, u32[]{:S(2)}) collective-permute-start(bf16[64,1664]{1,0:T(8,128)(2,1)} %get-tuple-element.67), channel_id=1, source_target_pairs={{0,4},{2,6},{4,0},{6,2},{8,12},{10,14},{12,8},{14,10},{1,5},{3,7},... | collective-permute-start | bytes 638984 | tf_op jit(solution)/shard_map/ppermute | solution.py:509
  41.0 25.6 %copy-start.4 = (f32[3,32,1536]{2,1,0:T(8,128)S(1)}, f32[3,32,1536]{2,1,0:T(8,128)}, u32[]{:S(2)}) copy-start(f32[3,32,1536]{2,1,0:T(8,128)} %table_ref.1) | copy-start | bytes 1769476
  41.0 25.6 %copy-start.18 = (bf16[8,1536]{1,0:T(8,128)(2,1)S(1)}, bf16[8,1536]{1,0:T(8,128)(2,1)}, u32[]{:S(2)}) copy-start(bf16[8,1536]{1,0:T(8,128)(2,1)} %refs_5_.3) | copy-start | bytes 73732
  41.0 37.0 %collective-permute-start.8 = (bf16[64,1664]{1,0:T(8,128)(2,1)}, bf16[64,1664]{1,0:T(8,128)(2,1)S(1)}, u32[]{:S(2)}, u32[]{:S(2)}) collective-permute-start(bf16[64,1664]{1,0:T(8,128)(2,1)} %get-tuple-element.68), channel_id=1, source_target_pairs={{0,6},{2,4},{4,2},{6,0},{8,14},{10,12},{12,10},{14,8},{1,7},{3,5},... | collective-permute-start | bytes 638984 | tf_op jit(solution)/shard_map/ppermute | solution.py:509
  60.1 21.0 %collective-permute-start.3 = (bf16[64,1536]{1,0:T(8,128)(2,1)}, bf16[64,1536]{1,0:T(8,128)(2,1)}, u32[]{:S(2)}, u32[]{:S(2)}) collective-permute-start(bf16[64,1536]{1,0:T(8,128)(2,1)} %get-tuple-element.60), channel_id=1, source_target_pairs={{0,2},{2,0},{4,6},{6,4},{8,10},{10,8},{12,14},{14,12},{1,3},{3,1},... | collective-permute-start | bytes 589832 | tf_op jit(solution)/shard_map/ppermute | solution.py:509
  61.3 19.9 %collective-permute-start.4 = (bf16[64,1536]{1,0:T(8,128)(2,1)}, bf16[64,1536]{1,0:T(8,128)(2,1)}, u32[]{:S(2)}, u32[]{:S(2)}) collective-permute-start(bf16[64,1536]{1,0:T(8,128)(2,1)} %get-tuple-element.61), channel_id=1, source_target_pairs={{0,4},{2,6},{4,0},{6,2},{8,12},{10,14},{12,8},{14,10},{1,5},{3,7},... | collective-permute-start | bytes 589832 | tf_op jit(solution)/shard_map/ppermute | solution.py:509
  66.5 14.6 %collective-permute-start.5 = (bf16[64,1536]{1,0:T(8,128)(2,1)}, bf16[64,1536]{1,0:T(8,128)(2,1)}, u32[]{:S(2)}, u32[]{:S(2)}) collective-permute-start(bf16[64,1536]{1,0:T(8,128)(2,1)} %get-tuple-element.62), channel_id=1, source_target_pairs={{0,6},{2,4},{4,2},{6,0},{8,14},{10,12},{12,10},{14,8},{1,7},{3,5},... | collective-permute-start | bytes 589832 | tf_op jit(solution)/shard_map/ppermute | solution.py:509
  66.6 1.7 %copy-start = (bf16[1,1536,768]{2,1,0:T(8,128)(2,1)S(1)}, bf16[1,1536,768]{2,1,0:T(8,128)(2,1)}, u32[]{:S(2)}) copy-start(bf16[1,1536,768]{2,1,0:T(8,128)(2,1)} %all-gather.9.cloned.1.call-done) | copy-start | bytes 7077892
  68.3 1.7 %copy-start.2 = (bf16[1,1536,768]{2,1,0:T(8,128)(2,1)S(1)}, bf16[1,1536,768]{2,1,0:T(8,128)(2,1)}, u32[]{:S(2)}) copy-start(bf16[1,1536,768]{2,1,0:T(8,128)(2,1)} %all-gather.11.cloned.1.call-done) | copy-start | bytes 7077892
  70.0 1.7 %copy-start.5 = (bf16[1,1536,768]{2,1,0:T(8,128)(2,1)S(1)}, bf16[1,1536,768]{2,1,0:T(8,128)(2,1)}, u32[]{:S(2)}) copy-start(bf16[1,1536,768]{2,1,0:T(8,128)(2,1)} %all-gather.7.cloned.1.call-done) | copy-start | bytes 7077892
  71.6 6.5 %copy-start.1 = (bf16[1,1536,768]{2,1,0:T(8,128)(2,1)S(1)}, bf16[1,1536,768]{2,1,0:T(8,128)(2,1)}, u32[]{:S(2)}) copy-start(bf16[1,1536,768]{2,1,0:T(8,128)(2,1)} %all-gather.9.cloned.1.call-done) | copy-start | bytes 7077892
  78.1 3.0 %copy-start.13 = (bf16[64,1664]{1,0:T(8,128)(2,1)}, bf16[64,1664]{1,0:T(8,128)(2,1)S(1)}, u32[]{:S(2)}) copy-start(bf16[64,1664]{1,0:T(8,128)(2,1)S(1)} %collective-permute-done.7.refs_2_.refs_3_) | copy-start | bytes 638980
  78.1 3.0 %copy-start.15 = (bf16[64,1664]{1,0:T(8,128)(2,1)}, bf16[64,1664]{1,0:T(8,128)(2,1)S(1)}, u32[]{:S(2)}) copy-start(bf16[64,1664]{1,0:T(8,128)(2,1)S(1)} %collective-permute-done.8.refs_3_.refs_4_) | copy-start | bytes 638980
  78.1 3.0 %copy-start.3 = (bf16[1,1536,768]{2,1,0:T(8,128)(2,1)S(1)}, bf16[1,1536,768]{2,1,0:T(8,128)(2,1)}, u32[]{:S(2)}) copy-start(bf16[1,1536,768]{2,1,0:T(8,128)(2,1)} %all-gather.11.cloned.1.call-done) | copy-start | bytes 7077892
  78.1 3.0 %copy-start.6 = (bf16[1,1536,768]{2,1,0:T(8,128)(2,1)S(1)}, bf16[1,1536,768]{2,1,0:T(8,128)(2,1)}, u32[]{:S(2)}) copy-start(bf16[1,1536,768]{2,1,0:T(8,128)(2,1)} %all-gather.7.cloned.1.call-done) | copy-start | bytes 7077892
  84.8 13.3 %collective-permute-start.10 = (bf16[64,1536]{1,0:T(8,128)(2,1)S(1)}, bf16[64,1536]{1,0:T(8,128)(2,1)S(1)}, u32[]{:S(2)}, u32[]{:S(2)}) collective-permute-start(bf16[64,1536]{1,0:T(8,128)(2,1)S(1)} %get-tuple-element.80.refs_8_), channel_id=1, source_target_pairs={{0,4},{2,6},{4,0},{6,2},{8,12},{10,14},{12,8},{14,10},{1,5},{3,7},... | collective-permute-start | bytes 589832 | tf_op jit(solution)/shard_map/ppermute | solution.py:509
  86.3 11.8 %collective-permute-start.11 = (bf16[64,1536]{1,0:T(8,128)(2,1)S(1)}, bf16[64,1536]{1,0:T(8,128)(2,1)S(1)}, u32[]{:S(2)}, u32[]{:S(2)}) collective-permute-start(bf16[64,1536]{1,0:T(8,128)(2,1)S(1)} %get-tuple-element.81.refs_9_), channel_id=1, source_target_pairs={{0,6},{2,4},{4,2},{6,0},{8,14},{10,12},{12,10},{14,8},{1,7},{3,5},... | collective-permute-start | bytes 589832 | tf_op jit(solution)/shard_map/ppermute | solution.py:509
  87.3 10.9 %collective-permute-start.9 = (bf16[64,1536]{1,0:T(8,128)(2,1)S(1)}, bf16[64,1536]{1,0:T(8,128)(2,1)S(1)}, u32[]{:S(2)}, u32[]{:S(2)}) collective-permute-start(bf16[64,1536]{1,0:T(8,128)(2,1)S(1)} %get-tuple-element.79.refs_7_), channel_id=1, source_target_pairs={{0,2},{2,0},{4,6},{6,4},{8,10},{10,8},{12,14},{14,12},{1,3},{3,1},... | collective-permute-start | bytes 589832 | tf_op jit(solution)/shard_map/ppermute | solution.py:509
  87.5 6.5 %copy-start.14 = (bf16[64,1664]{1,0:T(8,128)(2,1)S(1)}, bf16[64,1664]{1,0:T(8,128)(2,1)}, u32[]{:S(2)}) copy-start(bf16[64,1664]{1,0:T(8,128)(2,1)} %copy-done.13) | copy-start | bytes 638980
  87.5 6.5 %copy-start.16 = (bf16[64,1664]{1,0:T(8,128)(2,1)S(1)}, bf16[64,1664]{1,0:T(8,128)(2,1)}, u32[]{:S(2)}) copy-start(bf16[64,1664]{1,0:T(8,128)(2,1)} %copy-done.15) | copy-start | bytes 638980
  87.5 6.5 %copy-start.17 = (bf16[128,1536]{1,0:T(8,128)(2,1)S(1)}, bf16[128,1536]{1,0:T(8,128)(2,1)}, u32[]{:S(2)}) copy-start(bf16[128,1536]{1,0:T(8,128)(2,1)} %refs_16_.1) | copy-start | bytes 1179652
  94.0 4.0 %copy-start.7 = (bf16[1536,384]{1,0:T(8,128)(2,1)}, bf16[1536,384]{1,0:T(8,128)(2,1)S(1)}, u32[]{:S(2)}) copy-start(bf16[1536,384]{1,0:T(8,128)(2,1)S(1)} %get-tuple-element.92.refs_0_) | copy-start | bytes 3538948
  94.0 4.1 %copy-start.9 = (bf16[1536,384]{1,0:T(8,128)(2,1)}, bf16[1536,384]{1,0:T(8,128)(2,1)S(1)}, u32[]{:S(2)}) copy-start(bf16[1536,384]{1,0:T(8,128)(2,1)S(1)} %get-tuple-element.93.refs_1_) | copy-start | bytes 3538948
  94.0 4.1 %copy-start.11 = (bf16[1536,384]{1,0:T(8,128)(2,1)}, bf16[1536,384]{1,0:T(8,128)(2,1)S(1)}, u32[]{:S(2)}) copy-start(bf16[1536,384]{1,0:T(8,128)(2,1)S(1)} %get-tuple-element.94.refs_2_) | copy-start | bytes 3538948
  99.9 19.9 %collective-permute-start.15 = (bf16[3,1536,384]{2,1,0:T(8,128)(2,1)}, bf16[3,1536,384]{2,1,0:T(8,128)(2,1)}, u32[]{:S(2)}, u32[]{:S(2)}) collective-permute-start(bf16[3,1536,384]{2,1,0:T(8,128)(2,1)} %get-tuple-element.91), channel_id=1, source_target_pairs={{0,1},{1,0},{2,3},{3,2},{4,5},{5,4},{6,7},{7,6},{8,9},{9,8},{10,11... | collective-permute-start | bytes 10616840 | tf_op jit(solution)/shard_map/ppermute | solution.py:550
  104.1 6.0 %collective-permute-start.12 = (bf16[64,1536]{1,0:T(8,128)(2,1)S(1)}, bf16[64,1536]{1,0:T(8,128)(2,1)S(1)}, u32[]{:S(2)}, u32[]{:S(2)}) collective-permute-start(bf16[64,1536]{1,0:T(8,128)(2,1)S(1)} %select_convert_fusion), channel_id=1, source_target_pairs={{0,1},{1,0},{2,3},{3,2},{4,5},{5,4},{6,7},{7,6},{8,9},{9,8},{10,11... | collective-permute-start | bytes 589832 | tf_op jit(solution)/shard_map/ppermute | solution.py:427
  104.2 15.5 %copy-start.8 = (bf16[1536,384]{1,0:T(8,128)(2,1)S(1)}, bf16[1536,384]{1,0:T(8,128)(2,1)}, u32[]{:S(2)}) copy-start(bf16[1536,384]{1,0:T(8,128)(2,1)} %copy-done.7) | copy-start | bytes 3538948
  104.2 27.0 %all-to-all-start.1 = ((bf16[4,64,1536]{2,1,0:T(8,128)(2,1)}), bf16[4,64,1536]{2,1,0:T(8,128)(2,1)}, u32[]{:S(2)}, u32[]{:S(2)}) async-start(bf16[4,64,1536]{2,1,0:T(8,128)(2,1)} %bitcast.10), calls=%async_computation.1 | async-start | bytes 1572864 | tf_op jit(solution)/shard_map/all_to_all | solution.py:502
  108.6 11.2 %copy-start.10 = (bf16[1536,384]{1,0:T(8,128)(2,1)S(1)}, bf16[1536,384]{1,0:T(8,128)(2,1)}, u32[]{:S(2)}) copy-start(bf16[1536,384]{1,0:T(8,128)(2,1)} %copy-done.9) | copy-start | bytes 3538948
  108.6 11.2 %copy-start.12 = (bf16[1536,384]{1,0:T(8,128)(2,1)S(1)}, bf16[1536,384]{1,0:T(8,128)(2,1)}, u32[]{:S(2)}) copy-start(bf16[1536,384]{1,0:T(8,128)(2,1)} %copy-done.11) | copy-start | bytes 3538948
  110.2 9.5 %collective-permute-start.13 = (bf16[32,1536]{1,0:T(8,128)(2,1)S(1)}, bf16[32,1536]{1,0:T(8,128)(2,1)S(1)}, u32[]{:S(2)}, u32[]{:S(2)}) collective-permute-start(bf16[32,1536]{1,0:T(8,128)(2,1)S(1)} %select_convert_fusion.1), channel_id=1, source_target_pairs={{0,2},{2,0},{4,6},{6,4},{8,10},{10,8},{12,14},{14,12},{1,3},{3,1},... | collective-permute-start | bytes 294920 | tf_op jit(solution)/shard_map/ppermute | solution.py:427
  111.4 19.8 %collective-permute-start.14 = (bf16[128,1536]{1,0:T(8,128)(2,1)}, bf16[128,1536]{1,0:T(8,128)(2,1)S(1)}, u32[]{:S(2)}, u32[]{:S(2)}) collective-permute-start(bf16[128,1536]{1,0:T(8,128)(2,1)} %merge.1), channel_id=1, source_target_pairs={{0,8},{2,10},{4,12},{6,14},{8,0},{10,2},{12,4},{14,6},{1,9},{3,11}... | collective-permute-start | bytes 1179656 | tf_op jit(solution)/shard_map/ppermute | solution.py:498
  125.3 23.0 %copy-start.20 = (bf16[128,1536]{1,0:T(8,128)(2,1)S(1)}, bf16[128,1536]{1,0:T(8,128)(2,1)}, u32[]{:S(2)}) copy-start(bf16[128,1536]{1,0:T(8,128)(2,1)} %tok_ref.1) | copy-start | bytes 1179652
  131.3 3.5 %collective-permute-start.16 = (bf16[32,1536]{1,0:T(8,128)(2,1)S(1)}, bf16[32,1536]{1,0:T(8,128)(2,1)S(1)}, u32[]{:S(2)}, u32[]{:S(2)}) collective-permute-start(bf16[32,1536]{1,0:T(8,128)(2,1)S(1)} %reduce-precision_convert_fusion.1), channel_id=1, source_target_pairs={{0,4},{2,6},{4,0},{6,2},{8,12},{10,14},{12,8},{14,10},{1,5},{3,7},... | collective-permute-start | bytes 294920 | tf_op jit(solution)/shard_map/ppermute | solution.py:427
  134.8 5.2 %collective-permute-start.17 = (bf16[32,1536]{1,0:T(8,128)(2,1)S(1)}, bf16[32,1536]{1,0:T(8,128)(2,1)S(1)}, u32[]{:S(2)}, u32[]{:S(2)}) collective-permute-start(bf16[32,1536]{1,0:T(8,128)(2,1)S(1)} %fusion), channel_id=1, source_target_pairs={{0,8},{2,10},{4,12},{6,14},{8,0},{10,2},{12,4},{14,6},{1,9},{3,11}... | collective-permute-start | bytes 294920 | tf_op jit(solution)/shard_map/ppermute | solution.py:427
  140.1 3.5 %collective-permute-start.18 = (bf16[32,1536]{1,0:T(8,128)(2,1)S(1)}, bf16[32,1536]{1,0:T(8,128)(2,1)S(1)}, u32[]{:S(2)}, u32[]{:S(2)}) collective-permute-start(bf16[32,1536]{1,0:T(8,128)(2,1)S(1)} %reduce-precision_convert_fusion), channel_id=1, source_target_pairs={{0,2},{2,0},{4,6},{6,4},{8,10},{10,8},{12,14},{14,12},{1,3},{3,1},... | collective-permute-start | bytes 294920 | tf_op jit(solution)/shard_map/ppermute | solution.py:427
  143.7 7.5 %collective-permute-start.19 = (bf16[64,1536]{1,0:T(8,128)(2,1)S(1)}, bf16[64,1536]{1,0:T(8,128)(2,1)S(1)}, u32[]{:S(2)}, u32[]{:S(2)}) collective-permute-start(bf16[64,1536]{1,0:T(8,128)(2,1)S(1)} %pad_maximum_fusion.1), channel_id=1, source_target_pairs={{0,1},{1,0},{2,3},{3,2},{4,5},{5,4},{6,7},{7,6},{8,9},{9,8},{10,11... | collective-permute-start | bytes 589832 | tf_op jit(solution)/shard_map/ppermute | solution.py:427
Sparse Core Ops, SparseCore 0:
  9.6 13.3 all-gather.8
  24.5 12.0 all-gather.10
  38.2 12.0 all-gather.6

commit v4 on v3

--- a/solution.py
+++ b/solution.py
@@ -522,11 +522,16 @@
     far_tokens = hop(tokens)
     far_meta = hop(meta)
     (near,) = pack(me, meta, [tokens, cotangent], True, False, half, cap)
-    far_tokens, near, far_meta = lax.optimization_barrier((far_tokens, near, far_meta))
+    near, far_meta = lax.optimization_barrier((near, far_meta))
     near = trade(near)
-    far_cot = hop(after(cotangent, far_tokens))
-    far = fan(pack(me, far_meta, [far_tokens], True, True, half, cap))
-    far_cots = fan(pack(me, far_meta, [far_cot], False, True, half, cap))
+    far_cot = hop(cotangent)
+    far_cot, down = lax.optimization_barrier((far_cot, down))
+    far = pack(me, far_meta, [far_tokens], True, True, half, cap)
+    far_cots = pack(me, far_meta, [far_cot], False, True, half, cap)
+    far = fan(far)
+    near, kept = lax.optimization_barrier((near, far_cots[0]))
+    far_cots = [kept] + list(far_cots[1:])
+    far_cots = fan(far_cots)
 
     near_backs, near_late, near_stats = whole(me, [near], modulation, router, down, gate, up)
     near_late, far = lax.optimization_barrier((near_late, far))

time: 160 us -> 154 us (0.963)
  waiting for transfers between devices: 60.1 us -> 54.1 us
  local copies, waits for them, and re-layouts: 6.76 us -> 8.52 us
    ppermute x4, waiting for transfers between devices: 37.5 us -> 31.6 us  [hop(): return lax.ppermute(array, 'expert', across)]
    ppermute x9, starting transfers between devices: 11.8 us -> 9.16 us  [fan(): lax.ppermute(blocks[k], 'expert', [(e, e ^ k) for e in range(experts)])]
    ppermute x1, starting transfers between devices: 4.23 us -> 6.65 us  [local(): lax.ppermute(other, 'dp', [(i, dp_axis - 1 - i) for i in range(dp_axis)])]
    unnamed x46 -> x58, local copies, waits for them, and re-layouts: 5.08 us -> 6.83 us
where the time goes in v4:
time: 154 us; the launch traced here: 153 us
  waiting for transfers between devices  54.1 us (35%)
  Pallas kernels  39.1 us (25%)
  starting transfers between devices  37 us (24%)
  between operations  14.2 us (9%)
  local copies, waits for them, and re-layouts  8.52 us (6%)
    ppermute x4, waiting for transfers between devices, hop(): return lax.ppermute(array, 'expert', across)  31.6 us
    ppermute x6, waiting for transfers between devices, flip(): lax.ppermute(values.astype(bf16), name, [(i, i ^ bit) for i in range(size)])  20.4 us
    ppermute x9, starting transfers between devices, fan(): lax.ppermute(blocks[k], 'expert', [(e, e ^ k) for e in range(experts)])  9.16 us
    all_to_all x2, starting transfers between devices, trade(): lax.all_to_all(blocks, 'expert', split_axis=0, concat_axis=0, tiled=True,...  7.93 us
    unnamed x58, local copies, waits for them, and re-layouts  6.83 us
    ppermute x4, starting transfers between devices, hop(): return lax.ppermute(array, 'expert', across)  6.82 us
    ppermute x1, starting transfers between devices, local(): lax.ppermute(other, 'dp', [(i, dp_axis - 1 - i) for i in range(dp_axis)])  6.65 us
    pallas_call x1, Pallas kernels, grads(): pl.pallas_call(grads_kernel, out_shape=[jax.ShapeDtypeStruct((width, full...  6.48 us
  transfers between devices with their start and end apart: 25, of which 8 were waited for; matrix products, arithmetic and copies ran while one was open for 0% of the time, Pallas kernels for 22%

profile of v4, /device:TPU:1, one launch (start us, length us, event | category | flops | bytes accessed | tf_op | source)
XLA Modules:
  0.0 153.4 jit_solution(1683903709648480236)
XLA Ops:
  7.3 0.7 all-gather.7.cloned.1.call-update
  8.0 0.7 all-gather.9.cloned.1.call-update
  8.9 3.1 %collective-permute-start = (s32[8,128]{1,0:T(8,128)S(1)}, s32[8,128]{1,0:T(8,128)S(1)}, u32[]{:S(2)}, u32[]{:S(2)}) collective-permute-start(s32[8,128]{1,0:T(8,128)S(1)} %add_add_fusion.meta_ref.refs_14_), channel_id=1, source_target_pairs={{0,8},{2,10},{4,12},{6,14},{8,0},{10,2},{12,4},{14,6},{1,9},{3,11}... | collective-permute-start | bytes 12296 | tf_op jit(solution)/shard_map/ppermute | solution.py:498
  12.1 2.5 %pack.3 = bf16[256,3200]{1,0:T(8,128)(2,1)} custom-call(s32[3]{0:T(128)S(1)} %pad_add_fusion.me_ref, s32[8,128]{1,0:T(8,128)S(1)} %add_add_fusion.meta_ref.refs_14_, bf16[128,1536]{1,0:T(8,128)(2,1)S(1)} %copy-done.22, bf16[128,1536]{1,0:T(8,128)(2,1)S(1)} %copy-done.18), custom_call_target="tpu_custom_call" | custom-call | flops 1000000000 | bytes 4000000 | tf_op jit(solution)/shard_map/pack/pallas_call | solution.py:115
  14.6 3.6 %all-to-all-start = ((bf16[4,64,3200]{2,1,0:T(8,128)(2,1)}), bf16[4,64,3200]{2,1,0:T(8,128)(2,1)S(1)}, u32[]{:S(2)}, u32[]{:S(2)}) async-start(bf16[4,64,3200]{2,1,0:T(8,128)(2,1)} %bitcast.5), calls=%async_computation | async-start | bytes 3276800 | tf_op jit(solution)/shard_map/all_to_all | solution.py:502
  18.2 0.7 all-gather.11.cloned.1.call-update
  18.9 0.8 collective-permute-start.5
  19.7 1.6 %collective-permute-start.1 = (bf16[128,1536]{1,0:T(8,128)(2,1)S(1)}, bf16[128,1536]{1,0:T(8,128)(2,1)S(1)}, u32[]{:S(2)}, u32[]{:S(2)}) collective-permute-start(bf16[128,1536]{1,0:T(8,128)(2,1)S(1)} %copy-done.18), channel_id=1, source_target_pairs={{0,8},{2,10},{4,12},{6,14},{8,0},{10,2},{12,4},{14,6},{1,9},{3,11}... | collective-permute-start | bytes 1179656 | tf_op jit(solution)/shard_map/ppermute | solution.py:498
  21.3 22.2 %collective-permute-done.5.refs_0_ = bf16[128,1536]{1,0:T(8,128)(2,1)S(1)} collective-permute-done((bf16[128,1536]{1,0:T(8,128)(2,1)S(1)}, bf16[128,1536]{1,0:T(8,128)(2,1)S(1)}, u32[]{:S(2)}, u32[]{:S(2)}) %collective-permute-start.5) | collective-permute-done | bytes 393248 | tf_op jit(solution)/shard_map/ppermute | solution.py:498
  43.5 1.8 %pack.5 = (bf16[64,1664]{1,0:T(8,128)(2,1)S(1)}, bf16[64,1664]{1,0:T(8,128)(2,1)}, bf16[64,1664]{1,0:T(8,128)(2,1)}, bf16[64,1664]{1,0:T(8,128)(2,1)}) custom-call(s32[3]{0:T(128)S(1)} %pad_add_fusion.me_ref, s32[8,128]{1,0:T(8,128)S(1)} %collective-permute-done.meta_ref, bf16[128,1536]{1,0:T(8,128)(2,1)S(1)} %collective-permute-done.5.refs_0_), custom_call_target="tpu_custom_call" | custom-call | flops 1000000000 | bytes 4000000 | tf_op jit(solution)/shard_map/pack/pallas_call | solution.py:115
  45.3 1.1 collective-permute-start.6
  46.5 1.8 %collective-permute-start.7 = (bf16[64,1664]{1,0:T(8,128)(2,1)}, bf16[64,1664]{1,0:T(8,128)(2,1)S(1)}, u32[]{:S(2)}, u32[]{:S(2)}) collective-permute-start(bf16[64,1664]{1,0:T(8,128)(2,1)} %get-tuple-element.71), channel_id=1, source_target_pairs={{0,4},{2,6},{4,0},{6,2},{8,12},{10,14},{12,8},{14,10},{1,5},{3,7},... | collective-permute-start | bytes 638984 | tf_op jit(solution)/shard_map/ppermute | solution.py:509
  48.3 3.6 %collective-permute-done.1.refs_0_ = bf16[128,1536]{1,0:T(8,128)(2,1)S(1)} collective-permute-done((bf16[128,1536]{1,0:T(8,128)(2,1)S(1)}, bf16[128,1536]{1,0:T(8,128)(2,1)S(1)}, u32[]{:S(2)}, u32[]{:S(2)}) %collective-permute-start.1) | collective-permute-done | bytes 393248 | tf_op jit(solution)/shard_map/ppermute | solution.py:498
  52.0 0.7 copy-done.24
  52.7 1.0 copy-done.25
  53.7 1.7 %pack.4 = (bf16[64,1536]{1,0:T(8,128)(2,1)S(1)}, bf16[64,1536]{1,0:T(8,128)(2,1)}, bf16[64,1536]{1,0:T(8,128)(2,1)}, bf16[64,1536]{1,0:T(8,128)(2,1)S(1)}) custom-call(s32[3]{0:T(128)S(1)} %pad_add_fusion.me_ref, s32[8,128]{1,0:T(8,128)S(1)} %collective-permute-done.meta_ref, bf16[128,1536]{1,0:T(8,128)(2,1)S(1)} %copy-done.25), custom_call_target="tpu_custom_call" | custom-call | flops 1000000000 | bytes 4000000 | tf_op jit(solution)/shard_map/pack/pallas_call | solution.py:115
  55.4 1.1 collective-permute-start.2
  56.6 1.8 %collective-permute-start.3 = (bf16[64,1536]{1,0:T(8,128)(2,1)}, bf16[64,1536]{1,0:T(8,128)(2,1)}, u32[]{:S(2)}, u32[]{:S(2)}) collective-permute-start(bf16[64,1536]{1,0:T(8,128)(2,1)} %get-tuple-element.64), channel_id=1, source_target_pairs={{0,4},{2,6},{4,0},{6,2},{8,12},{10,14},{12,8},{14,10},{1,5},{3,7},... | collective-permute-start | bytes 589832 | tf_op jit(solution)/shard_map/ppermute | solution.py:509
  58.4 0.5 collective-permute-start.4
  58.9 1.7 %copy-done = bf16[1,1536,768]{2,1,0:T(8,128)(2,1)S(1)} copy-done((bf16[1,1536,768]{2,1,0:T(8,128)(2,1)S(1)}, bf16[1,1536,768]{2,1,0:T(8,128)(2,1)}, u32[]{:S(2)}) %copy-start) | copy-done | bytes 2359320
  60.6 1.7 %copy-done.2 = bf16[1,1536,768]{2,1,0:T(8,128)(2,1)S(1)} copy-done((bf16[1,1536,768]{2,1,0:T(8,128)(2,1)S(1)}, bf16[1,1536,768]{2,1,0:T(8,128)(2,1)}, u32[]{:S(2)}) %copy-start.2) | copy-done | bytes 2359320
  62.2 1.7 %copy-done.5 = bf16[1,1536,768]{2,1,0:T(8,128)(2,1)S(1)} copy-done((bf16[1,1536,768]{2,1,0:T(8,128)(2,1)S(1)}, bf16[1,1536,768]{2,1,0:T(8,128)(2,1)}, u32[]{:S(2)}) %copy-start.5) | copy-done | bytes 2359320
  63.9 6.4 %expert_whole.1 = (bf16[256,1536]{1,0:T(8,128)(2,1)}, bf16[256,5376]{1,0:T(8,128)(2,1)S(1)}, f32[256,128]{1,0:T(8,128)S(1)}) custom-call(s32[3]{0:T(128)S(1)} %pad_add_fusion.me_ref, bf16[256,3200]{1,0:T(8,128)(2,1)S(1)} %bitcast.20, f32[3,32,1536]{2,1,0:T(8,128)S(1)} %copy-done.4, bf16[8,1536]{1,0:T(8,128)(2,1)S(1)} %copy-done.21, ...), custom_call_target="tpu_custom_call" | custom-call | flops 3019898880 | bytes 11173888 | tf_op jit(solution)/shard_map/expert_whole/pallas_call | solution.py:271
  70.4 3.0 %expert_in.1 = (bf16[256,1536]{1,0:T(8,128)(2,1)S(1)}, f32[256,128]{1,0:T(8,128)S(1)}, f32[256,768]{1,0:T(8,128)S(1)}, f32[256,768]{1,0:T(8,128)S(1)}, bf16[256,768]{1,0:T(8,128)(2,1)S(1)}) custom-call(s32[3]{0:T(128)S(1)} %pad_add_fusion.me_ref, bf16[64,1664]{1,0:T(8,128)(2,1)S(1)} %get-tuple-element.73.refs_0_.refs_1_, ...), custom_call_target="tpu_custom_call" | custom-call | flops 1207959552 | bytes 7790592 | tf_op jit(solution)/shard_map/expert_in/pallas_call | solution.py:205
  73.5 3.6 %expert_back.1 = (bf16[64,1536]{1,0:T(8,128)(2,1)S(1)}, bf16[64,1536]{1,0:T(8,128)(2,1)S(1)}, bf16[64,1536]{1,0:T(8,128)(2,1)S(1)}, bf16[64,1536]{1,0:T(8,128)(2...) custom-call(s32[3]{0:T(128)S(1)} %pad_add_fusion.me_ref, bf16[64,1536]{1,0:T(8,128)(2,1)S(1)} %get-tuple-element.62.refs_0_, ...), custom_call_target="tpu_custom_call" | custom-call | flops 1811939328 | bytes 11173888 | tf_op jit(solution)/shard_map/expert_back/pallas_call | solution.py:244
  77.1 1.5 collective-permute-start.10
  78.5 0.6 collective-permute-start.11
  79.1 0.7 collective-permute-start.9
  79.8 6.5 %weight_grads.1 = (bf16[1536,384]{1,0:T(8,128)(2,1)S(1)}, bf16[1536,384]{1,0:T(8,128)(2,1)S(1)}, bf16[1536,384]{1,0:T(8,128)(2,1)S(1)}, bf16[3,1536,384]{2,1,0:T(8,128)(2,1)}) custom-call(s32[3]{0:T(128)S(1)} %pad_add_fusion.me_ref, bf16[256,5376]{1,0:T(8,128)(2,1)S(1)} %get-tuple-element.87.refs_10_.near_ref, ...), custom_call_target="tpu_custom_call" | custom-call | flops 1000000 | bytes 10000 | tf_op jit(solution)/shard_map/weight_grads/pallas_call | solution.py:364
  86.3 3.6 %table_sums.1 = f32[128,1536]{1,0:T(8,128)S(1)} custom-call(s32[3]{0:T(128)S(1)} %pad_add_fusion.me_ref, bf16[256,3200]{1,0:T(8,128)(2,1)S(1)} %bitcast.21, bf16[64,1664]{1,0:T(8,128)(2,1)S(1)} %get-tuple-element.73.refs_0_.refs_1_, bf16[64,1664]{1,0:T(8,128)(2,1)S(1)} %collective-permute-done.6.refs_1_.refs_2_, bf16[64,1664]{1,0:T(8,128)(2,1)S(1)} %copy-done.14, ...), custom_call_target="tpu_custom_call" | custom-call | flops 1000000 | bytes 10000 | tf_op jit(solution)/shard_map/table_sums/pallas_call | solution.py:335
  90.0 1.7 %merge.1 = bf16[128,1536]{1,0:T(8,128)(2,1)} custom-call(s32[3]{0:T(128)S(1)} %pad_add_fusion.me_ref, s32[8,128]{1,0:T(8,128)S(1)} %collective-permute-done.meta_ref, bf16[64,1536]{1,0:T(8,128)(2,1)S(1)} %get-tuple-element.82.refs_0_.refs_6_, bf16[64,1536]{1,0:T(8,128)(2,1)S(1)} %collective-permute-done.9.refs_1_, ...), custom_call_target="tpu_custom_call" | custom-call | flops 1000000000 | bytes 2000000 | tf_op jit(solution)/shard_map/merge/pallas_call | solution.py:384
  91.7 6.7 %collective-permute-start.15 = (bf16[3,1536,384]{2,1,0:T(8,128)(2,1)}, bf16[3,1536,384]{2,1,0:T(8,128)(2,1)}, u32[]{:S(2)}, u32[]{:S(2)}) collective-permute-start(bf16[3,1536,384]{2,1,0:T(8,128)(2,1)} %get-tuple-element.95), channel_id=1, source_target_pairs={{0,1},{1,0},{2,3},{3,2},{4,5},{5,4},{6,7},{7,6},{8,9},{9,8},{10,11... | collective-permute-start | bytes 10616840 | tf_op jit(solution)/shard_map/ppermute | solution.py:555
  98.5 4.4 %all-to-all-start.1 = ((bf16[4,64,1536]{2,1,0:T(8,128)(2,1)}), bf16[4,64,1536]{2,1,0:T(8,128)(2,1)}, u32[]{:S(2)}, u32[]{:S(2)}) async-start(bf16[4,64,1536]{2,1,0:T(8,128)(2,1)} %bitcast.10), calls=%async_computation.1 | async-start | bytes 1572864 | tf_op jit(solution)/shard_map/all_to_all | solution.py:502
  102.9 1.5 collective-permute-done.12
  104.5 1.1 collective-permute-start.13
  105.6 1.2 collective-permute-start.14
  106.8 7.3 %collective-permute-done.13 = bf16[32,1536]{1,0:T(8,128)(2,1)S(1)} collective-permute-done((bf16[32,1536]{1,0:T(8,128)(2,1)S(1)}, bf16[32,1536]{1,0:T(8,128)(2,1)S(1)}, u32[]{:S(2)}, u32[]{:S(2)}) %collective-permute-start.13) | collective-permute-done | bytes 98336 | tf_op jit(solution)/shard_map/ppermute | solution.py:427
  114.2 5.5 %add.34 = (bf16[1,1536,384]{2,1,0:T(8,128)(2,1)}, bf16[1,1536,384]{2,1,0:T(8,128)(2,1)}, bf16[1,1536,384]{2,1,0:T(8,128)(2,1)}) custom-call(bf16[3,1536,384]{2,1,0:T(8,128)(2,1)} %collective-permute-done.15.other_ref, bf16[1536,384]{1,0:T(8,128)(2,1)S(1)} %copy-done.8, bf16[1536,384]{1,0:T(8,128)(2,1)S(1)} %copy-done.10, bf16[1536,384]{1,0:T(8,128)(2,1)S(1)} %copy-done.12), custom_call_target="tpu_custom_call" | custom-call | flops 1000000 | bytes 10000 | tf_op jit(solution)/shard_map/add/pallas_call | solution.py:465
  119.7 5.7 %collective-permute-done.14.far_ref = bf16[128,1536]{1,0:T(8,128)(2,1)S(1)} collective-permute-done((bf16[128,1536]{1,0:T(8,128)(2,1)}, bf16[128,1536]{1,0:T(8,128)(2,1)S(1)}, u32[]{:S(2)}, u32[]{:S(2)}) %collective-permute-start.14) | collective-permute-done | bytes 393248 | tf_op jit(solution)/shard_map/ppermute | solution.py:498
  125.5 3.5 %collective-permute-done.16 = bf16[32,1536]{1,0:T(8,128)(2,1)S(1)} collective-permute-done((bf16[32,1536]{1,0:T(8,128)(2,1)S(1)}, bf16[32,1536]{1,0:T(8,128)(2,1)S(1)}, u32[]{:S(2)}, u32[]{:S(2)}) %collective-permute-start.16) | collective-permute-done | bytes 98336 | tf_op jit(solution)/shard_map/ppermute | solution.py:427
  129.1 5.1 %collective-permute-done.17 = bf16[32,1536]{1,0:T(8,128)(2,1)S(1)} collective-permute-done((bf16[32,1536]{1,0:T(8,128)(2,1)S(1)}, bf16[32,1536]{1,0:T(8,128)(2,1)S(1)}, u32[]{:S(2)}, u32[]{:S(2)}) %collective-permute-start.17) | collective-permute-done | bytes 98336 | tf_op jit(solution)/shard_map/ppermute | solution.py:427
  134.3 0.5 collective-permute-start.18
  134.7 3.1 %collective-permute-done.18 = bf16[32,1536]{1,0:T(8,128)(2,1)S(1)} collective-permute-done((bf16[32,1536]{1,0:T(8,128)(2,1)S(1)}, bf16[32,1536]{1,0:T(8,128)(2,1)S(1)}, u32[]{:S(2)}, u32[]{:S(2)}) %collective-permute-start.18) | collective-permute-done | bytes 98336 | tf_op jit(solution)/shard_map/ppermute | solution.py:427
  137.9 4.5 %collective-permute-start.19 = (bf16[64,1536]{1,0:T(8,128)(2,1)S(1)}, bf16[64,1536]{1,0:T(8,128)(2,1)S(1)}, u32[]{:S(2)}, u32[]{:S(2)}) collective-permute-start(bf16[64,1536]{1,0:T(8,128)(2,1)S(1)} %pad_maximum_fusion.1), channel_id=1, source_target_pairs={{0,1},{1,0},{2,3},{3,2},{4,5},{5,4},{6,7},{7,6},{8,9},{9,8},{10,11... | collective-permute-start | bytes 589832 | tf_op jit(solution)/shard_map/ppermute | solution.py:427
  142.4 0.1 copy.16.stamp_ref
  142.5 2.8 %final.1 = bf16[128,1536]{1,0:T(8,128)(2,1)} custom-call(s32[3]{0:T(128)S(1)} %pad_add_fusion.me_ref, s32[8,128]{1,0:T(8,128)S(1)} %add_add_fusion.meta_ref.refs_14_, s32[128,1]{1,0:T(8,128)S(1)} %copy.16.stamp_ref, bf16[128,1536]{1,0:T(8,128)(2,1)S(1)} %copy-done.23, bf16[128,1536]{1,0:T(8,128)(2,1)S(1)} %copy-done.20, f32[3,32,1536]{2,1,0:T(8,128)S(1)} %copy-done.4, ...), custom_call_target="tpu_custom_call" | custom-call | flops 1000000000 | bytes 4000000 | tf_op jit(solution)/shard_map/final/pallas_call | solution.py:411
  145.4 0.9 slice.27
  146.2 0.6 slice.26
  (92 shorter events, 1.1 us)
Async XLA Ops:
  7.2 4.9 %copy-start.22 = (bf16[128,1536]{1,0:T(8,128)(2,1)S(1)}, bf16[128,1536]{1,0:T(8,128)(2,1)}, u32[]{:S(2)}) copy-start(bf16[128,1536]{1,0:T(8,128)(2,1)} %tok_ref.1) | copy-start | bytes 1179652
  7.2 4.9 %copy-start.18 = (bf16[128,1536]{1,0:T(8,128)(2,1)S(1)}, bf16[128,1536]{1,0:T(8,128)(2,1)}, u32[]{:S(2)}) copy-start(bf16[128,1536]{1,0:T(8,128)(2,1)} %cot_ref.1) | copy-start | bytes 1179652
  7.2 45.5 %all-gather.7.cloned.1.call-start = ((), (), s32[]{:S(2)}) async-start(), calls=%async_computation.2 | async-start | bytes 3538944 | tf_op jit(solution)/shard_map/all_gather | solution.py:520
  7.9 51.0 %all-gather.9.cloned.1.call-start = ((), (), s32[]{:S(2)}) async-start(), calls=%async_computation.3 | async-start | bytes 3538944 | tf_op jit(solution)/shard_map/all_gather | solution.py:520
  8.9 5.7 %collective-permute-start = (s32[8,128]{1,0:T(8,128)S(1)}, s32[8,128]{1,0:T(8,128)S(1)}, u32[]{:S(2)}, u32[]{:S(2)}) collective-permute-start(s32[8,128]{1,0:T(8,128)S(1)} %add_add_fusion.meta_ref.refs_14_), channel_id=1, source_target_pairs={{0,8},{2,10},{4,12},{6,14},{8,0},{10,2},{12,4},{14,6},{1,9},{3,11}... | collective-permute-start | bytes 12296 | tf_op jit(solution)/shard_map/ppermute | solution.py:498
  14.6 43.8 %all-to-all-start = ((bf16[4,64,3200]{2,1,0:T(8,128)(2,1)}), bf16[4,64,3200]{2,1,0:T(8,128)(2,1)S(1)}, u32[]{:S(2)}, u32[]{:S(2)}) async-start(bf16[4,64,3200]{2,1,0:T(8,128)(2,1)} %bitcast.5), calls=%async_computation | async-start | bytes 3276800 | tf_op jit(solution)/shard_map/all_to_all | solution.py:502
  18.2 40.7 %all-gather.11.cloned.1.call-start = ((), (), s32[]{:S(2)}) async-start(), calls=%async_computation.4 | async-start | bytes 3538944 | tf_op jit(solution)/shard_map/all_gather | solution.py:520
  18.9 24.6 %collective-permute-start.5 = (bf16[128,1536]{1,0:T(8,128)(2,1)S(1)}, bf16[128,1536]{1,0:T(8,128)(2,1)S(1)}, u32[]{:S(2)}, u32[]{:S(2)}) collective-permute-start(bf16[128,1536]{1,0:T(8,128)(2,1)S(1)} %copy-done.22), channel_id=1, source_target_pairs={{0,8},{2,10},{4,12},{6,14},{8,0},{10,2},{12,4},{14,6},{1,9},{3,11}... | collective-permute-start | bytes 1179656 | tf_op jit(solution)/shard_map/ppermute | solution.py:498
  19.7 32.2 %collective-permute-start.1 = (bf16[128,1536]{1,0:T(8,128)(2,1)S(1)}, bf16[128,1536]{1,0:T(8,128)(2,1)S(1)}, u32[]{:S(2)}, u32[]{:S(2)}) collective-permute-start(bf16[128,1536]{1,0:T(8,128)(2,1)S(1)} %copy-done.18), channel_id=1, source_target_pairs={{0,8},{2,10},{4,12},{6,14},{8,0},{10,2},{12,4},{14,6},{1,9},{3,11}... | collective-permute-start | bytes 1179656 | tf_op jit(solution)/shard_map/ppermute | solution.py:498
  45.3 13.1 %collective-permute-start.6 = (bf16[64,1664]{1,0:T(8,128)(2,1)}, bf16[64,1664]{1,0:T(8,128)(2,1)S(1)}, u32[]{:S(2)}, u32[]{:S(2)}) collective-permute-start(bf16[64,1664]{1,0:T(8,128)(2,1)} %get-tuple-element.70), channel_id=1, source_target_pairs={{0,2},{2,0},{4,6},{6,4},{8,10},{10,8},{12,14},{14,12},{1,3},{3,1},... | collective-permute-start | bytes 638984 | tf_op jit(solution)/shard_map/ppermute | solution.py:509
  46.5 23.9 %collective-permute-start.7 = (bf16[64,1664]{1,0:T(8,128)(2,1)}, bf16[64,1664]{1,0:T(8,128)(2,1)S(1)}, u32[]{:S(2)}, u32[]{:S(2)}) collective-permute-start(bf16[64,1664]{1,0:T(8,128)(2,1)} %get-tuple-element.71), channel_id=1, source_target_pairs={{0,4},{2,6},{4,0},{6,2},{8,12},{10,14},{12,8},{14,10},{1,5},{3,7},... | collective-permute-start | bytes 638984 | tf_op jit(solution)/shard_map/ppermute | solution.py:509
  48.3 22.1 %collective-permute-start.8 = (bf16[64,1664]{1,0:T(8,128)(2,1)}, bf16[64,1664]{1,0:T(8,128)(2,1)S(1)}, u32[]{:S(2)}, u32[]{:S(2)}) collective-permute-start(bf16[64,1664]{1,0:T(8,128)(2,1)} %get-tuple-element.72), channel_id=1, source_target_pairs={{0,6},{2,4},{4,2},{6,0},{8,14},{10,12},{12,10},{14,8},{1,7},{3,5},... | collective-permute-start | bytes 638984 | tf_op jit(solution)/shard_map/ppermute | solution.py:509
  53.7 5.2 %copy-start.4 = (f32[3,32,1536]{2,1,0:T(8,128)S(1)}, f32[3,32,1536]{2,1,0:T(8,128)}, u32[]{:S(2)}) copy-start(f32[3,32,1536]{2,1,0:T(8,128)} %table_ref.1) | copy-start | bytes 1769476
  53.7 5.2 %copy-start.21 = (bf16[8,1536]{1,0:T(8,128)(2,1)S(1)}, bf16[8,1536]{1,0:T(8,128)(2,1)}, u32[]{:S(2)}) copy-start(bf16[8,1536]{1,0:T(8,128)(2,1)} %refs_5_.3) | copy-start | bytes 73732
  55.4 18.0 %collective-permute-start.2 = (bf16[64,1536]{1,0:T(8,128)(2,1)}, bf16[64,1536]{1,0:T(8,128)(2,1)}, u32[]{:S(2)}, u32[]{:S(2)}) collective-permute-start(bf16[64,1536]{1,0:T(8,128)(2,1)} %get-tuple-element.63), channel_id=1, source_target_pairs={{0,2},{2,0},{4,6},{6,4},{8,10},{10,8},{12,14},{14,12},{1,3},{3,1},... | collective-permute-start | bytes 589832 | tf_op jit(solution)/shard_map/ppermute | solution.py:509
  56.6 16.8 %collective-permute-start.3 = (bf16[64,1536]{1,0:T(8,128)(2,1)}, bf16[64,1536]{1,0:T(8,128)(2,1)}, u32[]{:S(2)}, u32[]{:S(2)}) collective-permute-start(bf16[64,1536]{1,0:T(8,128)(2,1)} %get-tuple-element.64), channel_id=1, source_target_pairs={{0,4},{2,6},{4,0},{6,2},{8,12},{10,14},{12,8},{14,10},{1,5},{3,7},... | collective-permute-start | bytes 589832 | tf_op jit(solution)/shard_map/ppermute | solution.py:509
  58.4 15.0 %collective-permute-start.4 = (bf16[64,1536]{1,0:T(8,128)(2,1)}, bf16[64,1536]{1,0:T(8,128)(2,1)}, u32[]{:S(2)}, u32[]{:S(2)}) collective-permute-start(bf16[64,1536]{1,0:T(8,128)(2,1)} %copy-done.26), channel_id=1, source_target_pairs={{0,6},{2,4},{4,2},{6,0},{8,14},{10,12},{12,10},{14,8},{1,7},{3,5},... | collective-permute-start | bytes 589832 | tf_op jit(solution)/shard_map/ppermute | solution.py:509
  58.9 1.7 %copy-start = (bf16[1,1536,768]{2,1,0:T(8,128)(2,1)S(1)}, bf16[1,1536,768]{2,1,0:T(8,128)(2,1)}, u32[]{:S(2)}) copy-start(bf16[1,1536,768]{2,1,0:T(8,128)(2,1)} %all-gather.9.cloned.1.call-done) | copy-start | bytes 7077892
  60.6 1.7 %copy-start.2 = (bf16[1,1536,768]{2,1,0:T(8,128)(2,1)S(1)}, bf16[1,1536,768]{2,1,0:T(8,128)(2,1)}, u32[]{:S(2)}) copy-start(bf16[1,1536,768]{2,1,0:T(8,128)(2,1)} %all-gather.11.cloned.1.call-done) | copy-start | bytes 7077892
  63.9 6.5 %copy-start.1 = (bf16[1,1536,768]{2,1,0:T(8,128)(2,1)S(1)}, bf16[1,1536,768]{2,1,0:T(8,128)(2,1)}, u32[]{:S(2)}) copy-start(bf16[1,1536,768]{2,1,0:T(8,128)(2,1)} %all-gather.9.cloned.1.call-done) | copy-start | bytes 7077892
  70.4 3.0 %copy-start.13 = (bf16[64,1664]{1,0:T(8,128)(2,1)}, bf16[64,1664]{1,0:T(8,128)(2,1)S(1)}, u32[]{:S(2)}) copy-start(bf16[64,1664]{1,0:T(8,128)(2,1)S(1)} %collective-permute-done.7.refs_2_.refs_3_) | copy-start | bytes 638980
  70.4 3.0 %copy-start.15 = (bf16[64,1664]{1,0:T(8,128)(2,1)}, bf16[64,1664]{1,0:T(8,128)(2,1)S(1)}, u32[]{:S(2)}) copy-start(bf16[64,1664]{1,0:T(8,128)(2,1)S(1)} %collective-permute-done.8.refs_3_.refs_4_) | copy-start | bytes 638980
  70.4 3.0 %copy-start.3 = (bf16[1,1536,768]{2,1,0:T(8,128)(2,1)S(1)}, bf16[1,1536,768]{2,1,0:T(8,128)(2,1)}, u32[]{:S(2)}) copy-start(bf16[1,1536,768]{2,1,0:T(8,128)(2,1)} %all-gather.11.cloned.1.call-done) | copy-start | bytes 7077892
  70.4 3.0 %copy-start.6 = (bf16[1,1536,768]{2,1,0:T(8,128)(2,1)S(1)}, bf16[1,1536,768]{2,1,0:T(8,128)(2,1)}, u32[]{:S(2)}) copy-start(bf16[1,1536,768]{2,1,0:T(8,128)(2,1)} %all-gather.7.cloned.1.call-done) | copy-start | bytes 7077892
  77.1 12.9 %collective-permute-start.10 = (bf16[64,1536]{1,0:T(8,128)(2,1)S(1)}, bf16[64,1536]{1,0:T(8,128)(2,1)S(1)}, u32[]{:S(2)}, u32[]{:S(2)}) collective-permute-start(bf16[64,1536]{1,0:T(8,128)(2,1)S(1)} %get-tuple-element.84.refs_8_), channel_id=1, source_target_pairs={{0,4},{2,6},{4,0},{6,2},{8,12},{10,14},{12,8},{14,10},{1,5},{3,7},... | collective-permute-start | bytes 589832 | tf_op jit(solution)/shard_map/ppermute | solution.py:509
  78.5 11.4 %collective-permute-start.11 = (bf16[64,1536]{1,0:T(8,128)(2,1)S(1)}, bf16[64,1536]{1,0:T(8,128)(2,1)S(1)}, u32[]{:S(2)}, u32[]{:S(2)}) collective-permute-start(bf16[64,1536]{1,0:T(8,128)(2,1)S(1)} %get-tuple-element.85.refs_9_), channel_id=1, source_target_pairs={{0,6},{2,4},{4,2},{6,0},{8,14},{10,12},{12,10},{14,8},{1,7},{3,5},... | collective-permute-start | bytes 589832 | tf_op jit(solution)/shard_map/ppermute | solution.py:509
  79.1 10.9 %collective-permute-start.9 = (bf16[64,1536]{1,0:T(8,128)(2,1)S(1)}, bf16[64,1536]{1,0:T(8,128)(2,1)S(1)}, u32[]{:S(2)}, u32[]{:S(2)}) collective-permute-start(bf16[64,1536]{1,0:T(8,128)(2,1)S(1)} %get-tuple-element.83.refs_7_), channel_id=1, source_target_pairs={{0,2},{2,0},{4,6},{6,4},{8,10},{10,8},{12,14},{14,12},{1,3},{3,1},... | collective-permute-start | bytes 589832 | tf_op jit(solution)/shard_map/ppermute | solution.py:509
  79.8 6.5 %copy-start.14 = (bf16[64,1664]{1,0:T(8,128)(2,1)S(1)}, bf16[64,1664]{1,0:T(8,128)(2,1)}, u32[]{:S(2)}) copy-start(bf16[64,1664]{1,0:T(8,128)(2,1)} %copy-done.13) | copy-start | bytes 638980
  79.8 6.5 %copy-start.16 = (bf16[64,1664]{1,0:T(8,128)(2,1)S(1)}, bf16[64,1664]{1,0:T(8,128)(2,1)}, u32[]{:S(2)}) copy-start(bf16[64,1664]{1,0:T(8,128)(2,1)} %copy-done.15) | copy-start | bytes 638980
  79.8 6.5 %copy-start.17 = (bf16[128,1536]{1,0:T(8,128)(2,1)S(1)}, bf16[128,1536]{1,0:T(8,128)(2,1)}, u32[]{:S(2)}) copy-start(bf16[128,1536]{1,0:T(8,128)(2,1)} %refs_16_.1) | copy-start | bytes 1179652
  79.8 6.5 %copy-start.19 = (bf16[128,1536]{1,0:T(8,128)(2,1)S(1)}, bf16[128,1536]{1,0:T(8,128)(2,1)}, u32[]{:S(2)}) copy-start(bf16[128,1536]{1,0:T(8,128)(2,1)} %cot_ref.1) | copy-start | bytes 1179652
  86.3 3.6 %copy-start.7 = (bf16[1536,384]{1,0:T(8,128)(2,1)}, bf16[1536,384]{1,0:T(8,128)(2,1)S(1)}, u32[]{:S(2)}) copy-start(bf16[1536,384]{1,0:T(8,128)(2,1)S(1)} %get-tuple-element.96.refs_0_) | copy-start | bytes 3538948
  86.3 3.7 %copy-start.9 = (bf16[1536,384]{1,0:T(8,128)(2,1)}, bf16[1536,384]{1,0:T(8,128)(2,1)S(1)}, u32[]{:S(2)}) copy-start(bf16[1536,384]{1,0:T(8,128)(2,1)S(1)} %get-tuple-element.97.refs_1_) | copy-start | bytes 3538948
  86.3 3.7 %copy-start.11 = (bf16[1536,384]{1,0:T(8,128)(2,1)}, bf16[1536,384]{1,0:T(8,128)(2,1)S(1)}, u32[]{:S(2)}) copy-start(bf16[1536,384]{1,0:T(8,128)(2,1)S(1)} %get-tuple-element.98.refs_2_) | copy-start | bytes 3538948
  91.7 22.4 %collective-permute-start.15 = (bf16[3,1536,384]{2,1,0:T(8,128)(2,1)}, bf16[3,1536,384]{2,1,0:T(8,128)(2,1)}, u32[]{:S(2)}, u32[]{:S(2)}) collective-permute-start(bf16[3,1536,384]{2,1,0:T(8,128)(2,1)} %get-tuple-element.95), channel_id=1, source_target_pairs={{0,1},{1,0},{2,3},{3,2},{4,5},{5,4},{6,7},{7,6},{8,9},{9,8},{10,11... | collective-permute-start | bytes 10616840 | tf_op jit(solution)/shard_map/ppermute | solution.py:555
  98.4 6.0 %collective-permute-start.12 = (bf16[64,1536]{1,0:T(8,128)(2,1)S(1)}, bf16[64,1536]{1,0:T(8,128)(2,1)S(1)}, u32[]{:S(2)}, u32[]{:S(2)}) collective-permute-start(bf16[64,1536]{1,0:T(8,128)(2,1)S(1)} %select_convert_fusion), channel_id=1, source_target_pairs={{0,1},{1,0},{2,3},{3,2},{4,5},{5,4},{6,7},{7,6},{8,9},{9,8},{10,11... | collective-permute-start | bytes 589832 | tf_op jit(solution)/shard_map/ppermute | solution.py:427
  98.5 15.7 %copy-start.8 = (bf16[1536,384]{1,0:T(8,128)(2,1)S(1)}, bf16[1536,384]{1,0:T(8,128)(2,1)}, u32[]{:S(2)}) copy-start(bf16[1536,384]{1,0:T(8,128)(2,1)} %copy-done.7) | copy-start | bytes 3538948
  98.5 26.9 %all-to-all-start.1 = ((bf16[4,64,1536]{2,1,0:T(8,128)(2,1)}), bf16[4,64,1536]{2,1,0:T(8,128)(2,1)}, u32[]{:S(2)}, u32[]{:S(2)}) async-start(bf16[4,64,1536]{2,1,0:T(8,128)(2,1)} %bitcast.10), calls=%async_computation.1 | async-start | bytes 1572864 | tf_op jit(solution)/shard_map/all_to_all | solution.py:502
  102.9 11.3 %copy-start.10 = (bf16[1536,384]{1,0:T(8,128)(2,1)S(1)}, bf16[1536,384]{1,0:T(8,128)(2,1)}, u32[]{:S(2)}) copy-start(bf16[1536,384]{1,0:T(8,128)(2,1)} %copy-done.9) | copy-start | bytes 3538948
  102.9 11.3 %copy-start.12 = (bf16[1536,384]{1,0:T(8,128)(2,1)S(1)}, bf16[1536,384]{1,0:T(8,128)(2,1)}, u32[]{:S(2)}) copy-start(bf16[1536,384]{1,0:T(8,128)(2,1)} %copy-done.11) | copy-start | bytes 3538948
  104.5 9.7 %collective-permute-start.13 = (bf16[32,1536]{1,0:T(8,128)(2,1)S(1)}, bf16[32,1536]{1,0:T(8,128)(2,1)S(1)}, u32[]{:S(2)}, u32[]{:S(2)}) collective-permute-start(bf16[32,1536]{1,0:T(8,128)(2,1)S(1)} %select_convert_fusion.1), channel_id=1, source_target_pairs={{0,2},{2,0},{4,6},{6,4},{8,10},{10,8},{12,14},{14,12},{1,3},{3,1},... | collective-permute-start | bytes 294920 | tf_op jit(solution)/shard_map/ppermute | solution.py:427
  105.6 19.8 %collective-permute-start.14 = (bf16[128,1536]{1,0:T(8,128)(2,1)}, bf16[128,1536]{1,0:T(8,128)(2,1)S(1)}, u32[]{:S(2)}, u32[]{:S(2)}) collective-permute-start(bf16[128,1536]{1,0:T(8,128)(2,1)} %merge.1), channel_id=1, source_target_pairs={{0,8},{2,10},{4,12},{6,14},{8,0},{10,2},{12,4},{14,6},{1,9},{3,11}... | collective-permute-start | bytes 1179656 | tf_op jit(solution)/shard_map/ppermute | solution.py:498
  119.7 22.8 %copy-start.20 = (bf16[128,1536]{1,0:T(8,128)(2,1)S(1)}, bf16[128,1536]{1,0:T(8,128)(2,1)}, u32[]{:S(2)}) copy-start(bf16[128,1536]{1,0:T(8,128)(2,1)} %cot_ref.1) | copy-start | bytes 1179652
  119.7 22.8 %copy-start.23 = (bf16[128,1536]{1,0:T(8,128)(2,1)S(1)}, bf16[128,1536]{1,0:T(8,128)(2,1)}, u32[]{:S(2)}) copy-start(bf16[128,1536]{1,0:T(8,128)(2,1)} %tok_ref.1) | copy-start | bytes 1179652
  125.5 3.5 %collective-permute-start.16 = (bf16[32,1536]{1,0:T(8,128)(2,1)S(1)}, bf16[32,1536]{1,0:T(8,128)(2,1)S(1)}, u32[]{:S(2)}, u32[]{:S(2)}) collective-permute-start(bf16[32,1536]{1,0:T(8,128)(2,1)S(1)} %reduce-precision_convert_fusion.1), channel_id=1, source_target_pairs={{0,4},{2,6},{4,0},{6,2},{8,12},{10,14},{12,8},{14,10},{1,5},{3,7},... | collective-permute-start | bytes 294920 | tf_op jit(solution)/shard_map/ppermute | solution.py:427
  129.0 5.2 %collective-permute-start.17 = (bf16[32,1536]{1,0:T(8,128)(2,1)S(1)}, bf16[32,1536]{1,0:T(8,128)(2,1)S(1)}, u32[]{:S(2)}, u32[]{:S(2)}) collective-permute-start(bf16[32,1536]{1,0:T(8,128)(2,1)S(1)} %fusion), channel_id=1, source_target_pairs={{0,8},{2,10},{4,12},{6,14},{8,0},{10,2},{12,4},{14,6},{1,9},{3,11}... | collective-permute-start | bytes 294920 | tf_op jit(solution)/shard_map/ppermute | solution.py:427
  134.3 3.5 %collective-permute-start.18 = (bf16[32,1536]{1,0:T(8,128)(2,1)S(1)}, bf16[32,1536]{1,0:T(8,128)(2,1)S(1)}, u32[]{:S(2)}, u32[]{:S(2)}) collective-permute-start(bf16[32,1536]{1,0:T(8,128)(2,1)S(1)} %reduce-precision_convert_fusion), channel_id=1, source_target_pairs={{0,2},{2,0},{4,6},{6,4},{8,10},{10,8},{12,14},{14,12},{1,3},{3,1},... | collective-permute-start | bytes 294920 | tf_op jit(solution)/shard_map/ppermute | solution.py:427
  137.9 7.4 %collective-permute-start.19 = (bf16[64,1536]{1,0:T(8,128)(2,1)S(1)}, bf16[64,1536]{1,0:T(8,128)(2,1)S(1)}, u32[]{:S(2)}, u32[]{:S(2)}) collective-permute-start(bf16[64,1536]{1,0:T(8,128)(2,1)S(1)} %pad_maximum_fusion.1), channel_id=1, source_target_pairs={{0,1},{1,0},{2,3},{3,2},{4,5},{5,4},{6,7},{7,6},{8,9},{9,8},{10,11... | collective-permute-start | bytes 589832 | tf_op jit(solution)/shard_map/ppermute | solution.py:427
  (6 other events, 7.8 us)
Sparse Core Ops, SparseCore 0:
  9.6 13.3 all-gather.6
  24.5 12.0 all-gather.8
  38.2 12.0 all-gather.10

commit v5 on v4

--- a/solution.py
+++ b/solution.py
@@ -525,7 +525,6 @@
     near, far_meta = lax.optimization_barrier((near, far_meta))
     near = trade(near)
     far_cot = hop(cotangent)
-    far_cot, down = lax.optimization_barrier((far_cot, down))
     far = pack(me, far_meta, [far_tokens], True, True, half, cap)
     far_cots = pack(me, far_meta, [far_cot], False, True, half, cap)
     far = fan(far)

time: 154 us -> 153 us (level)
  local copies, waits for them, and re-layouts: 8.52 us -> 6.76 us
  starting transfers between devices: 37 us -> 35.3 us
    unnamed x58 -> x46, local copies, waits for them, and re-layouts: 6.83 us -> 5.08 us
  transfers between devices with their start and end apart: 25 -> 25, of which waited for: 8 -> 9; matrix products, arithmetic and copies ran while one was open for 0% -> 0% of each run, Pallas kernels for 22% -> 23%
where the time goes in v5:
time: 153 us; the launch traced here: 152 us
  waiting for transfers between devices  55.3 us (36%)
  Pallas kernels  40.3 us (26%)
  starting transfers between devices  35.3 us (23%)
  between operations  14.1 us (9%)
  local copies, waits for them, and re-layouts  6.76 us (4%)
    ppermute x4, waiting for transfers between devices, hop(): return lax.ppermute(array, 'expert', across)  32.3 us
    ppermute x6, waiting for transfers between devices, flip(): lax.ppermute(values.astype(bf16), name, [(i, i ^ bit) for i in range(size)])  19.7 us
    ppermute x9, starting transfers between devices, fan(): lax.ppermute(blocks[k], 'expert', [(e, e ^ k) for e in range(experts)])  8.01 us
    all_to_all x2, starting transfers between devices, trade(): lax.all_to_all(blocks, 'expert', split_axis=0, concat_axis=0, tiled=True,...  7.96 us
    ppermute x4, starting transfers between devices, hop(): return lax.ppermute(array, 'expert', across)  7.28 us
    pallas_call x1, Pallas kernels, whole(): pl.pallas_call(functools.partial(whole_kernel, number), out_shape=backwar...  6.57 us
    pallas_call x1, Pallas kernels, grads(): pl.pallas_call(grads_kernel, out_shape=[jax.ShapeDtypeStruct((width, full...  6.57 us
    ppermute x6, starting transfers between devices, flip(): lax.ppermute(values.astype(bf16), name, [(i, i ^ bit) for i in range(size)])  6.5 us
  transfers between devices with their start and end apart: 25, of which 9 were waited for; matrix products, arithmetic and copies ran while one was open for 0% of the time, Pallas kernels for 23%

profile of v5, /device:TPU:1, one launch (start us, length us, event | category | flops | bytes accessed | tf_op | source)
XLA Modules:
  0.0 152.3 jit_solution(11976248198722671395)
XLA Ops:
  7.2 0.7 all-gather.9.cloned.1.call-update
  8.0 0.7 all-gather.11.cloned.1.call-update
  8.8 3.1 %collective-permute-start = (s32[8,128]{1,0:T(8,128)S(1)}, s32[8,128]{1,0:T(8,128)S(1)}, u32[]{:S(2)}, u32[]{:S(2)}) collective-permute-start(s32[8,128]{1,0:T(8,128)S(1)} %add_add_fusion.meta_ref.refs_14_), channel_id=1, source_target_pairs={{0,8},{2,10},{4,12},{6,14},{8,0},{10,2},{12,4},{14,6},{1,9},{3,11}... | collective-permute-start | bytes 12296 | tf_op jit(solution)/shard_map/ppermute | solution.py:498
  12.1 3.0 %pack.3 = bf16[256,3200]{1,0:T(8,128)(2,1)} custom-call(s32[3]{0:T(128)S(1)} %pad_add_fusion.me_ref, s32[8,128]{1,0:T(8,128)S(1)} %add_add_fusion.meta_ref.refs_14_, bf16[128,1536]{1,0:T(8,128)(2,1)S(1)} %copy-done.19, bf16[128,1536]{1,0:T(8,128)(2,1)} %cot_ref.1), custom_call_target="tpu_custom_call" | custom-call | flops 1000000000 | bytes 4000000 | tf_op jit(solution)/shard_map/pack/pallas_call | solution.py:115
  15.0 3.6 %all-to-all-start = ((bf16[4,64,3200]{2,1,0:T(8,128)(2,1)}), bf16[4,64,3200]{2,1,0:T(8,128)(2,1)S(1)}, u32[]{:S(2)}, u32[]{:S(2)}) async-start(bf16[4,64,3200]{2,1,0:T(8,128)(2,1)} %bitcast.5), calls=%async_computation | async-start | bytes 3276800 | tf_op jit(solution)/shard_map/all_to_all | solution.py:502
  18.7 0.7 all-gather.7.cloned.1.call-update
  19.4 0.3 collective-permute-start.5
  19.7 2.1 %collective-permute-start.1 = (bf16[128,1536]{1,0:T(8,128)(2,1)}, bf16[128,1536]{1,0:T(8,128)(2,1)S(1)}, u32[]{:S(2)}, u32[]{:S(2)}) collective-permute-start(bf16[128,1536]{1,0:T(8,128)(2,1)} %cot_ref.1), channel_id=1, source_target_pairs={{0,8},{2,10},{4,12},{6,14},{8,0},{10,2},{12,4},{14,6},{1,9},{3,11}... | collective-permute-start | bytes 1179656 | tf_op jit(solution)/shard_map/ppermute | solution.py:498
  21.8 22.2 %collective-permute-done.5.refs_0_ = bf16[128,1536]{1,0:T(8,128)(2,1)S(1)} collective-permute-done((bf16[128,1536]{1,0:T(8,128)(2,1)S(1)}, bf16[128,1536]{1,0:T(8,128)(2,1)S(1)}, u32[]{:S(2)}, u32[]{:S(2)}) %collective-permute-start.5) | collective-permute-done | bytes 393248 | tf_op jit(solution)/shard_map/ppermute | solution.py:498
  44.0 1.8 %pack.5 = (bf16[64,1664]{1,0:T(8,128)(2,1)S(1)}, bf16[64,1664]{1,0:T(8,128)(2,1)}, bf16[64,1664]{1,0:T(8,128)(2,1)}, bf16[64,1664]{1,0:T(8,128)(2,1)}) custom-call(s32[3]{0:T(128)S(1)} %pad_add_fusion.me_ref, s32[8,128]{1,0:T(8,128)S(1)} %collective-permute-done.meta_ref, bf16[128,1536]{1,0:T(8,128)(2,1)S(1)} %collective-permute-done.5.refs_0_), custom_call_target="tpu_custom_call" | custom-call | flops 1000000000 | bytes 4000000 | tf_op jit(solution)/shard_map/pack/pallas_call | solution.py:115
  45.8 1.1 collective-permute-start.6
  47.0 1.3 collective-permute-start.7
  48.3 0.2 collective-permute-start.8
  48.5 4.1 %collective-permute-done.1.refs_0_ = bf16[128,1536]{1,0:T(8,128)(2,1)S(1)} collective-permute-done((bf16[128,1536]{1,0:T(8,128)(2,1)}, bf16[128,1536]{1,0:T(8,128)(2,1)S(1)}, u32[]{:S(2)}, u32[]{:S(2)}) %collective-permute-start.1) | collective-permute-done | bytes 393248 | tf_op jit(solution)/shard_map/ppermute | solution.py:498
  52.5 1.7 %pack.4 = (bf16[64,1536]{1,0:T(8,128)(2,1)S(1)}, bf16[64,1536]{1,0:T(8,128)(2,1)}, bf16[64,1536]{1,0:T(8,128)(2,1)}, bf16[64,1536]{1,0:T(8,128)(2,1)S(1)}) custom-call(s32[3]{0:T(128)S(1)} %pad_add_fusion.me_ref, s32[8,128]{1,0:T(8,128)S(1)} %collective-permute-done.meta_ref, bf16[128,1536]{1,0:T(8,128)(2,1)S(1)} %collective-permute-done.1.refs_0_), custom_call_target="tpu_custom_call" | custom-call | flops 1000000000 | bytes 4000000 | tf_op jit(solution)/shard_map/pack/pallas_call | solution.py:115
  54.3 1.1 collective-permute-start.2
  55.4 1.2 collective-permute-start.3
  56.6 0.3 collective-permute-start.4
  57.0 1.7 %copy-done = bf16[1,1536,768]{2,1,0:T(8,128)(2,1)S(1)} copy-done((bf16[1,1536,768]{2,1,0:T(8,128)(2,1)S(1)}, bf16[1,1536,768]{2,1,0:T(8,128)(2,1)}, u32[]{:S(2)}) %copy-start) | copy-done | bytes 2359320
  58.6 1.7 %copy-done.2 = bf16[1,1536,768]{2,1,0:T(8,128)(2,1)S(1)} copy-done((bf16[1,1536,768]{2,1,0:T(8,128)(2,1)S(1)}, bf16[1,1536,768]{2,1,0:T(8,128)(2,1)}, u32[]{:S(2)}) %copy-start.2) | copy-done | bytes 2359320
  60.3 1.7 %copy-done.5 = bf16[1,1536,768]{2,1,0:T(8,128)(2,1)S(1)} copy-done((bf16[1,1536,768]{2,1,0:T(8,128)(2,1)S(1)}, bf16[1,1536,768]{2,1,0:T(8,128)(2,1)}, u32[]{:S(2)}) %copy-start.5) | copy-done | bytes 2359320
  61.9 6.6 %expert_whole.1 = (bf16[256,1536]{1,0:T(8,128)(2,1)}, bf16[256,5376]{1,0:T(8,128)(2,1)S(1)}, f32[256,128]{1,0:T(8,128)S(1)}) custom-call(s32[3]{0:T(128)S(1)} %pad_add_fusion.me_ref, bf16[256,3200]{1,0:T(8,128)(2,1)S(1)} %bitcast.20, f32[3,32,1536]{2,1,0:T(8,128)S(1)} %copy-done.4, bf16[8,1536]{1,0:T(8,128)(2,1)S(1)} %copy-done.18, ...), custom_call_target="tpu_custom_call" | custom-call | flops 3019898880 | bytes 11173888 | tf_op jit(solution)/shard_map/expert_whole/pallas_call | solution.py:271
  68.6 3.0 %expert_in.1 = (bf16[256,1536]{1,0:T(8,128)(2,1)S(1)}, f32[256,128]{1,0:T(8,128)S(1)}, f32[256,768]{1,0:T(8,128)S(1)}, f32[256,768]{1,0:T(8,128)S(1)}, bf16[256,768]{1,0:T(8,128)(2,1)S(1)}) custom-call(s32[3]{0:T(128)S(1)} %pad_add_fusion.me_ref, bf16[64,1664]{1,0:T(8,128)(2,1)S(1)} %get-tuple-element.69.refs_0_.refs_1_, ...), custom_call_target="tpu_custom_call" | custom-call | flops 1207959552 | bytes 7790592 | tf_op jit(solution)/shard_map/expert_in/pallas_call | solution.py:205
  71.6 1.3 collective-permute-done.4.refs_3_
  72.9 3.6 %expert_back.1 = (bf16[64,1536]{1,0:T(8,128)(2,1)S(1)}, bf16[64,1536]{1,0:T(8,128)(2,1)S(1)}, bf16[64,1536]{1,0:T(8,128)(2,1)S(1)}, bf16[64,1536]{1,0:T(8,128)(2...) custom-call(s32[3]{0:T(128)S(1)} %pad_add_fusion.me_ref, bf16[64,1536]{1,0:T(8,128)(2,1)S(1)} %get-tuple-element.59.refs_0_, ...), custom_call_target="tpu_custom_call" | custom-call | flops 1811939328 | bytes 11173888 | tf_op jit(solution)/shard_map/expert_back/pallas_call | solution.py:244
  76.5 0.3 collective-permute-start.10
  76.8 1.2 collective-permute-start.11
  78.1 1.2 collective-permute-start.9
  79.3 6.6 %weight_grads.1 = (bf16[1536,384]{1,0:T(8,128)(2,1)S(1)}, bf16[1536,384]{1,0:T(8,128)(2,1)S(1)}, bf16[1536,384]{1,0:T(8,128)(2,1)S(1)}, bf16[3,1536,384]{2,1,0:T(8,128)(2,1)}) custom-call(s32[3]{0:T(128)S(1)} %pad_add_fusion.me_ref, bf16[256,5376]{1,0:T(8,128)(2,1)S(1)} %get-tuple-element.83.refs_10_.near_ref, ...), custom_call_target="tpu_custom_call" | custom-call | flops 1000000 | bytes 10000 | tf_op jit(solution)/shard_map/weight_grads/pallas_call | solution.py:364
  85.9 4.0 %table_sums.1 = f32[128,1536]{1,0:T(8,128)S(1)} custom-call(s32[3]{0:T(128)S(1)} %pad_add_fusion.me_ref, bf16[256,3200]{1,0:T(8,128)(2,1)S(1)} %bitcast.21, bf16[64,1664]{1,0:T(8,128)(2,1)S(1)} %get-tuple-element.69.refs_0_.refs_1_, bf16[64,1664]{1,0:T(8,128)(2,1)S(1)} %collective-permute-done.6.refs_1_.refs_2_, bf16[64,1664]{1,0:T(8,128)(2,1)S(1)} %copy-done.14, ...), custom_call_target="tpu_custom_call" | custom-call | flops 1000000 | bytes 10000 | tf_op jit(solution)/shard_map/table_sums/pallas_call | solution.py:335
  89.9 1.7 %merge.1 = bf16[128,1536]{1,0:T(8,128)(2,1)} custom-call(s32[3]{0:T(128)S(1)} %pad_add_fusion.me_ref, s32[8,128]{1,0:T(8,128)S(1)} %collective-permute-done.meta_ref, bf16[64,1536]{1,0:T(8,128)(2,1)S(1)} %get-tuple-element.78.refs_0_.refs_6_, bf16[64,1536]{1,0:T(8,128)(2,1)S(1)} %collective-permute-done.9.refs_1_, ...), custom_call_target="tpu_custom_call" | custom-call | flops 1000000000 | bytes 2000000 | tf_op jit(solution)/shard_map/merge/pallas_call | solution.py:384
  91.6 5.5 %collective-permute-start.15 = (bf16[3,1536,384]{2,1,0:T(8,128)(2,1)}, bf16[3,1536,384]{2,1,0:T(8,128)(2,1)}, u32[]{:S(2)}, u32[]{:S(2)}) collective-permute-start(bf16[3,1536,384]{2,1,0:T(8,128)(2,1)} %get-tuple-element.91), channel_id=1, source_target_pairs={{0,1},{1,0},{2,3},{3,2},{4,5},{5,4},{6,7},{7,6},{8,9},{9,8},{10,11... | collective-permute-start | bytes 10616840 | tf_op jit(solution)/shard_map/ppermute | solution.py:554
  97.2 4.4 %all-to-all-start.1 = ((bf16[4,64,1536]{2,1,0:T(8,128)(2,1)}), bf16[4,64,1536]{2,1,0:T(8,128)(2,1)}, u32[]{:S(2)}, u32[]{:S(2)}) async-start(bf16[4,64,1536]{2,1,0:T(8,128)(2,1)} %bitcast.10), calls=%async_computation.1 | async-start | bytes 1572864 | tf_op jit(solution)/shard_map/all_to_all | solution.py:502
  101.6 1.5 collective-permute-done.12
  103.2 1.2 collective-permute-start.13
  104.4 1.7 %collective-permute-start.14 = (bf16[128,1536]{1,0:T(8,128)(2,1)}, bf16[128,1536]{1,0:T(8,128)(2,1)S(1)}, u32[]{:S(2)}, u32[]{:S(2)}) collective-permute-start(bf16[128,1536]{1,0:T(8,128)(2,1)} %merge.1), channel_id=1, source_target_pairs={{0,8},{2,10},{4,12},{6,14},{8,0},{10,2},{12,4},{14,6},{1,9},{3,11}... | collective-permute-start | bytes 1179656 | tf_op jit(solution)/shard_map/ppermute | solution.py:498
  106.1 6.6 %collective-permute-done.13 = bf16[32,1536]{1,0:T(8,128)(2,1)S(1)} collective-permute-done((bf16[32,1536]{1,0:T(8,128)(2,1)S(1)}, bf16[32,1536]{1,0:T(8,128)(2,1)S(1)}, u32[]{:S(2)}, u32[]{:S(2)}) %collective-permute-start.13) | collective-permute-done | bytes 98336 | tf_op jit(solution)/shard_map/ppermute | solution.py:427
  112.8 5.5 %add.34 = (bf16[1,1536,384]{2,1,0:T(8,128)(2,1)}, bf16[1,1536,384]{2,1,0:T(8,128)(2,1)}, bf16[1,1536,384]{2,1,0:T(8,128)(2,1)}) custom-call(bf16[3,1536,384]{2,1,0:T(8,128)(2,1)} %collective-permute-done.15.other_ref, bf16[1536,384]{1,0:T(8,128)(2,1)S(1)} %copy-done.8, bf16[1536,384]{1,0:T(8,128)(2,1)S(1)} %copy-done.10, bf16[1536,384]{1,0:T(8,128)(2,1)S(1)} %copy-done.12), custom_call_target="tpu_custom_call" | custom-call | flops 1000000 | bytes 10000 | tf_op jit(solution)/shard_map/add/pallas_call | solution.py:465
  118.3 6.0 %collective-permute-done.14.far_ref = bf16[128,1536]{1,0:T(8,128)(2,1)S(1)} collective-permute-done((bf16[128,1536]{1,0:T(8,128)(2,1)}, bf16[128,1536]{1,0:T(8,128)(2,1)S(1)}, u32[]{:S(2)}, u32[]{:S(2)}) %collective-permute-start.14) | collective-permute-done | bytes 393248 | tf_op jit(solution)/shard_map/ppermute | solution.py:498
  124.3 3.5 %collective-permute-done.16 = bf16[32,1536]{1,0:T(8,128)(2,1)S(1)} collective-permute-done((bf16[32,1536]{1,0:T(8,128)(2,1)S(1)}, bf16[32,1536]{1,0:T(8,128)(2,1)S(1)}, u32[]{:S(2)}, u32[]{:S(2)}) %collective-permute-start.16) | collective-permute-done | bytes 98336 | tf_op jit(solution)/shard_map/ppermute | solution.py:427
  127.8 0.2 collective-permute-start.17
  128.1 5.0 %collective-permute-done.17 = bf16[32,1536]{1,0:T(8,128)(2,1)S(1)} collective-permute-done((bf16[32,1536]{1,0:T(8,128)(2,1)S(1)}, bf16[32,1536]{1,0:T(8,128)(2,1)S(1)}, u32[]{:S(2)}, u32[]{:S(2)}) %collective-permute-start.17) | collective-permute-done | bytes 98336 | tf_op jit(solution)/shard_map/ppermute | solution.py:427
  133.1 0.4 collective-permute-start.18
  133.5 3.2 %collective-permute-done.18 = bf16[32,1536]{1,0:T(8,128)(2,1)S(1)} collective-permute-done((bf16[32,1536]{1,0:T(8,128)(2,1)S(1)}, bf16[32,1536]{1,0:T(8,128)(2,1)S(1)}, u32[]{:S(2)}, u32[]{:S(2)}) %collective-permute-start.18) | collective-permute-done | bytes 98336 | tf_op jit(solution)/shard_map/ppermute | solution.py:427
  136.7 4.5 %collective-permute-start.19 = (bf16[64,1536]{1,0:T(8,128)(2,1)S(1)}, bf16[64,1536]{1,0:T(8,128)(2,1)S(1)}, u32[]{:S(2)}, u32[]{:S(2)}) collective-permute-start(bf16[64,1536]{1,0:T(8,128)(2,1)S(1)} %pad_maximum_fusion.1), channel_id=1, source_target_pairs={{0,1},{1,0},{2,3},{3,2},{4,5},{5,4},{6,7},{7,6},{8,9},{9,8},{10,11... | collective-permute-start | bytes 589832 | tf_op jit(solution)/shard_map/ppermute | solution.py:427
  141.3 2.9 %final.1 = bf16[128,1536]{1,0:T(8,128)(2,1)} custom-call(s32[3]{0:T(128)S(1)} %pad_add_fusion.me_ref, s32[8,128]{1,0:T(8,128)S(1)} %add_add_fusion.meta_ref.refs_14_, s32[128,1]{1,0:T(8,128)S(1)} %copy.16.stamp_ref, bf16[128,1536]{1,0:T(8,128)(2,1)S(1)} %copy-done.20, bf16[128,1536]{1,0:T(8,128)(2,1)} %cot_ref.1, f32[3,32,1536]{2,1,0:T(8,128)S(1)} %copy-done.4, ...), custom_call_target="tpu_custom_call" | custom-call | flops 1000000000 | bytes 4000000 | tf_op jit(solution)/shard_map/final/pallas_call | solution.py:411
  144.3 0.9 slice.27
  145.2 0.6 slice.26
  (80 shorter events, 1.1 us)
Async XLA Ops:
  7.2 1.6 %copy-start.22 = (s32[128,2]{0,1:T(2,128)S(1)}, s32[128,2]{0,1:T(2,128)}, u32[]{:S(2)}) copy-start(s32[128,2]{0,1:T(2,128)} %param.14) | copy-start | bytes 3076
  7.2 1.6 %copy-start.21 = (s32[128]{0:T(128)S(1)}, s32[128]{0:T(128)}, u32[]{:S(2)}) copy-start(s32[128]{0:T(128)} %param.13) | copy-start | bytes 1540
  7.2 4.9 %copy-start.19 = (bf16[128,1536]{1,0:T(8,128)(2,1)S(1)}, bf16[128,1536]{1,0:T(8,128)(2,1)}, u32[]{:S(2)}) copy-start(bf16[128,1536]{1,0:T(8,128)(2,1)} %tok_ref.1) | copy-start | bytes 1179652
  7.2 49.7 %all-gather.9.cloned.1.call-start = ((), (), s32[]{:S(2)}) async-start(), calls=%async_computation.3 | async-start | bytes 3538944 | tf_op jit(solution)/shard_map/all_gather | solution.py:520
  7.9 49.0 %all-gather.11.cloned.1.call-start = ((), (), s32[]{:S(2)}) async-start(), calls=%async_computation.4 | async-start | bytes 3538944 | tf_op jit(solution)/shard_map/all_gather | solution.py:520
  8.8 6.2 %collective-permute-start = (s32[8,128]{1,0:T(8,128)S(1)}, s32[8,128]{1,0:T(8,128)S(1)}, u32[]{:S(2)}, u32[]{:S(2)}) collective-permute-start(s32[8,128]{1,0:T(8,128)S(1)} %add_add_fusion.meta_ref.refs_14_), channel_id=1, source_target_pairs={{0,8},{2,10},{4,12},{6,14},{8,0},{10,2},{12,4},{14,6},{1,9},{3,11}... | collective-permute-start | bytes 12296 | tf_op jit(solution)/shard_map/ppermute | solution.py:498
  15.0 41.6 %all-to-all-start = ((bf16[4,64,3200]{2,1,0:T(8,128)(2,1)}), bf16[4,64,3200]{2,1,0:T(8,128)(2,1)S(1)}, u32[]{:S(2)}, u32[]{:S(2)}) async-start(bf16[4,64,3200]{2,1,0:T(8,128)(2,1)} %bitcast.5), calls=%async_computation | async-start | bytes 3276800 | tf_op jit(solution)/shard_map/all_to_all | solution.py:502
  18.6 38.3 %all-gather.7.cloned.1.call-start = ((), (), s32[]{:S(2)}) async-start(), calls=%async_computation.2 | async-start | bytes 3538944 | tf_op jit(solution)/shard_map/all_gather | solution.py:520
  19.4 24.6 %collective-permute-start.5 = (bf16[128,1536]{1,0:T(8,128)(2,1)S(1)}, bf16[128,1536]{1,0:T(8,128)(2,1)S(1)}, u32[]{:S(2)}, u32[]{:S(2)}) collective-permute-start(bf16[128,1536]{1,0:T(8,128)(2,1)S(1)} %copy-done.19), channel_id=1, source_target_pairs={{0,8},{2,10},{4,12},{6,14},{8,0},{10,2},{12,4},{14,6},{1,9},{3,11}... | collective-permute-start | bytes 1179656 | tf_op jit(solution)/shard_map/ppermute | solution.py:498
  19.7 32.8 %collective-permute-start.1 = (bf16[128,1536]{1,0:T(8,128)(2,1)}, bf16[128,1536]{1,0:T(8,128)(2,1)S(1)}, u32[]{:S(2)}, u32[]{:S(2)}) collective-permute-start(bf16[128,1536]{1,0:T(8,128)(2,1)} %cot_ref.1), channel_id=1, source_target_pairs={{0,8},{2,10},{4,12},{6,14},{8,0},{10,2},{12,4},{14,6},{1,9},{3,11}... | collective-permute-start | bytes 1179656 | tf_op jit(solution)/shard_map/ppermute | solution.py:498
  45.8 10.8 %collective-permute-start.6 = (bf16[64,1664]{1,0:T(8,128)(2,1)}, bf16[64,1664]{1,0:T(8,128)(2,1)S(1)}, u32[]{:S(2)}, u32[]{:S(2)}) collective-permute-start(bf16[64,1664]{1,0:T(8,128)(2,1)} %get-tuple-element.66), channel_id=1, source_target_pairs={{0,2},{2,0},{4,6},{6,4},{8,10},{10,8},{12,14},{14,12},{1,3},{3,1},... | collective-permute-start | bytes 638984 | tf_op jit(solution)/shard_map/ppermute | solution.py:509
  47.0 21.6 %collective-permute-start.7 = (bf16[64,1664]{1,0:T(8,128)(2,1)}, bf16[64,1664]{1,0:T(8,128)(2,1)S(1)}, u32[]{:S(2)}, u32[]{:S(2)}) collective-permute-start(bf16[64,1664]{1,0:T(8,128)(2,1)} %get-tuple-element.67), channel_id=1, source_target_pairs={{0,4},{2,6},{4,0},{6,2},{8,12},{10,14},{12,8},{14,10},{1,5},{3,7},... | collective-permute-start | bytes 638984 | tf_op jit(solution)/shard_map/ppermute | solution.py:509
  48.3 8.6 %copy-start.4 = (f32[3,32,1536]{2,1,0:T(8,128)S(1)}, f32[3,32,1536]{2,1,0:T(8,128)}, u32[]{:S(2)}) copy-start(f32[3,32,1536]{2,1,0:T(8,128)} %table_ref.1) | copy-start | bytes 1769476
  48.3 8.6 %copy-start.18 = (bf16[8,1536]{1,0:T(8,128)(2,1)S(1)}, bf16[8,1536]{1,0:T(8,128)(2,1)}, u32[]{:S(2)}) copy-start(bf16[8,1536]{1,0:T(8,128)(2,1)} %refs_5_.3) | copy-start | bytes 73732
  48.3 20.2 %collective-permute-start.8 = (bf16[64,1664]{1,0:T(8,128)(2,1)}, bf16[64,1664]{1,0:T(8,128)(2,1)S(1)}, u32[]{:S(2)}, u32[]{:S(2)}) collective-permute-start(bf16[64,1664]{1,0:T(8,128)(2,1)} %get-tuple-element.68), channel_id=1, source_target_pairs={{0,6},{2,4},{4,2},{6,0},{8,14},{10,12},{12,10},{14,8},{1,7},{3,5},... | collective-permute-start | bytes 638984 | tf_op jit(solution)/shard_map/ppermute | solution.py:509
  54.3 17.3 %collective-permute-start.2 = (bf16[64,1536]{1,0:T(8,128)(2,1)}, bf16[64,1536]{1,0:T(8,128)(2,1)}, u32[]{:S(2)}, u32[]{:S(2)}) collective-permute-start(bf16[64,1536]{1,0:T(8,128)(2,1)} %get-tuple-element.60), channel_id=1, source_target_pairs={{0,2},{2,0},{4,6},{6,4},{8,10},{10,8},{12,14},{14,12},{1,3},{3,1},... | collective-permute-start | bytes 589832 | tf_op jit(solution)/shard_map/ppermute | solution.py:509
  55.4 16.2 %collective-permute-start.3 = (bf16[64,1536]{1,0:T(8,128)(2,1)}, bf16[64,1536]{1,0:T(8,128)(2,1)}, u32[]{:S(2)}, u32[]{:S(2)}) collective-permute-start(bf16[64,1536]{1,0:T(8,128)(2,1)} %get-tuple-element.61), channel_id=1, source_target_pairs={{0,4},{2,6},{4,0},{6,2},{8,12},{10,14},{12,8},{14,10},{1,5},{3,7},... | collective-permute-start | bytes 589832 | tf_op jit(solution)/shard_map/ppermute | solution.py:509
  56.6 16.3 %collective-permute-start.4 = (bf16[64,1536]{1,0:T(8,128)(2,1)S(1)}, bf16[64,1536]{1,0:T(8,128)(2,1)}, u32[]{:S(2)}, u32[]{:S(2)}) collective-permute-start(bf16[64,1536]{1,0:T(8,128)(2,1)S(1)} %get-tuple-element.62), channel_id=1, source_target_pairs={{0,6},{2,4},{4,2},{6,0},{8,14},{10,12},{12,10},{14,8},{1,7},{3,5},... | collective-permute-start | bytes 589832 | tf_op jit(solution)/shard_map/ppermute | solution.py:509
  56.9 1.7 %copy-start = (bf16[1,1536,768]{2,1,0:T(8,128)(2,1)S(1)}, bf16[1,1536,768]{2,1,0:T(8,128)(2,1)}, u32[]{:S(2)}) copy-start(bf16[1,1536,768]{2,1,0:T(8,128)(2,1)} %all-gather.9.cloned.1.call-done) | copy-start | bytes 7077892
  58.6 1.7 %copy-start.2 = (bf16[1,1536,768]{2,1,0:T(8,128)(2,1)S(1)}, bf16[1,1536,768]{2,1,0:T(8,128)(2,1)}, u32[]{:S(2)}) copy-start(bf16[1,1536,768]{2,1,0:T(8,128)(2,1)} %all-gather.11.cloned.1.call-done) | copy-start | bytes 7077892
  60.3 1.7 %copy-start.5 = (bf16[1,1536,768]{2,1,0:T(8,128)(2,1)S(1)}, bf16[1,1536,768]{2,1,0:T(8,128)(2,1)}, u32[]{:S(2)}) copy-start(bf16[1,1536,768]{2,1,0:T(8,128)(2,1)} %all-gather.7.cloned.1.call-done) | copy-start | bytes 7077892
  61.9 6.6 %copy-start.1 = (bf16[1,1536,768]{2,1,0:T(8,128)(2,1)S(1)}, bf16[1,1536,768]{2,1,0:T(8,128)(2,1)}, u32[]{:S(2)}) copy-start(bf16[1,1536,768]{2,1,0:T(8,128)(2,1)} %all-gather.9.cloned.1.call-done) | copy-start | bytes 7077892
  68.5 3.0 %copy-start.13 = (bf16[64,1664]{1,0:T(8,128)(2,1)}, bf16[64,1664]{1,0:T(8,128)(2,1)S(1)}, u32[]{:S(2)}) copy-start(bf16[64,1664]{1,0:T(8,128)(2,1)S(1)} %collective-permute-done.7.refs_2_.refs_3_) | copy-start | bytes 638980
  68.5 3.0 %copy-start.15 = (bf16[64,1664]{1,0:T(8,128)(2,1)}, bf16[64,1664]{1,0:T(8,128)(2,1)S(1)}, u32[]{:S(2)}) copy-start(bf16[64,1664]{1,0:T(8,128)(2,1)S(1)} %collective-permute-done.8.refs_3_.refs_4_) | copy-start | bytes 638980
  68.6 4.4 %copy-start.3 = (bf16[1,1536,768]{2,1,0:T(8,128)(2,1)S(1)}, bf16[1,1536,768]{2,1,0:T(8,128)(2,1)}, u32[]{:S(2)}) copy-start(bf16[1,1536,768]{2,1,0:T(8,128)(2,1)} %all-gather.11.cloned.1.call-done) | copy-start | bytes 7077892
  68.6 4.4 %copy-start.6 = (bf16[1,1536,768]{2,1,0:T(8,128)(2,1)S(1)}, bf16[1,1536,768]{2,1,0:T(8,128)(2,1)}, u32[]{:S(2)}) copy-start(bf16[1,1536,768]{2,1,0:T(8,128)(2,1)} %all-gather.7.cloned.1.call-done) | copy-start | bytes 7077892
  76.5 13.3 %collective-permute-start.10 = (bf16[64,1536]{1,0:T(8,128)(2,1)S(1)}, bf16[64,1536]{1,0:T(8,128)(2,1)S(1)}, u32[]{:S(2)}, u32[]{:S(2)}) collective-permute-start(bf16[64,1536]{1,0:T(8,128)(2,1)S(1)} %get-tuple-element.80.refs_8_), channel_id=1, source_target_pairs={{0,4},{2,6},{4,0},{6,2},{8,12},{10,14},{12,8},{14,10},{1,5},{3,7},... | collective-permute-start | bytes 589832 | tf_op jit(solution)/shard_map/ppermute | solution.py:509
  76.8 13.0 %collective-permute-start.11 = (bf16[64,1536]{1,0:T(8,128)(2,1)S(1)}, bf16[64,1536]{1,0:T(8,128)(2,1)S(1)}, u32[]{:S(2)}, u32[]{:S(2)}) collective-permute-start(bf16[64,1536]{1,0:T(8,128)(2,1)S(1)} %get-tuple-element.81.refs_9_), channel_id=1, source_target_pairs={{0,6},{2,4},{4,2},{6,0},{8,14},{10,12},{12,10},{14,8},{1,7},{3,5},... | collective-permute-start | bytes 589832 | tf_op jit(solution)/shard_map/ppermute | solution.py:509
  78.1 11.8 %collective-permute-start.9 = (bf16[64,1536]{1,0:T(8,128)(2,1)S(1)}, bf16[64,1536]{1,0:T(8,128)(2,1)S(1)}, u32[]{:S(2)}, u32[]{:S(2)}) collective-permute-start(bf16[64,1536]{1,0:T(8,128)(2,1)S(1)} %get-tuple-element.79.refs_7_), channel_id=1, source_target_pairs={{0,2},{2,0},{4,6},{6,4},{8,10},{10,8},{12,14},{14,12},{1,3},{3,1},... | collective-permute-start | bytes 589832 | tf_op jit(solution)/shard_map/ppermute | solution.py:509
  79.2 6.6 %copy-start.14 = (bf16[64,1664]{1,0:T(8,128)(2,1)S(1)}, bf16[64,1664]{1,0:T(8,128)(2,1)}, u32[]{:S(2)}) copy-start(bf16[64,1664]{1,0:T(8,128)(2,1)} %copy-done.13) | copy-start | bytes 638980
  79.2 6.6 %copy-start.16 = (bf16[64,1664]{1,0:T(8,128)(2,1)S(1)}, bf16[64,1664]{1,0:T(8,128)(2,1)}, u32[]{:S(2)}) copy-start(bf16[64,1664]{1,0:T(8,128)(2,1)} %copy-done.15) | copy-start | bytes 638980
  79.3 6.6 %copy-start.17 = (bf16[128,1536]{1,0:T(8,128)(2,1)S(1)}, bf16[128,1536]{1,0:T(8,128)(2,1)}, u32[]{:S(2)}) copy-start(bf16[128,1536]{1,0:T(8,128)(2,1)} %refs_16_.1) | copy-start | bytes 1179652
  85.8 4.0 %copy-start.7 = (bf16[1536,384]{1,0:T(8,128)(2,1)}, bf16[1536,384]{1,0:T(8,128)(2,1)S(1)}, u32[]{:S(2)}) copy-start(bf16[1536,384]{1,0:T(8,128)(2,1)S(1)} %get-tuple-element.92.refs_0_) | copy-start | bytes 3538948
  85.8 4.0 %copy-start.9 = (bf16[1536,384]{1,0:T(8,128)(2,1)}, bf16[1536,384]{1,0:T(8,128)(2,1)S(1)}, u32[]{:S(2)}) copy-start(bf16[1536,384]{1,0:T(8,128)(2,1)S(1)} %get-tuple-element.93.refs_1_) | copy-start | bytes 3538948
  85.8 4.0 %copy-start.11 = (bf16[1536,384]{1,0:T(8,128)(2,1)}, bf16[1536,384]{1,0:T(8,128)(2,1)S(1)}, u32[]{:S(2)}) copy-start(bf16[1536,384]{1,0:T(8,128)(2,1)S(1)} %get-tuple-element.94.refs_2_) | copy-start | bytes 3538948
  91.6 21.1 %collective-permute-start.15 = (bf16[3,1536,384]{2,1,0:T(8,128)(2,1)}, bf16[3,1536,384]{2,1,0:T(8,128)(2,1)}, u32[]{:S(2)}, u32[]{:S(2)}) collective-permute-start(bf16[3,1536,384]{2,1,0:T(8,128)(2,1)} %get-tuple-element.91), channel_id=1, source_target_pairs={{0,1},{1,0},{2,3},{3,2},{4,5},{5,4},{6,7},{7,6},{8,9},{9,8},{10,11... | collective-permute-start | bytes 10616840 | tf_op jit(solution)/shard_map/ppermute | solution.py:554
  97.1 6.0 %collective-permute-start.12 = (bf16[64,1536]{1,0:T(8,128)(2,1)S(1)}, bf16[64,1536]{1,0:T(8,128)(2,1)S(1)}, u32[]{:S(2)}, u32[]{:S(2)}) collective-permute-start(bf16[64,1536]{1,0:T(8,128)(2,1)S(1)} %select_convert_fusion), channel_id=1, source_target_pairs={{0,1},{1,0},{2,3},{3,2},{4,5},{5,4},{6,7},{7,6},{8,9},{9,8},{10,11... | collective-permute-start | bytes 589832 | tf_op jit(solution)/shard_map/ppermute | solution.py:427
  97.2 15.6 %copy-start.8 = (bf16[1536,384]{1,0:T(8,128)(2,1)S(1)}, bf16[1536,384]{1,0:T(8,128)(2,1)}, u32[]{:S(2)}) copy-start(bf16[1536,384]{1,0:T(8,128)(2,1)} %copy-done.7) | copy-start | bytes 3538948
  97.2 27.0 %all-to-all-start.1 = ((bf16[4,64,1536]{2,1,0:T(8,128)(2,1)}), bf16[4,64,1536]{2,1,0:T(8,128)(2,1)}, u32[]{:S(2)}, u32[]{:S(2)}) async-start(bf16[4,64,1536]{2,1,0:T(8,128)(2,1)} %bitcast.10), calls=%async_computation.1 | async-start | bytes 1572864 | tf_op jit(solution)/shard_map/all_to_all | solution.py:502
  101.6 11.2 %copy-start.10 = (bf16[1536,384]{1,0:T(8,128)(2,1)S(1)}, bf16[1536,384]{1,0:T(8,128)(2,1)}, u32[]{:S(2)}) copy-start(bf16[1536,384]{1,0:T(8,128)(2,1)} %copy-done.9) | copy-start | bytes 3538948
  101.6 11.2 %copy-start.12 = (bf16[1536,384]{1,0:T(8,128)(2,1)S(1)}, bf16[1536,384]{1,0:T(8,128)(2,1)}, u32[]{:S(2)}) copy-start(bf16[1536,384]{1,0:T(8,128)(2,1)} %copy-done.11) | copy-start | bytes 3538948
  103.2 9.6 %collective-permute-start.13 = (bf16[32,1536]{1,0:T(8,128)(2,1)S(1)}, bf16[32,1536]{1,0:T(8,128)(2,1)S(1)}, u32[]{:S(2)}, u32[]{:S(2)}) collective-permute-start(bf16[32,1536]{1,0:T(8,128)(2,1)S(1)} %select_convert_fusion.1), channel_id=1, source_target_pairs={{0,2},{2,0},{4,6},{6,4},{8,10},{10,8},{12,14},{14,12},{1,3},{3,1},... | collective-permute-start | bytes 294920 | tf_op jit(solution)/shard_map/ppermute | solution.py:427
  104.4 19.8 %collective-permute-start.14 = (bf16[128,1536]{1,0:T(8,128)(2,1)}, bf16[128,1536]{1,0:T(8,128)(2,1)S(1)}, u32[]{:S(2)}, u32[]{:S(2)}) collective-permute-start(bf16[128,1536]{1,0:T(8,128)(2,1)} %merge.1), channel_id=1, source_target_pairs={{0,8},{2,10},{4,12},{6,14},{8,0},{10,2},{12,4},{14,6},{1,9},{3,11}... | collective-permute-start | bytes 1179656 | tf_op jit(solution)/shard_map/ppermute | solution.py:498
  118.3 23.0 %copy-start.20 = (bf16[128,1536]{1,0:T(8,128)(2,1)S(1)}, bf16[128,1536]{1,0:T(8,128)(2,1)}, u32[]{:S(2)}) copy-start(bf16[128,1536]{1,0:T(8,128)(2,1)} %tok_ref.1) | copy-start | bytes 1179652
  124.3 3.5 %collective-permute-start.16 = (bf16[32,1536]{1,0:T(8,128)(2,1)S(1)}, bf16[32,1536]{1,0:T(8,128)(2,1)S(1)}, u32[]{:S(2)}, u32[]{:S(2)}) collective-permute-start(bf16[32,1536]{1,0:T(8,128)(2,1)S(1)} %reduce-precision_convert_fusion.1), channel_id=1, source_target_pairs={{0,4},{2,6},{4,0},{6,2},{8,12},{10,14},{12,8},{14,10},{1,5},{3,7},... | collective-permute-start | bytes 294920 | tf_op jit(solution)/shard_map/ppermute | solution.py:427
  127.8 5.2 %collective-permute-start.17 = (bf16[32,1536]{1,0:T(8,128)(2,1)S(1)}, bf16[32,1536]{1,0:T(8,128)(2,1)S(1)}, u32[]{:S(2)}, u32[]{:S(2)}) collective-permute-start(bf16[32,1536]{1,0:T(8,128)(2,1)S(1)} %fusion), channel_id=1, source_target_pairs={{0,8},{2,10},{4,12},{6,14},{8,0},{10,2},{12,4},{14,6},{1,9},{3,11}... | collective-permute-start | bytes 294920 | tf_op jit(solution)/shard_map/ppermute | solution.py:427
  133.1 3.5 %collective-permute-start.18 = (bf16[32,1536]{1,0:T(8,128)(2,1)S(1)}, bf16[32,1536]{1,0:T(8,128)(2,1)S(1)}, u32[]{:S(2)}, u32[]{:S(2)}) collective-permute-start(bf16[32,1536]{1,0:T(8,128)(2,1)S(1)} %reduce-precision_convert_fusion), channel_id=1, source_target_pairs={{0,2},{2,0},{4,6},{6,4},{8,10},{10,8},{12,14},{14,12},{1,3},{3,1},... | collective-permute-start | bytes 294920 | tf_op jit(solution)/shard_map/ppermute | solution.py:427
  136.7 7.5 %collective-permute-start.19 = (bf16[64,1536]{1,0:T(8,128)(2,1)S(1)}, bf16[64,1536]{1,0:T(8,128)(2,1)S(1)}, u32[]{:S(2)}, u32[]{:S(2)}) collective-permute-start(bf16[64,1536]{1,0:T(8,128)(2,1)S(1)} %pad_maximum_fusion.1), channel_id=1, source_target_pairs={{0,1},{1,0},{2,3},{3,2},{4,5},{5,4},{6,7},{7,6},{8,9},{9,8},{10,11... | collective-permute-start | bytes 589832 | tf_op jit(solution)/shard_map/ppermute | solution.py:427
Sparse Core Ops, SparseCore 0:
  9.6 13.3 all-gather.8
  24.5 12.0 all-gather.10
  38.2 12.0 all-gather.6

commit v6 on v5

--- a/solution.py
+++ b/solution.py
@@ -546,9 +546,8 @@
     )
     mine, other = grads(me, lates, *gate.shape)
     merged = merge(me, far_meta, far_back, cap)
-    merged, table, other, near_back = lax.optimization_barrier(
-        (merged, table, other, near_backs[0])
-    )
+    merged, table, other = lax.optimization_barrier((merged, table, other))
+    near_back = near_backs[0]
     far_grad = hop(merged)
     near_back = trade(near_back)
     other = lax.ppermute(other, "dp", [(i, dp_axis - 1 - i) for i in range(dp_axis)])

time: 153 us -> 153 us (level)
  no operation moved by 1% of the time
where the time goes in v6:
time: 153 us; the launch traced here: 152 us
  waiting for transfers between devices  55.3 us (36%)
  Pallas kernels  40.3 us (26%)
  starting transfers between devices  35.3 us (23%)
  between operations  14.1 us (9%)
  local copies, waits for them, and re-layouts  6.76 us (4%)
    ppermute x4, waiting for transfers between devices, hop(): return lax.ppermute(array, 'expert', across)  32.3 us
    ppermute x6, waiting for transfers between devices, flip(): lax.ppermute(values.astype(bf16), name, [(i, i ^ bit) for i in range(size)])  19.7 us
    ppermute x9, starting transfers between devices, fan(): lax.ppermute(blocks[k], 'expert', [(e, e ^ k) for e in range(experts)])  8.01 us
    all_to_all x2, starting transfers between devices, trade(): lax.all_to_all(blocks, 'expert', split_axis=0, concat_axis=0, tiled=True,...  7.96 us
    ppermute x4, starting transfers between devices, hop(): return lax.ppermute(array, 'expert', across)  7.28 us
    pallas_call x1, Pallas kernels, whole(): pl.pallas_call(functools.partial(whole_kernel, number), out_shape=backwar...  6.57 us
    pallas_call x1, Pallas kernels, grads(): pl.pallas_call(grads_kernel, out_shape=[jax.ShapeDtypeStruct((width, full...  6.57 us
    ppermute x6, starting transfers between devices, flip(): lax.ppermute(values.astype(bf16), name, [(i, i ^ bit) for i in range(size)])  6.5 us
  transfers between devices with their start and end apart: 25, of which 9 were waited for; matrix products, arithmetic and copies ran while one was open for 0% of the time, Pallas kernels for 23%

profile of v6, /device:TPU:1, one launch (start us, length us, event | category | flops | bytes accessed | tf_op | source)
XLA Modules:
  0.0 152.3 jit_solution(11976248198722671395)
XLA Ops:
  7.2 0.7 all-gather.9.cloned.1.call-update
  8.0 0.7 all-gather.11.cloned.1.call-update
  8.8 3.1 %collective-permute-start = (s32[8,128]{1,0:T(8,128)S(1)}, s32[8,128]{1,0:T(8,128)S(1)}, u32[]{:S(2)}, u32[]{:S(2)}) collective-permute-start(s32[8,128]{1,0:T(8,128)S(1)} %add_add_fusion.meta_ref.refs_14_), channel_id=1, source_target_pairs={{0,8},{2,10},{4,12},{6,14},{8,0},{10,2},{12,4},{14,6},{1,9},{3,11}... | collective-permute-start | bytes 12296 | tf_op jit(solution)/shard_map/ppermute | solution.py:498
  12.1 3.0 %pack.3 = bf16[256,3200]{1,0:T(8,128)(2,1)} custom-call(s32[3]{0:T(128)S(1)} %pad_add_fusion.me_ref, s32[8,128]{1,0:T(8,128)S(1)} %add_add_fusion.meta_ref.refs_14_, bf16[128,1536]{1,0:T(8,128)(2,1)S(1)} %copy-done.19, bf16[128,1536]{1,0:T(8,128)(2,1)} %cot_ref.1), custom_call_target="tpu_custom_call" | custom-call | flops 1000000000 | bytes 4000000 | tf_op jit(solution)/shard_map/pack/pallas_call | solution.py:115
  15.0 3.6 %all-to-all-start = ((bf16[4,64,3200]{2,1,0:T(8,128)(2,1)}), bf16[4,64,3200]{2,1,0:T(8,128)(2,1)S(1)}, u32[]{:S(2)}, u32[]{:S(2)}) async-start(bf16[4,64,3200]{2,1,0:T(8,128)(2,1)} %bitcast.5), calls=%async_computation | async-start | bytes 3276800 | tf_op jit(solution)/shard_map/all_to_all | solution.py:502
  18.7 0.7 all-gather.7.cloned.1.call-update
  19.4 0.3 collective-permute-start.5
  19.7 2.1 %collective-permute-start.1 = (bf16[128,1536]{1,0:T(8,128)(2,1)}, bf16[128,1536]{1,0:T(8,128)(2,1)S(1)}, u32[]{:S(2)}, u32[]{:S(2)}) collective-permute-start(bf16[128,1536]{1,0:T(8,128)(2,1)} %cot_ref.1), channel_id=1, source_target_pairs={{0,8},{2,10},{4,12},{6,14},{8,0},{10,2},{12,4},{14,6},{1,9},{3,11}... | collective-permute-start | bytes 1179656 | tf_op jit(solution)/shard_map/ppermute | solution.py:498
  21.8 22.2 %collective-permute-done.5.refs_0_ = bf16[128,1536]{1,0:T(8,128)(2,1)S(1)} collective-permute-done((bf16[128,1536]{1,0:T(8,128)(2,1)S(1)}, bf16[128,1536]{1,0:T(8,128)(2,1)S(1)}, u32[]{:S(2)}, u32[]{:S(2)}) %collective-permute-start.5) | collective-permute-done | bytes 393248 | tf_op jit(solution)/shard_map/ppermute | solution.py:498
  44.0 1.8 %pack.5 = (bf16[64,1664]{1,0:T(8,128)(2,1)S(1)}, bf16[64,1664]{1,0:T(8,128)(2,1)}, bf16[64,1664]{1,0:T(8,128)(2,1)}, bf16[64,1664]{1,0:T(8,128)(2,1)}) custom-call(s32[3]{0:T(128)S(1)} %pad_add_fusion.me_ref, s32[8,128]{1,0:T(8,128)S(1)} %collective-permute-done.meta_ref, bf16[128,1536]{1,0:T(8,128)(2,1)S(1)} %collective-permute-done.5.refs_0_), custom_call_target="tpu_custom_call" | custom-call | flops 1000000000 | bytes 4000000 | tf_op jit(solution)/shard_map/pack/pallas_call | solution.py:115
  45.8 1.1 collective-permute-start.6
  47.0 1.3 collective-permute-start.7
  48.3 0.2 collective-permute-start.8
  48.5 4.1 %collective-permute-done.1.refs_0_ = bf16[128,1536]{1,0:T(8,128)(2,1)S(1)} collective-permute-done((bf16[128,1536]{1,0:T(8,128)(2,1)}, bf16[128,1536]{1,0:T(8,128)(2,1)S(1)}, u32[]{:S(2)}, u32[]{:S(2)}) %collective-permute-start.1) | collective-permute-done | bytes 393248 | tf_op jit(solution)/shard_map/ppermute | solution.py:498
  52.5 1.7 %pack.4 = (bf16[64,1536]{1,0:T(8,128)(2,1)S(1)}, bf16[64,1536]{1,0:T(8,128)(2,1)}, bf16[64,1536]{1,0:T(8,128)(2,1)}, bf16[64,1536]{1,0:T(8,128)(2,1)S(1)}) custom-call(s32[3]{0:T(128)S(1)} %pad_add_fusion.me_ref, s32[8,128]{1,0:T(8,128)S(1)} %collective-permute-done.meta_ref, bf16[128,1536]{1,0:T(8,128)(2,1)S(1)} %collective-permute-done.1.refs_0_), custom_call_target="tpu_custom_call" | custom-call | flops 1000000000 | bytes 4000000 | tf_op jit(solution)/shard_map/pack/pallas_call | solution.py:115
  54.3 1.1 collective-permute-start.2
  55.4 1.2 collective-permute-start.3
  56.6 0.3 collective-permute-start.4
  57.0 1.7 %copy-done = bf16[1,1536,768]{2,1,0:T(8,128)(2,1)S(1)} copy-done((bf16[1,1536,768]{2,1,0:T(8,128)(2,1)S(1)}, bf16[1,1536,768]{2,1,0:T(8,128)(2,1)}, u32[]{:S(2)}) %copy-start) | copy-done | bytes 2359320
  58.6 1.7 %copy-done.2 = bf16[1,1536,768]{2,1,0:T(8,128)(2,1)S(1)} copy-done((bf16[1,1536,768]{2,1,0:T(8,128)(2,1)S(1)}, bf16[1,1536,768]{2,1,0:T(8,128)(2,1)}, u32[]{:S(2)}) %copy-start.2) | copy-done | bytes 2359320
  60.3 1.7 %copy-done.5 = bf16[1,1536,768]{2,1,0:T(8,128)(2,1)S(1)} copy-done((bf16[1,1536,768]{2,1,0:T(8,128)(2,1)S(1)}, bf16[1,1536,768]{2,1,0:T(8,128)(2,1)}, u32[]{:S(2)}) %copy-start.5) | copy-done | bytes 2359320
  61.9 6.6 %expert_whole.1 = (bf16[256,1536]{1,0:T(8,128)(2,1)}, bf16[256,5376]{1,0:T(8,128)(2,1)S(1)}, f32[256,128]{1,0:T(8,128)S(1)}) custom-call(s32[3]{0:T(128)S(1)} %pad_add_fusion.me_ref, bf16[256,3200]{1,0:T(8,128)(2,1)S(1)} %bitcast.20, f32[3,32,1536]{2,1,0:T(8,128)S(1)} %copy-done.4, bf16[8,1536]{1,0:T(8,128)(2,1)S(1)} %copy-done.18, ...), custom_call_target="tpu_custom_call" | custom-call | flops 3019898880 | bytes 11173888 | tf_op jit(solution)/shard_map/expert_whole/pallas_call | solution.py:271
  68.6 3.0 %expert_in.1 = (bf16[256,1536]{1,0:T(8,128)(2,1)S(1)}, f32[256,128]{1,0:T(8,128)S(1)}, f32[256,768]{1,0:T(8,128)S(1)}, f32[256,768]{1,0:T(8,128)S(1)}, bf16[256,768]{1,0:T(8,128)(2,1)S(1)}) custom-call(s32[3]{0:T(128)S(1)} %pad_add_fusion.me_ref, bf16[64,1664]{1,0:T(8,128)(2,1)S(1)} %get-tuple-element.68.refs_0_.refs_1_, ...), custom_call_target="tpu_custom_call" | custom-call | flops 1207959552 | bytes 7790592 | tf_op jit(solution)/shard_map/expert_in/pallas_call | solution.py:205
  71.6 1.3 collective-permute-done.4.refs_3_
  72.9 3.6 %expert_back.1 = (bf16[64,1536]{1,0:T(8,128)(2,1)S(1)}, bf16[64,1536]{1,0:T(8,128)(2,1)S(1)}, bf16[64,1536]{1,0:T(8,128)(2,1)S(1)}, bf16[64,1536]{1,0:T(8,128)(2...) custom-call(s32[3]{0:T(128)S(1)} %pad_add_fusion.me_ref, bf16[64,1536]{1,0:T(8,128)(2,1)S(1)} %get-tuple-element.58.refs_0_, ...), custom_call_target="tpu_custom_call" | custom-call | flops 1811939328 | bytes 11173888 | tf_op jit(solution)/shard_map/expert_back/pallas_call | solution.py:244
  76.5 0.3 collective-permute-start.10
  76.8 1.2 collective-permute-start.11
  78.1 1.2 collective-permute-start.9
  79.3 6.6 %weight_grads.1 = (bf16[1536,384]{1,0:T(8,128)(2,1)S(1)}, bf16[1536,384]{1,0:T(8,128)(2,1)S(1)}, bf16[1536,384]{1,0:T(8,128)(2,1)S(1)}, bf16[3,1536,384]{2,1,0:T(8,128)(2,1)}) custom-call(s32[3]{0:T(128)S(1)} %pad_add_fusion.me_ref, bf16[256,5376]{1,0:T(8,128)(2,1)S(1)} %get-tuple-element.82.refs_10_.near_ref, ...), custom_call_target="tpu_custom_call" | custom-call | flops 1000000 | bytes 10000 | tf_op jit(solution)/shard_map/weight_grads/pallas_call | solution.py:364
  85.9 4.0 %table_sums.1 = f32[128,1536]{1,0:T(8,128)S(1)} custom-call(s32[3]{0:T(128)S(1)} %pad_add_fusion.me_ref, bf16[256,3200]{1,0:T(8,128)(2,1)S(1)} %bitcast.21, bf16[64,1664]{1,0:T(8,128)(2,1)S(1)} %get-tuple-element.68.refs_0_.refs_1_, bf16[64,1664]{1,0:T(8,128)(2,1)S(1)} %collective-permute-done.6.refs_1_.refs_2_, bf16[64,1664]{1,0:T(8,128)(2,1)S(1)} %copy-done.14, ...), custom_call_target="tpu_custom_call" | custom-call | flops 1000000 | bytes 10000 | tf_op jit(solution)/shard_map/table_sums/pallas_call | solution.py:335
  89.9 1.7 %merge.1 = bf16[128,1536]{1,0:T(8,128)(2,1)} custom-call(s32[3]{0:T(128)S(1)} %pad_add_fusion.me_ref, s32[8,128]{1,0:T(8,128)S(1)} %collective-permute-done.meta_ref, bf16[64,1536]{1,0:T(8,128)(2,1)S(1)} %get-tuple-element.77.refs_0_.refs_6_, bf16[64,1536]{1,0:T(8,128)(2,1)S(1)} %collective-permute-done.9.refs_1_, ...), custom_call_target="tpu_custom_call" | custom-call | flops 1000000000 | bytes 2000000 | tf_op jit(solution)/shard_map/merge/pallas_call | solution.py:384
  91.6 5.5 %collective-permute-start.15 = (bf16[3,1536,384]{2,1,0:T(8,128)(2,1)}, bf16[3,1536,384]{2,1,0:T(8,128)(2,1)}, u32[]{:S(2)}, u32[]{:S(2)}) collective-permute-start(bf16[3,1536,384]{2,1,0:T(8,128)(2,1)} %get-tuple-element.89), channel_id=1, source_target_pairs={{0,1},{1,0},{2,3},{3,2},{4,5},{5,4},{6,7},{7,6},{8,9},{9,8},{10,11... | collective-permute-start | bytes 10616840 | tf_op jit(solution)/shard_map/ppermute | solution.py:553
  97.2 4.4 %all-to-all-start.1 = ((bf16[4,64,1536]{2,1,0:T(8,128)(2,1)}), bf16[4,64,1536]{2,1,0:T(8,128)(2,1)}, u32[]{:S(2)}, u32[]{:S(2)}) async-start(bf16[4,64,1536]{2,1,0:T(8,128)(2,1)} %bitcast.10), calls=%async_computation.1 | async-start | bytes 1572864 | tf_op jit(solution)/shard_map/all_to_all | solution.py:502
  101.6 1.5 collective-permute-done.12
  103.2 1.2 collective-permute-start.13
  104.4 1.7 %collective-permute-start.14 = (bf16[128,1536]{1,0:T(8,128)(2,1)}, bf16[128,1536]{1,0:T(8,128)(2,1)S(1)}, u32[]{:S(2)}, u32[]{:S(2)}) collective-permute-start(bf16[128,1536]{1,0:T(8,128)(2,1)} %merge.1), channel_id=1, source_target_pairs={{0,8},{2,10},{4,12},{6,14},{8,0},{10,2},{12,4},{14,6},{1,9},{3,11}... | collective-permute-start | bytes 1179656 | tf_op jit(solution)/shard_map/ppermute | solution.py:498
  106.1 6.6 %collective-permute-done.13 = bf16[32,1536]{1,0:T(8,128)(2,1)S(1)} collective-permute-done((bf16[32,1536]{1,0:T(8,128)(2,1)S(1)}, bf16[32,1536]{1,0:T(8,128)(2,1)S(1)}, u32[]{:S(2)}, u32[]{:S(2)}) %collective-permute-start.13) | collective-permute-done | bytes 98336 | tf_op jit(solution)/shard_map/ppermute | solution.py:427
  112.8 5.5 %add.34 = (bf16[1,1536,384]{2,1,0:T(8,128)(2,1)}, bf16[1,1536,384]{2,1,0:T(8,128)(2,1)}, bf16[1,1536,384]{2,1,0:T(8,128)(2,1)}) custom-call(bf16[3,1536,384]{2,1,0:T(8,128)(2,1)} %collective-permute-done.15.other_ref, bf16[1536,384]{1,0:T(8,128)(2,1)S(1)} %copy-done.8, bf16[1536,384]{1,0:T(8,128)(2,1)S(1)} %copy-done.10, bf16[1536,384]{1,0:T(8,128)(2,1)S(1)} %copy-done.12), custom_call_target="tpu_custom_call" | custom-call | flops 1000000 | bytes 10000 | tf_op jit(solution)/shard_map/add/pallas_call | solution.py:465
  118.3 6.0 %collective-permute-done.14.far_ref = bf16[128,1536]{1,0:T(8,128)(2,1)S(1)} collective-permute-done((bf16[128,1536]{1,0:T(8,128)(2,1)}, bf16[128,1536]{1,0:T(8,128)(2,1)S(1)}, u32[]{:S(2)}, u32[]{:S(2)}) %collective-permute-start.14) | collective-permute-done | bytes 393248 | tf_op jit(solution)/shard_map/ppermute | solution.py:498
  124.3 3.5 %collective-permute-done.16 = bf16[32,1536]{1,0:T(8,128)(2,1)S(1)} collective-permute-done((bf16[32,1536]{1,0:T(8,128)(2,1)S(1)}, bf16[32,1536]{1,0:T(8,128)(2,1)S(1)}, u32[]{:S(2)}, u32[]{:S(2)}) %collective-permute-start.16) | collective-permute-done | bytes 98336 | tf_op jit(solution)/shard_map/ppermute | solution.py:427
  127.8 0.2 collective-permute-start.17
  128.1 5.0 %collective-permute-done.17 = bf16[32,1536]{1,0:T(8,128)(2,1)S(1)} collective-permute-done((bf16[32,1536]{1,0:T(8,128)(2,1)S(1)}, bf16[32,1536]{1,0:T(8,128)(2,1)S(1)}, u32[]{:S(2)}, u32[]{:S(2)}) %collective-permute-start.17) | collective-permute-done | bytes 98336 | tf_op jit(solution)/shard_map/ppermute | solution.py:427
  133.1 0.4 collective-permute-start.18
  133.5 3.2 %collective-permute-done.18 = bf16[32,1536]{1,0:T(8,128)(2,1)S(1)} collective-permute-done((bf16[32,1536]{1,0:T(8,128)(2,1)S(1)}, bf16[32,1536]{1,0:T(8,128)(2,1)S(1)}, u32[]{:S(2)}, u32[]{:S(2)}) %collective-permute-start.18) | collective-permute-done | bytes 98336 | tf_op jit(solution)/shard_map/ppermute | solution.py:427
  136.7 4.5 %collective-permute-start.19 = (bf16[64,1536]{1,0:T(8,128)(2,1)S(1)}, bf16[64,1536]{1,0:T(8,128)(2,1)S(1)}, u32[]{:S(2)}, u32[]{:S(2)}) collective-permute-start(bf16[64,1536]{1,0:T(8,128)(2,1)S(1)} %pad_maximum_fusion.1), channel_id=1, source_target_pairs={{0,1},{1,0},{2,3},{3,2},{4,5},{5,4},{6,7},{7,6},{8,9},{9,8},{10,11... | collective-permute-start | bytes 589832 | tf_op jit(solution)/shard_map/ppermute | solution.py:427
  141.3 2.9 %final.1 = bf16[128,1536]{1,0:T(8,128)(2,1)} custom-call(s32[3]{0:T(128)S(1)} %pad_add_fusion.me_ref, s32[8,128]{1,0:T(8,128)S(1)} %add_add_fusion.meta_ref.refs_14_, s32[128,1]{1,0:T(8,128)S(1)} %copy.16.stamp_ref, bf16[128,1536]{1,0:T(8,128)(2,1)S(1)} %copy-done.20, bf16[128,1536]{1,0:T(8,128)(2,1)} %cot_ref.1, f32[3,32,1536]{2,1,0:T(8,128)S(1)} %copy-done.4, ...), custom_call_target="tpu_custom_call" | custom-call | flops 1000000000 | bytes 4000000 | tf_op jit(solution)/shard_map/final/pallas_call | solution.py:411
  144.3 0.9 slice.27
  145.2 0.6 slice.26
  (80 shorter events, 1.1 us)
Async XLA Ops:
  7.2 1.6 %copy-start.22 = (s32[128,2]{0,1:T(2,128)S(1)}, s32[128,2]{0,1:T(2,128)}, u32[]{:S(2)}) copy-start(s32[128,2]{0,1:T(2,128)} %param.14) | copy-start | bytes 3076
  7.2 1.6 %copy-start.21 = (s32[128]{0:T(128)S(1)}, s32[128]{0:T(128)}, u32[]{:S(2)}) copy-start(s32[128]{0:T(128)} %param.13) | copy-start | bytes 1540
  7.2 4.9 %copy-start.19 = (bf16[128,1536]{1,0:T(8,128)(2,1)S(1)}, bf16[128,1536]{1,0:T(8,128)(2,1)}, u32[]{:S(2)}) copy-start(bf16[128,1536]{1,0:T(8,128)(2,1)} %tok_ref.1) | copy-start | bytes 1179652
  7.2 49.7 %all-gather.9.cloned.1.call-start = ((), (), s32[]{:S(2)}) async-start(), calls=%async_computation.3 | async-start | bytes 3538944 | tf_op jit(solution)/shard_map/all_gather | solution.py:520
  7.9 49.0 %all-gather.11.cloned.1.call-start = ((), (), s32[]{:S(2)}) async-start(), calls=%async_computation.4 | async-start | bytes 3538944 | tf_op jit(solution)/shard_map/all_gather | solution.py:520
  8.8 6.2 %collective-permute-start = (s32[8,128]{1,0:T(8,128)S(1)}, s32[8,128]{1,0:T(8,128)S(1)}, u32[]{:S(2)}, u32[]{:S(2)}) collective-permute-start(s32[8,128]{1,0:T(8,128)S(1)} %add_add_fusion.meta_ref.refs_14_), channel_id=1, source_target_pairs={{0,8},{2,10},{4,12},{6,14},{8,0},{10,2},{12,4},{14,6},{1,9},{3,11}... | collective-permute-start | bytes 12296 | tf_op jit(solution)/shard_map/ppermute | solution.py:498
  15.0 41.6 %all-to-all-start = ((bf16[4,64,3200]{2,1,0:T(8,128)(2,1)}), bf16[4,64,3200]{2,1,0:T(8,128)(2,1)S(1)}, u32[]{:S(2)}, u32[]{:S(2)}) async-start(bf16[4,64,3200]{2,1,0:T(8,128)(2,1)} %bitcast.5), calls=%async_computation | async-start | bytes 3276800 | tf_op jit(solution)/shard_map/all_to_all | solution.py:502
  18.6 38.3 %all-gather.7.cloned.1.call-start = ((), (), s32[]{:S(2)}) async-start(), calls=%async_computation.2 | async-start | bytes 3538944 | tf_op jit(solution)/shard_map/all_gather | solution.py:520
  19.4 24.6 %collective-permute-start.5 = (bf16[128,1536]{1,0:T(8,128)(2,1)S(1)}, bf16[128,1536]{1,0:T(8,128)(2,1)S(1)}, u32[]{:S(2)}, u32[]{:S(2)}) collective-permute-start(bf16[128,1536]{1,0:T(8,128)(2,1)S(1)} %copy-done.19), channel_id=1, source_target_pairs={{0,8},{2,10},{4,12},{6,14},{8,0},{10,2},{12,4},{14,6},{1,9},{3,11}... | collective-permute-start | bytes 1179656 | tf_op jit(solution)/shard_map/ppermute | solution.py:498
  19.7 32.8 %collective-permute-start.1 = (bf16[128,1536]{1,0:T(8,128)(2,1)}, bf16[128,1536]{1,0:T(8,128)(2,1)S(1)}, u32[]{:S(2)}, u32[]{:S(2)}) collective-permute-start(bf16[128,1536]{1,0:T(8,128)(2,1)} %cot_ref.1), channel_id=1, source_target_pairs={{0,8},{2,10},{4,12},{6,14},{8,0},{10,2},{12,4},{14,6},{1,9},{3,11}... | collective-permute-start | bytes 1179656 | tf_op jit(solution)/shard_map/ppermute | solution.py:498
  45.8 10.8 %collective-permute-start.6 = (bf16[64,1664]{1,0:T(8,128)(2,1)}, bf16[64,1664]{1,0:T(8,128)(2,1)S(1)}, u32[]{:S(2)}, u32[]{:S(2)}) collective-permute-start(bf16[64,1664]{1,0:T(8,128)(2,1)} %get-tuple-element.65), channel_id=1, source_target_pairs={{0,2},{2,0},{4,6},{6,4},{8,10},{10,8},{12,14},{14,12},{1,3},{3,1},... | collective-permute-start | bytes 638984 | tf_op jit(solution)/shard_map/ppermute | solution.py:509
  47.0 21.6 %collective-permute-start.7 = (bf16[64,1664]{1,0:T(8,128)(2,1)}, bf16[64,1664]{1,0:T(8,128)(2,1)S(1)}, u32[]{:S(2)}, u32[]{:S(2)}) collective-permute-start(bf16[64,1664]{1,0:T(8,128)(2,1)} %get-tuple-element.66), channel_id=1, source_target_pairs={{0,4},{2,6},{4,0},{6,2},{8,12},{10,14},{12,8},{14,10},{1,5},{3,7},... | collective-permute-start | bytes 638984 | tf_op jit(solution)/shard_map/ppermute | solution.py:509
  48.3 8.6 %copy-start.4 = (f32[3,32,1536]{2,1,0:T(8,128)S(1)}, f32[3,32,1536]{2,1,0:T(8,128)}, u32[]{:S(2)}) copy-start(f32[3,32,1536]{2,1,0:T(8,128)} %table_ref.1) | copy-start | bytes 1769476
  48.3 8.6 %copy-start.18 = (bf16[8,1536]{1,0:T(8,128)(2,1)S(1)}, bf16[8,1536]{1,0:T(8,128)(2,1)}, u32[]{:S(2)}) copy-start(bf16[8,1536]{1,0:T(8,128)(2,1)} %refs_5_.3) | copy-start | bytes 73732
  48.3 20.2 %collective-permute-start.8 = (bf16[64,1664]{1,0:T(8,128)(2,1)}, bf16[64,1664]{1,0:T(8,128)(2,1)S(1)}, u32[]{:S(2)}, u32[]{:S(2)}) collective-permute-start(bf16[64,1664]{1,0:T(8,128)(2,1)} %get-tuple-element.67), channel_id=1, source_target_pairs={{0,6},{2,4},{4,2},{6,0},{8,14},{10,12},{12,10},{14,8},{1,7},{3,5},... | collective-permute-start | bytes 638984 | tf_op jit(solution)/shard_map/ppermute | solution.py:509
  54.3 17.3 %collective-permute-start.2 = (bf16[64,1536]{1,0:T(8,128)(2,1)}, bf16[64,1536]{1,0:T(8,128)(2,1)}, u32[]{:S(2)}, u32[]{:S(2)}) collective-permute-start(bf16[64,1536]{1,0:T(8,128)(2,1)} %get-tuple-element.59), channel_id=1, source_target_pairs={{0,2},{2,0},{4,6},{6,4},{8,10},{10,8},{12,14},{14,12},{1,3},{3,1},... | collective-permute-start | bytes 589832 | tf_op jit(solution)/shard_map/ppermute | solution.py:509
  55.4 16.2 %collective-permute-start.3 = (bf16[64,1536]{1,0:T(8,128)(2,1)}, bf16[64,1536]{1,0:T(8,128)(2,1)}, u32[]{:S(2)}, u32[]{:S(2)}) collective-permute-start(bf16[64,1536]{1,0:T(8,128)(2,1)} %get-tuple-element.60), channel_id=1, source_target_pairs={{0,4},{2,6},{4,0},{6,2},{8,12},{10,14},{12,8},{14,10},{1,5},{3,7},... | collective-permute-start | bytes 589832 | tf_op jit(solution)/shard_map/ppermute | solution.py:509
  56.6 16.3 %collective-permute-start.4 = (bf16[64,1536]{1,0:T(8,128)(2,1)S(1)}, bf16[64,1536]{1,0:T(8,128)(2,1)}, u32[]{:S(2)}, u32[]{:S(2)}) collective-permute-start(bf16[64,1536]{1,0:T(8,128)(2,1)S(1)} %get-tuple-element.61), channel_id=1, source_target_pairs={{0,6},{2,4},{4,2},{6,0},{8,14},{10,12},{12,10},{14,8},{1,7},{3,5},... | collective-permute-start | bytes 589832 | tf_op jit(solution)/shard_map/ppermute | solution.py:509
  56.9 1.7 %copy-start = (bf16[1,1536,768]{2,1,0:T(8,128)(2,1)S(1)}, bf16[1,1536,768]{2,1,0:T(8,128)(2,1)}, u32[]{:S(2)}) copy-start(bf16[1,1536,768]{2,1,0:T(8,128)(2,1)} %all-gather.9.cloned.1.call-done) | copy-start | bytes 7077892
  58.6 1.7 %copy-start.2 = (bf16[1,1536,768]{2,1,0:T(8,128)(2,1)S(1)}, bf16[1,1536,768]{2,1,0:T(8,128)(2,1)}, u32[]{:S(2)}) copy-start(bf16[1,1536,768]{2,1,0:T(8,128)(2,1)} %all-gather.11.cloned.1.call-done) | copy-start | bytes 7077892
  60.3 1.7 %copy-start.5 = (bf16[1,1536,768]{2,1,0:T(8,128)(2,1)S(1)}, bf16[1,1536,768]{2,1,0:T(8,128)(2,1)}, u32[]{:S(2)}) copy-start(bf16[1,1536,768]{2,1,0:T(8,128)(2,1)} %all-gather.7.cloned.1.call-done) | copy-start | bytes 7077892
  61.9 6.6 %copy-start.1 = (bf16[1,1536,768]{2,1,0:T(8,128)(2,1)S(1)}, bf16[1,1536,768]{2,1,0:T(8,128)(2,1)}, u32[]{:S(2)}) copy-start(bf16[1,1536,768]{2,1,0:T(8,128)(2,1)} %all-gather.9.cloned.1.call-done) | copy-start | bytes 7077892
  68.5 3.0 %copy-start.13 = (bf16[64,1664]{1,0:T(8,128)(2,1)}, bf16[64,1664]{1,0:T(8,128)(2,1)S(1)}, u32[]{:S(2)}) copy-start(bf16[64,1664]{1,0:T(8,128)(2,1)S(1)} %collective-permute-done.7.refs_2_.refs_3_) | copy-start | bytes 638980
  68.5 3.0 %copy-start.15 = (bf16[64,1664]{1,0:T(8,128)(2,1)}, bf16[64,1664]{1,0:T(8,128)(2,1)S(1)}, u32[]{:S(2)}) copy-start(bf16[64,1664]{1,0:T(8,128)(2,1)S(1)} %collective-permute-done.8.refs_3_.refs_4_) | copy-start | bytes 638980
  68.6 4.4 %copy-start.3 = (bf16[1,1536,768]{2,1,0:T(8,128)(2,1)S(1)}, bf16[1,1536,768]{2,1,0:T(8,128)(2,1)}, u32[]{:S(2)}) copy-start(bf16[1,1536,768]{2,1,0:T(8,128)(2,1)} %all-gather.11.cloned.1.call-done) | copy-start | bytes 7077892
  68.6 4.4 %copy-start.6 = (bf16[1,1536,768]{2,1,0:T(8,128)(2,1)S(1)}, bf16[1,1536,768]{2,1,0:T(8,128)(2,1)}, u32[]{:S(2)}) copy-start(bf16[1,1536,768]{2,1,0:T(8,128)(2,1)} %all-gather.7.cloned.1.call-done) | copy-start | bytes 7077892
  76.5 13.3 %collective-permute-start.10 = (bf16[64,1536]{1,0:T(8,128)(2,1)S(1)}, bf16[64,1536]{1,0:T(8,128)(2,1)S(1)}, u32[]{:S(2)}, u32[]{:S(2)}) collective-permute-start(bf16[64,1536]{1,0:T(8,128)(2,1)S(1)} %get-tuple-element.79.refs_8_), channel_id=1, source_target_pairs={{0,4},{2,6},{4,0},{6,2},{8,12},{10,14},{12,8},{14,10},{1,5},{3,7},... | collective-permute-start | bytes 589832 | tf_op jit(solution)/shard_map/ppermute | solution.py:509
  76.8 13.0 %collective-permute-start.11 = (bf16[64,1536]{1,0:T(8,128)(2,1)S(1)}, bf16[64,1536]{1,0:T(8,128)(2,1)S(1)}, u32[]{:S(2)}, u32[]{:S(2)}) collective-permute-start(bf16[64,1536]{1,0:T(8,128)(2,1)S(1)} %get-tuple-element.80.refs_9_), channel_id=1, source_target_pairs={{0,6},{2,4},{4,2},{6,0},{8,14},{10,12},{12,10},{14,8},{1,7},{3,5},... | collective-permute-start | bytes 589832 | tf_op jit(solution)/shard_map/ppermute | solution.py:509
  78.1 11.8 %collective-permute-start.9 = (bf16[64,1536]{1,0:T(8,128)(2,1)S(1)}, bf16[64,1536]{1,0:T(8,128)(2,1)S(1)}, u32[]{:S(2)}, u32[]{:S(2)}) collective-permute-start(bf16[64,1536]{1,0:T(8,128)(2,1)S(1)} %get-tuple-element.78.refs_7_), channel_id=1, source_target_pairs={{0,2},{2,0},{4,6},{6,4},{8,10},{10,8},{12,14},{14,12},{1,3},{3,1},... | collective-permute-start | bytes 589832 | tf_op jit(solution)/shard_map/ppermute | solution.py:509
  79.2 6.6 %copy-start.14 = (bf16[64,1664]{1,0:T(8,128)(2,1)S(1)}, bf16[64,1664]{1,0:T(8,128)(2,1)}, u32[]{:S(2)}) copy-start(bf16[64,1664]{1,0:T(8,128)(2,1)} %copy-done.13) | copy-start | bytes 638980
  79.2 6.6 %copy-start.16 = (bf16[64,1664]{1,0:T(8,128)(2,1)S(1)}, bf16[64,1664]{1,0:T(8,128)(2,1)}, u32[]{:S(2)}) copy-start(bf16[64,1664]{1,0:T(8,128)(2,1)} %copy-done.15) | copy-start | bytes 638980
  79.3 6.6 %copy-start.17 = (bf16[128,1536]{1,0:T(8,128)(2,1)S(1)}, bf16[128,1536]{1,0:T(8,128)(2,1)}, u32[]{:S(2)}) copy-start(bf16[128,1536]{1,0:T(8,128)(2,1)} %refs_16_.1) | copy-start | bytes 1179652
  85.8 4.0 %copy-start.7 = (bf16[1536,384]{1,0:T(8,128)(2,1)}, bf16[1536,384]{1,0:T(8,128)(2,1)S(1)}, u32[]{:S(2)}) copy-start(bf16[1536,384]{1,0:T(8,128)(2,1)S(1)} %get-tuple-element.90.refs_0_) | copy-start | bytes 3538948
  85.8 4.0 %copy-start.9 = (bf16[1536,384]{1,0:T(8,128)(2,1)}, bf16[1536,384]{1,0:T(8,128)(2,1)S(1)}, u32[]{:S(2)}) copy-start(bf16[1536,384]{1,0:T(8,128)(2,1)S(1)} %get-tuple-element.91.refs_1_) | copy-start | bytes 3538948
  85.8 4.0 %copy-start.11 = (bf16[1536,384]{1,0:T(8,128)(2,1)}, bf16[1536,384]{1,0:T(8,128)(2,1)S(1)}, u32[]{:S(2)}) copy-start(bf16[1536,384]{1,0:T(8,128)(2,1)S(1)} %get-tuple-element.92.refs_2_) | copy-start | bytes 3538948
  91.6 21.1 %collective-permute-start.15 = (bf16[3,1536,384]{2,1,0:T(8,128)(2,1)}, bf16[3,1536,384]{2,1,0:T(8,128)(2,1)}, u32[]{:S(2)}, u32[]{:S(2)}) collective-permute-start(bf16[3,1536,384]{2,1,0:T(8,128)(2,1)} %get-tuple-element.89), channel_id=1, source_target_pairs={{0,1},{1,0},{2,3},{3,2},{4,5},{5,4},{6,7},{7,6},{8,9},{9,8},{10,11... | collective-permute-start | bytes 10616840 | tf_op jit(solution)/shard_map/ppermute | solution.py:553
  97.1 6.0 %collective-permute-start.12 = (bf16[64,1536]{1,0:T(8,128)(2,1)S(1)}, bf16[64,1536]{1,0:T(8,128)(2,1)S(1)}, u32[]{:S(2)}, u32[]{:S(2)}) collective-permute-start(bf16[64,1536]{1,0:T(8,128)(2,1)S(1)} %select_convert_fusion), channel_id=1, source_target_pairs={{0,1},{1,0},{2,3},{3,2},{4,5},{5,4},{6,7},{7,6},{8,9},{9,8},{10,11... | collective-permute-start | bytes 589832 | tf_op jit(solution)/shard_map/ppermute | solution.py:427
  97.2 15.6 %copy-start.8 = (bf16[1536,384]{1,0:T(8,128)(2,1)S(1)}, bf16[1536,384]{1,0:T(8,128)(2,1)}, u32[]{:S(2)}) copy-start(bf16[1536,384]{1,0:T(8,128)(2,1)} %copy-done.7) | copy-start | bytes 3538948
  97.2 27.0 %all-to-all-start.1 = ((bf16[4,64,1536]{2,1,0:T(8,128)(2,1)}), bf16[4,64,1536]{2,1,0:T(8,128)(2,1)}, u32[]{:S(2)}, u32[]{:S(2)}) async-start(bf16[4,64,1536]{2,1,0:T(8,128)(2,1)} %bitcast.10), calls=%async_computation.1 | async-start | bytes 1572864 | tf_op jit(solution)/shard_map/all_to_all | solution.py:502
  101.6 11.2 %copy-start.10 = (bf16[1536,384]{1,0:T(8,128)(2,1)S(1)}, bf16[1536,384]{1,0:T(8,128)(2,1)}, u32[]{:S(2)}) copy-start(bf16[1536,384]{1,0:T(8,128)(2,1)} %copy-done.9) | copy-start | bytes 3538948
  101.6 11.2 %copy-start.12 = (bf16[1536,384]{1,0:T(8,128)(2,1)S(1)}, bf16[1536,384]{1,0:T(8,128)(2,1)}, u32[]{:S(2)}) copy-start(bf16[1536,384]{1,0:T(8,128)(2,1)} %copy-done.11) | copy-start | bytes 3538948
  103.2 9.6 %collective-permute-start.13 = (bf16[32,1536]{1,0:T(8,128)(2,1)S(1)}, bf16[32,1536]{1,0:T(8,128)(2,1)S(1)}, u32[]{:S(2)}, u32[]{:S(2)}) collective-permute-start(bf16[32,1536]{1,0:T(8,128)(2,1)S(1)} %select_convert_fusion.1), channel_id=1, source_target_pairs={{0,2},{2,0},{4,6},{6,4},{8,10},{10,8},{12,14},{14,12},{1,3},{3,1},... | collective-permute-start | bytes 294920 | tf_op jit(solution)/shard_map/ppermute | solution.py:427
  104.4 19.8 %collective-permute-start.14 = (bf16[128,1536]{1,0:T(8,128)(2,1)}, bf16[128,1536]{1,0:T(8,128)(2,1)S(1)}, u32[]{:S(2)}, u32[]{:S(2)}) collective-permute-start(bf16[128,1536]{1,0:T(8,128)(2,1)} %merge.1), channel_id=1, source_target_pairs={{0,8},{2,10},{4,12},{6,14},{8,0},{10,2},{12,4},{14,6},{1,9},{3,11}... | collective-permute-start | bytes 1179656 | tf_op jit(solution)/shard_map/ppermute | solution.py:498
  118.3 23.0 %copy-start.20 = (bf16[128,1536]{1,0:T(8,128)(2,1)S(1)}, bf16[128,1536]{1,0:T(8,128)(2,1)}, u32[]{:S(2)}) copy-start(bf16[128,1536]{1,0:T(8,128)(2,1)} %tok_ref.1) | copy-start | bytes 1179652
  124.3 3.5 %collective-permute-start.16 = (bf16[32,1536]{1,0:T(8,128)(2,1)S(1)}, bf16[32,1536]{1,0:T(8,128)(2,1)S(1)}, u32[]{:S(2)}, u32[]{:S(2)}) collective-permute-start(bf16[32,1536]{1,0:T(8,128)(2,1)S(1)} %reduce-precision_convert_fusion.1), channel_id=1, source_target_pairs={{0,4},{2,6},{4,0},{6,2},{8,12},{10,14},{12,8},{14,10},{1,5},{3,7},... | collective-permute-start | bytes 294920 | tf_op jit(solution)/shard_map/ppermute | solution.py:427
  127.8 5.2 %collective-permute-start.17 = (bf16[32,1536]{1,0:T(8,128)(2,1)S(1)}, bf16[32,1536]{1,0:T(8,128)(2,1)S(1)}, u32[]{:S(2)}, u32[]{:S(2)}) collective-permute-start(bf16[32,1536]{1,0:T(8,128)(2,1)S(1)} %fusion), channel_id=1, source_target_pairs={{0,8},{2,10},{4,12},{6,14},{8,0},{10,2},{12,4},{14,6},{1,9},{3,11}... | collective-permute-start | bytes 294920 | tf_op jit(solution)/shard_map/ppermute | solution.py:427
  133.1 3.5 %collective-permute-start.18 = (bf16[32,1536]{1,0:T(8,128)(2,1)S(1)}, bf16[32,1536]{1,0:T(8,128)(2,1)S(1)}, u32[]{:S(2)}, u32[]{:S(2)}) collective-permute-start(bf16[32,1536]{1,0:T(8,128)(2,1)S(1)} %reduce-precision_convert_fusion), channel_id=1, source_target_pairs={{0,2},{2,0},{4,6},{6,4},{8,10},{10,8},{12,14},{14,12},{1,3},{3,1},... | collective-permute-start | bytes 294920 | tf_op jit(solution)/shard_map/ppermute | solution.py:427
  136.7 7.5 %collective-permute-start.19 = (bf16[64,1536]{1,0:T(8,128)(2,1)S(1)}, bf16[64,1536]{1,0:T(8,128)(2,1)S(1)}, u32[]{:S(2)}, u32[]{:S(2)}) collective-permute-start(bf16[64,1536]{1,0:T(8,128)(2,1)S(1)} %pad_maximum_fusion.1), channel_id=1, source_target_pairs={{0,1},{1,0},{2,3},{3,2},{4,5},{5,4},{6,7},{7,6},{8,9},{9,8},{10,11... | collective-permute-start | bytes 589832 | tf_op jit(solution)/shard_map/ppermute | solution.py:427
Sparse Core Ops, SparseCore 0:
  9.6 13.3 all-gather.8
  24.5 12.0 all-gather.10
  38.2 12.0 all-gather.6
